TPU v7x, 32 devices: a whole 2x2x4 slice. The times are simulated.
32 devices in a mesh: row: 16 (over z, y, core), col: 2 (over x).
Axes of the slice: x: 2, y: 2, z: 4, core: 2. Of those that a mesh axis runs over, the one named last changes fastest.
Arguments:
- grad_x: float32 [1536, 1024], P('row', 'col'), may hold values from -6 to 6
- grad_y: float32 [1536, 1024], P('row', 'col'), may hold values from -6 to 6
- weight_x: float32 [1536, 1024], P('row', 'col'), may hold values from 0.1 to 10
- weight_y: float32 [1536, 1024], P('row', 'col'), may hold values from 0.1 to 10
- anchor: float32 [1536, 1024], P('row', 'col'), may hold values from 0.02 to 0.5
- prior: float32 [1536, 1024], P('row', 'col'), may hold values from -6 to 6
Outputs:
- heights: float32 [1536, 1024], P('row', 'col')
- residual: float32 [1536, 1024], P('row', 'col')
All inputs are finite; a program needn't handle non-finite values.
Results may differ from a plain program's by a relative error of at most 0.0002.
Values sent between devices are 32-bit elements; how exact they have to be, the bound alone decides.
No kernel may reach another device: no remote copies, remote signals or barrier semaphores. Data moves between devices by JAX's collectives and lax.ppermute only.
A program may use at most 64 MiB of HBM per device.

v0:
```python
import jax
import jax.numpy as jnp
from jax import lax
from jax.sharding import PartitionSpec as P

ITERS = 3
SWEEPS = 4


damping = 2.0 / 3.0


def shifted(block, axis, distance):
    devices = range(lax.axis_size(axis))
    route = [(i - distance, i) for i in devices if i - distance in devices]
    return lax.ppermute(block, axis, route)


def with_halo(array, sides, width):
    for axis, dim in sides:
        size, length = (lax.axis_size(axis), array.shape[dim])
        up = [(i, (i + 1) % size) for i in range(size - 1)]
        down = [(j, i) for i, j in up]
        last = lax.slice_in_dim(array, length - width, length, axis=dim)
        first = lax.slice_in_dim(array, 0, width, axis=dim)
        before = lax.ppermute(last, axis, up)
        after = lax.ppermute(first, axis, down)
        array = jnp.concatenate([before, array, after], axis=dim)
    return array


def block_view(field):
    return field.reshape(field.shape[0] // 4, 4, field.shape[1] // 4, 4)


def sweep(padded, coarse, coeffs):
    centre = padded[1:-1, 1:-1]
    beside = coeffs[0] * padded[1:-1, :-2] + coeffs[1] * padded[1:-1, 2:]
    beside = beside + coeffs[2] * padded[:-2, 1:-1] + coeffs[3] * padded[2:, 1:-1]
    return (1.0 - damping) * centre + damping * coeffs[4] * (coarse + beside)


def paired_total(resid, smooth, image):
    return lax.psum((jnp.sum(resid * smooth), jnp.sum(smooth * image)), ("row", "col"))


def local(grad_x, grad_y, weight_x, weight_y, anchor, prior):
    tile_rows, tile_cols = grad_x.shape
    row_ids = lax.axis_index("row") * tile_rows + lax.broadcasted_iota(jnp.int32, grad_x.shape, 0)
    col_ids = lax.axis_index("col") * tile_cols + lax.broadcasted_iota(jnp.int32, grad_x.shape, 1)
    right_w = jnp.where(col_ids < tile_cols * lax.axis_size("col") - 1, weight_x, jnp.float32(0.0))
    down_w = jnp.where(row_ids < tile_rows * lax.axis_size("row") - 1, weight_y, jnp.float32(0.0))
    flux_x = right_w * grad_x
    flux_y = down_w * grad_y
    left_edge = shifted(jnp.stack([right_w[:, -1], flux_x[:, -1]]), "col", 1)
    top_edge = shifted(jnp.stack([down_w[-1, :], flux_y[-1, :]]), "row", 1)
    left_w = jnp.concatenate([left_edge[0][:, None], right_w[:, :-1]], 1)
    left_flux = jnp.concatenate([left_edge[1][:, None], flux_x[:, :-1]], 1)
    up_w = jnp.concatenate([top_edge[0][None, :], down_w[:-1, :]], 0)
    up_flux = jnp.concatenate([top_edge[1][None, :], flux_y[:-1, :]], 0)
    source = anchor * prior + left_flux - flux_x + up_flux - flux_y
    diag = anchor + left_w + right_w + up_w + down_w
    inverse = 1.0 / diag
    c_left = block_view(left_w)[:, :, :, 0].sum(1)
    c_right = block_view(right_w)[:, :, :, 3].sum(1)
    c_up = block_view(up_w)[:, 0, :, :].sum(2)
    c_down = block_view(down_w)[:, 3, :, :].sum(2)
    c_anchor = block_view(anchor).sum((1, 3))
    c_inverse = 1.0 / (c_anchor + c_left + c_right + c_up + c_down)
    coeffs = jnp.stack([c_left, c_right, c_up, c_down, c_inverse])

    def operate(field):
        padded = with_halo(field, (("row", 0), ("col", 1)), 1)
        beside = left_w * padded[1:-1, :-2] + right_w * padded[1:-1, 2:]
        beside = beside + up_w * padded[:-2, 1:-1] + down_w * padded[2:, 1:-1]
        return diag * field - beside

    def precondition(resid):
        coarse = block_view(resid).sum((1, 3))
        level = damping * coeffs[4] * coarse
        for turn in range(SWEEPS - 1):
            padded = with_halo(level, (("row", 0), ("col", 1)), 1)
            level = sweep(padded, coarse, coeffs)
        spread = jnp.broadcast_to(level[:, None, :, None], (level.shape[0], 4, level.shape[1], 4))
        return inverse * resid + spread.reshape(resid.shape)

    heights = jnp.zeros_like(source)
    residual = source
    smooth = precondition(residual)
    image = operate(smooth)
    agree, product = paired_total(residual, smooth, image)
    alpha = agree / product
    direction, along = (smooth, image)
    for step in range(ITERS):
        heights = heights + alpha * direction
        residual = residual - alpha * along
        if step + 1 < ITERS:
            smooth = precondition(residual)
            image = operate(smooth)
            agree_next, product = paired_total(residual, smooth, image)
            ratio = agree_next / agree
            alpha = agree_next / (product - ratio * agree_next / alpha)
            direction = smooth + ratio * direction
            along = image + ratio * along
            agree = agree_next
    return (heights, residual)


def solution(mesh):
    return jax.shard_map(
        local,
        mesh=mesh,
        in_specs=(
            P("row", "col"),
            P("row", "col"),
            P("row", "col"),
            P("row", "col"),
            P("row", "col"),
            P("row", "col"),
        ),
        out_specs=(P("row", "col"), P("row", "col")),
        check_vma=False,
    )
```

profile of v0, /device:TPU:0, one launch (start us, length us, event | category | flops | bytes accessed | tf_op | source)
XLA Modules:
  0.0 449.2 jit_solution(10927884112025161138)
XLA Ops:
  1.9 4.8 %collective-permute-start = (f32[2,96]{1,0:T(2,128)S(1)}, f32[2,96]{1,0:T(2,128)S(1)}, u32[]{:S(2)}, u32[]{:S(2)}) collective-permute-start(f32[2,96]{1,0:T(2,128)S(1)} %pad_maximum_fusion.117), channel_id=1, source_target_pairs={{0,1},{2,3},{4,5},{6,7},{8,9},{10,11},{12,13},{14,15},{16,17},{18,... | collective-permute-start | bytes 2312 | tf_op jit(solution)/shard_map/ppermute | solution.py:16
  9.4 7.9 %reshape.44 = f32[24,4,128,4]{3,2,1,0:T(8,128)} reshape(f32[96,512]{1,0:T(8,128)S(1)} %get-tuple-element.24) | data formatting | bytes 393216 | tf_op jit(solution)/shard_map/reshape | solution.py:33
  17.3 7.9 %reshape.42 = f32[24,4,128,4]{3,2,1,0:T(8,128)} reshape(f32[96,512]{1,0:T(8,128)S(1)} %get-tuple-element.22) | data formatting | bytes 393216 | tf_op jit(solution)/shard_map/reshape | solution.py:33
  25.1 4.9 %slice_reduce_fusion = f32[24,128]{1,0:T(8,128)S(1)} fusion(f32[24,4,128,4]{3,2,1,0:T(8,128)} %reshape.42), kind=kLoop, calls=%fused_computation | loop fusion | flops 9216 | bytes 61440 | tf_op jit(solution)/shard_map/reduce_sum | solution.py:65
  31.9 7.9 %reshape.40 = f32[24,4,128,4]{3,2,1,0:T(8,128)} reshape(f32[96,512]{1,0:T(8,128)S(1)} %copy-done) | data formatting | bytes 393216 | tf_op jit(solution)/shard_map/reshape | solution.py:33
  43.4 7.9 %reshape.41 = f32[24,4,128,4]{3,2,1,0:T(8,128)} reshape(f32[96,512]{1,0:T(8,128)S(1)} %pad_maximum_fusion.24) | data formatting | bytes 393216 | tf_op jit(solution)/shard_map/reshape | solution.py:33
  54.7 7.9 %reshape.43 = f32[24,4,128,4]{3,2,1,0:T(8,128)} reshape(f32[96,512]{1,0:T(8,128)S(1)} %pad_maximum_fusion.25) | data formatting | bytes 393216 | tf_op jit(solution)/shard_map/reshape | solution.py:33
  64.6 7.9 %reshape.45 = f32[24,4,128,4]{3,2,1,0:T(8,128)} reshape(f32[96,512]{1,0:T(8,128)S(1)} %fusion.26) | data formatting | bytes 393216 | tf_op jit(solution)/shard_map/reshape | solution.py:33
  85.6 4.2 collective-permute-done.5
  99.5 4.3 collective-permute-done.9
  114.0 4.2 collective-permute-done.13
  121.8 6.6 %reshape.46 = f32[96,512]{1,0:T(8,128)S(1)} reshape(f32[24,4,128,4]{3,2,1,0:T(8,128)} %broadcast_in_dim.12) | data formatting | bytes 393216 | tf_op jit(solution)/shard_map/reshape | solution.py:85
  139.9 4.3 collective-permute-done.17
  145.1 43.1 %all-reduce.2 = (f32[]{:T(128)}, f32[]{:T(128)}) all-reduce(f32[]{:T(128)} %get-tuple-element.7, f32[]{:T(128)} %get-tuple-element.6), channel_id=1, replica_groups=mesh['row'=16,'col'=2] {'row','col'}, use_global_device_ids=true, to_apply=%region_7.8 | all-reduce | flops 2 | bytes 16 | tf_op jit(solution)/shard_map/psum | solution.py:44
  189.6 7.9 %reshape.47 = f32[24,4,128,4]{3,2,1,0:T(8,128)} reshape(f32[96,512]{1,0:T(8,128)S(1)} %multiply_subtract_fusion.2) | data formatting | bytes 393216 | tf_op jit(solution)/shard_map/reshape | solution.py:33
  203.4 4.4 collective-permute-done.19
  248.9 6.6 %reshape.48 = f32[96,512]{1,0:T(8,128)S(1)} reshape(f32[24,4,128,4]{3,2,1,0:T(8,128)} %broadcast_in_dim.13) | data formatting | bytes 393216 | tf_op jit(solution)/shard_map/reshape | solution.py:85
  266.9 4.3 collective-permute-done.33
  272.1 43.1 %all-reduce.1 = (f32[]{:T(128)}, f32[]{:T(128)}) all-reduce(f32[]{:T(128)} %get-tuple-element.5, f32[]{:T(128)} %get-tuple-element.4), channel_id=1, replica_groups=mesh['row'=16,'col'=2] {'row','col'}, use_global_device_ids=true, to_apply=%region_12.13 | all-reduce | flops 2 | bytes 16 | tf_op jit(solution)/shard_map/psum | solution.py:44
  319.6 7.9 %reshape.49 = f32[24,4,128,4]{3,2,1,0:T(8,128)} reshape(f32[96,512]{1,0:T(8,128)S(1)} %multiply_subtract_fusion.1) | data formatting | bytes 393216 | tf_op jit(solution)/shard_map/reshape | solution.py:33
  333.4 4.4 collective-permute-done.35
  377.9 6.6 %reshape.50 = f32[96,512]{1,0:T(8,128)S(1)} reshape(f32[24,4,128,4]{3,2,1,0:T(8,128)} %broadcast_in_dim.26) | data formatting | bytes 393216 | tf_op jit(solution)/shard_map/reshape | solution.py:85
  395.9 4.3 collective-permute-done.49
  401.0 42.9 %all-reduce = (f32[]{:T(128)}, f32[]{:T(128)}) all-reduce(f32[]{:T(128)} %get-tuple-element.3, f32[]{:T(128)} %get-tuple-element.2), channel_id=1, replica_groups=mesh['row'=16,'col'=2] {'row','col'}, use_global_device_ids=true, to_apply=%region_17.18 | all-reduce | flops 2 | bytes 16 | tf_op jit(solution)/shard_map/psum | solution.py:44
  (176 shorter events, 182.1 us)
Async XLA Ops:
  1.9 41.2 %collective-permute-start = (f32[2,96]{1,0:T(2,128)S(1)}, f32[2,96]{1,0:T(2,128)S(1)}, u32[]{:S(2)}, u32[]{:S(2)}) collective-permute-start(f32[2,96]{1,0:T(2,128)S(1)} %pad_maximum_fusion.117), channel_id=1, source_target_pairs={{0,1},{2,3},{4,5},{6,7},{8,9},{10,11},{12,13},{14,15},{16,17},{18,... | collective-permute-start | bytes 2312 | tf_op jit(solution)/shard_map/ppermute | solution.py:16
  7.9 46.7 %collective-permute-start.1 = (f32[2,512]{1,0:T(2,128)S(1)}, f32[2,512]{1,0:T(2,128)S(1)}, u32[]{:S(2)}, u32[]{:S(2)}) collective-permute-start(f32[2,512]{1,0:T(2,128)S(1)} %pad_maximum_fusion.116), channel_id=1, source_target_pairs={{0,2},{2,4},{4,6},{6,8},{8,10},{10,12},{12,14},{14,16},{16,18},{18... | collective-permute-start | bytes 12296 | tf_op jit(solution)/shard_map/ppermute | solution.py:16
  75.8 5.3 %collective-permute-start.2 = (f32[1,128]{1,0:T(1,128)S(1)}, f32[1,128]{1,0:T(1,128)S(1)}, u32[]{:S(2)}, u32[]{:S(2)}) collective-permute-start(f32[1,128]{1,0:T(1,128)S(1)} %get-tuple-element.71), channel_id=1, source_target_pairs={{0,2},{2,4},{4,6},{6,8},{8,10},{10,12},{12,14},{14,16},{16,18},{18... | collective-permute-start | bytes 1544 | tf_op jit(solution)/shard_map/ppermute | solution.py:26
  84.2 5.6 %collective-permute-start.5 = (f32[26,1]{1,0:T(8,128)S(1)}, f32[26,1]{1,0:T(8,128)S(1)}, u32[]{:S(2)}, u32[]{:S(2)}) collective-permute-start(f32[26,1]{1,0:T(8,128)S(1)} %get-tuple-element.54), channel_id=1, source_target_pairs={{1,0},{3,2},{5,4},{7,6},{9,8},{11,10},{13,12},{15,14},{17,16},{19,... | collective-permute-start | bytes 320 | tf_op jit(solution)/shard_map/ppermute | solution.py:27
  98.2 5.6 %collective-permute-start.9 = (f32[26,1]{1,0:T(8,128)S(1)}, f32[26,1]{1,0:T(8,128)S(1)}, u32[]{:S(2)}, u32[]{:S(2)}) collective-permute-start(f32[26,1]{1,0:T(8,128)S(1)} %get-tuple-element.52), channel_id=1, source_target_pairs={{1,0},{3,2},{5,4},{7,6},{9,8},{11,10},{13,12},{15,14},{17,16},{19,... | collective-permute-start | bytes 320 | tf_op jit(solution)/shard_map/ppermute | solution.py:27
  112.6 5.6 %collective-permute-start.13 = (f32[26,1]{1,0:T(8,128)S(1)}, f32[26,1]{1,0:T(8,128)S(1)}, u32[]{:S(2)}, u32[]{:S(2)}) collective-permute-start(f32[26,1]{1,0:T(8,128)S(1)} %get-tuple-element.50), channel_id=1, source_target_pairs={{1,0},{3,2},{5,4},{7,6},{9,8},{11,10},{13,12},{15,14},{17,16},{19,... | collective-permute-start | bytes 320 | tf_op jit(solution)/shard_map/ppermute | solution.py:27
  128.6 4.5 %collective-permute-start.14 = (f32[1,512]{1,0:T(1,128)S(1)}, f32[1,512]{1,0:T(1,128)S(1)}, u32[]{:S(2)}, u32[]{:S(2)}) collective-permute-start(f32[1,512]{1,0:T(1,128)S(1)} %get-tuple-element.35), channel_id=1, source_target_pairs={{0,2},{2,4},{4,6},{6,8},{8,10},{10,12},{12,14},{14,16},{16,18},{18... | collective-permute-start | bytes 6152 | tf_op jit(solution)/shard_map/ppermute | solution.py:26
  131.8 4.6 %collective-permute-start.15 = (f32[1,512]{1,0:T(1,128)S(1)}, f32[1,512]{1,0:T(1,128)S(1)}, u32[]{:S(2)}, u32[]{:S(2)}) collective-permute-start(f32[1,512]{1,0:T(1,128)S(1)} %get-tuple-element.36), channel_id=1, source_target_pairs={{2,0},{4,2},{6,4},{8,6},{10,8},{12,10},{14,12},{16,14},{18,16},{20... | collective-permute-start | bytes 6152 | tf_op jit(solution)/shard_map/ppermute | solution.py:27
  138.2 6.0 %collective-permute-start.17 = (f32[98,1]{1,0:T(8,128)S(1)}, f32[98,1]{1,0:T(8,128)S(1)}, u32[]{:S(2)}, u32[]{:S(2)}) collective-permute-start(f32[98,1]{1,0:T(8,128)S(1)} %get-tuple-element.30), channel_id=1, source_target_pairs={{1,0},{3,2},{5,4},{7,6},{9,8},{11,10},{13,12},{15,14},{17,16},{19,... | collective-permute-start | bytes 1184 | tf_op jit(solution)/shard_map/ppermute | solution.py:27
  202.1 5.7 %collective-permute-start.19 = (f32[1,128]{1,0:T(1,128)S(1)}, f32[1,128]{1,0:T(1,128)S(1)}, u32[]{:S(2)}, u32[]{:S(2)}) collective-permute-start(f32[1,128]{1,0:T(1,128)S(1)} %get-tuple-element.66), channel_id=1, source_target_pairs={{2,0},{4,2},{6,4},{8,6},{10,8},{12,10},{14,12},{16,14},{18,16},{20... | collective-permute-start | bytes 1544 | tf_op jit(solution)/shard_map/ppermute | solution.py:27
  209.8 5.6 %collective-permute-start.21 = (f32[26,1]{1,0:T(8,128)S(1)}, f32[26,1]{1,0:T(8,128)S(1)}, u32[]{:S(2)}, u32[]{:S(2)}) collective-permute-start(f32[26,1]{1,0:T(8,128)S(1)} %get-tuple-element.48), channel_id=1, source_target_pairs={{1,0},{3,2},{5,4},{7,6},{9,8},{11,10},{13,12},{15,14},{17,16},{19,... | collective-permute-start | bytes 320 | tf_op jit(solution)/shard_map/ppermute | solution.py:27
  224.5 5.6 %collective-permute-start.25 = (f32[26,1]{1,0:T(8,128)S(1)}, f32[26,1]{1,0:T(8,128)S(1)}, u32[]{:S(2)}, u32[]{:S(2)}) collective-permute-start(f32[26,1]{1,0:T(8,128)S(1)} %get-tuple-element.46), channel_id=1, source_target_pairs={{1,0},{3,2},{5,4},{7,6},{9,8},{11,10},{13,12},{15,14},{17,16},{19,... | collective-permute-start | bytes 320 | tf_op jit(solution)/shard_map/ppermute | solution.py:27
  230.3 4.5 %collective-permute-start.26 = (f32[1,128]{1,0:T(1,128)S(1)}, f32[1,128]{1,0:T(1,128)S(1)}, u32[]{:S(2)}, u32[]{:S(2)}) collective-permute-start(f32[1,128]{1,0:T(1,128)S(1)} %get-tuple-element.61), channel_id=1, source_target_pairs={{0,2},{2,4},{4,6},{6,8},{8,10},{10,12},{12,14},{14,16},{16,18},{18... | collective-permute-start | bytes 1544 | tf_op jit(solution)/shard_map/ppermute | solution.py:26
  233.5 4.6 %collective-permute-start.27 = (f32[1,128]{1,0:T(1,128)S(1)}, f32[1,128]{1,0:T(1,128)S(1)}, u32[]{:S(2)}, u32[]{:S(2)}) collective-permute-start(f32[1,128]{1,0:T(1,128)S(1)} %get-tuple-element.62), channel_id=1, source_target_pairs={{2,0},{4,2},{6,4},{8,6},{10,8},{12,10},{14,12},{16,14},{18,16},{20... | collective-permute-start | bytes 1544 | tf_op jit(solution)/shard_map/ppermute | solution.py:27
  239.7 5.6 %collective-permute-start.29 = (f32[26,1]{1,0:T(8,128)S(1)}, f32[26,1]{1,0:T(8,128)S(1)}, u32[]{:S(2)}, u32[]{:S(2)}) collective-permute-start(f32[26,1]{1,0:T(8,128)S(1)} %get-tuple-element.44), channel_id=1, source_target_pairs={{1,0},{3,2},{5,4},{7,6},{9,8},{11,10},{13,12},{15,14},{17,16},{19,... | collective-permute-start | bytes 320 | tf_op jit(solution)/shard_map/ppermute | solution.py:27
  255.7 4.5 %collective-permute-start.30 = (f32[1,512]{1,0:T(1,128)S(1)}, f32[1,512]{1,0:T(1,128)S(1)}, u32[]{:S(2)}, u32[]{:S(2)}) collective-permute-start(f32[1,512]{1,0:T(1,128)S(1)} %get-tuple-element.33), channel_id=1, source_target_pairs={{0,2},{2,4},{4,6},{6,8},{8,10},{10,12},{12,14},{14,16},{16,18},{18... | collective-permute-start | bytes 6152 | tf_op jit(solution)/shard_map/ppermute | solution.py:26
  258.8 4.6 %collective-permute-start.31 = (f32[1,512]{1,0:T(1,128)S(1)}, f32[1,512]{1,0:T(1,128)S(1)}, u32[]{:S(2)}, u32[]{:S(2)}) collective-permute-start(f32[1,512]{1,0:T(1,128)S(1)} %get-tuple-element.34), channel_id=1, source_target_pairs={{2,0},{4,2},{6,4},{8,6},{10,8},{12,10},{14,12},{16,14},{18,16},{20... | collective-permute-start | bytes 6152 | tf_op jit(solution)/shard_map/ppermute | solution.py:27
  265.2 6.0 %collective-permute-start.33 = (f32[98,1]{1,0:T(8,128)S(1)}, f32[98,1]{1,0:T(8,128)S(1)}, u32[]{:S(2)}, u32[]{:S(2)}) collective-permute-start(f32[98,1]{1,0:T(8,128)S(1)} %get-tuple-element.28), channel_id=1, source_target_pairs={{1,0},{3,2},{5,4},{7,6},{9,8},{11,10},{13,12},{15,14},{17,16},{19,... | collective-permute-start | bytes 1184 | tf_op jit(solution)/shard_map/ppermute | solution.py:27
  332.1 5.7 %collective-permute-start.35 = (f32[1,128]{1,0:T(1,128)S(1)}, f32[1,128]{1,0:T(1,128)S(1)}, u32[]{:S(2)}, u32[]{:S(2)}) collective-permute-start(f32[1,128]{1,0:T(1,128)S(1)} %get-tuple-element.60), channel_id=1, source_target_pairs={{2,0},{4,2},{6,4},{8,6},{10,8},{12,10},{14,12},{16,14},{18,16},{20... | collective-permute-start | bytes 1544 | tf_op jit(solution)/shard_map/ppermute | solution.py:27
  340.0 5.6 %collective-permute-start.37 = (f32[26,1]{1,0:T(8,128)S(1)}, f32[26,1]{1,0:T(8,128)S(1)}, u32[]{:S(2)}, u32[]{:S(2)}) collective-permute-start(f32[26,1]{1,0:T(8,128)S(1)} %get-tuple-element.42), channel_id=1, source_target_pairs={{1,0},{3,2},{5,4},{7,6},{9,8},{11,10},{13,12},{15,14},{17,16},{19,... | collective-permute-start | bytes 320 | tf_op jit(solution)/shard_map/ppermute | solution.py:27
  354.3 5.6 %collective-permute-start.41 = (f32[26,1]{1,0:T(8,128)S(1)}, f32[26,1]{1,0:T(8,128)S(1)}, u32[]{:S(2)}, u32[]{:S(2)}) collective-permute-start(f32[26,1]{1,0:T(8,128)S(1)} %get-tuple-element.40), channel_id=1, source_target_pairs={{1,0},{3,2},{5,4},{7,6},{9,8},{11,10},{13,12},{15,14},{17,16},{19,... | collective-permute-start | bytes 320 | tf_op jit(solution)/shard_map/ppermute | solution.py:27
  368.7 5.6 %collective-permute-start.45 = (f32[26,1]{1,0:T(8,128)S(1)}, f32[26,1]{1,0:T(8,128)S(1)}, u32[]{:S(2)}, u32[]{:S(2)}) collective-permute-start(f32[26,1]{1,0:T(8,128)S(1)} %get-tuple-element.38), channel_id=1, source_target_pairs={{1,0},{3,2},{5,4},{7,6},{9,8},{11,10},{13,12},{15,14},{17,16},{19,... | collective-permute-start | bytes 320 | tf_op jit(solution)/shard_map/ppermute | solution.py:27
  387.8 4.6 %collective-permute-start.47 = (f32[1,512]{1,0:T(1,128)S(1)}, f32[1,512]{1,0:T(1,128)S(1)}, u32[]{:S(2)}, u32[]{:S(2)}) collective-permute-start(f32[1,512]{1,0:T(1,128)S(1)} %get-tuple-element.32), channel_id=1, source_target_pairs={{2,0},{4,2},{6,4},{8,6},{10,8},{12,10},{14,12},{16,14},{18,16},{20... | collective-permute-start | bytes 6152 | tf_op jit(solution)/shard_map/ppermute | solution.py:27
  394.1 6.0 %collective-permute-start.49 = (f32[98,1]{1,0:T(8,128)S(1)}, f32[98,1]{1,0:T(8,128)S(1)}, u32[]{:S(2)}, u32[]{:S(2)}) collective-permute-start(f32[98,1]{1,0:T(8,128)S(1)} %get-tuple-element.26), channel_id=1, source_target_pairs={{1,0},{3,2},{5,4},{7,6},{9,8},{11,10},{13,12},{15,14},{17,16},{19,... | collective-permute-start | bytes 1184 | tf_op jit(solution)/shard_map/ppermute | solution.py:27
  (28 other events, 119.8 us)
where the time goes:
time: 451 us; the launch traced here: 449 us
  blocking collectives  129 us (29%)
  local copies, waits for them, and re-layouts  94.5 us (21%)
  waiting for transfers between devices  90.8 us (20%)
  starting transfers between devices  90.6 us (20%)
  other arithmetic  33.2 us (7%)
  between operations  11 us (2%)
    psum x3, blocking collectives, paired_total(): lax.psum((jnp.sum(resid * smooth), jnp.sum(smooth * image)), ('row', 'col'))  129 us
    ppermute x24, waiting for transfers between devices, with_halo(): after = lax.ppermute(first, axis, down)  88.4 us
    reshape x8, local copies, waits for them, and re-layouts, block_view(): return field.reshape(field.shape[0] // 4, 4, field.shape[1] // 4, 4)  63 us
    ppermute x24, starting transfers between devices, with_halo(): before = lax.ppermute(last, axis, up)  53.3 us
    ppermute x24, starting transfers between devices, with_halo(): after = lax.ppermute(first, axis, down)  31 us
    reshape x3, local copies, waits for them, and re-layouts, precondition(): return inverse * resid + spread.reshape(resid.shape)  19.9 us
    broadcast_in_dim x3, local copies, waits for them, and re-layouts, precondition(): jnp.broadcast_to(level[:, None, :, None], (level.shape[0], 4, level.shape...  10.4 us
    reduce_sum x3, other arithmetic, precondition(): coarse = block_view(resid).sum((1, 3))  9.84 us
  transfers between devices with their start and end apart: 50, of which 35 were waited for; matrix products, arithmetic and copies ran while one was open for 10% of the time, Pallas kernels for 0%

commit v1 on v0

v1 whole, which is shorter than its diff:
```python
import functools

import jax
import jax.numpy as jnp
from jax import lax
from jax.experimental import pallas as pl
from jax.experimental.pallas import tpu as pltpu
from jax.sharding import PartitionSpec as P

DAMP = 2.0 / 3.0
SHIFT = 1.0
HC = 64
HR = 20
FG = 24
GUARD = 8
VMEM = pl.BlockSpec(memory_space=pltpu.VMEM)
SMEM = pl.BlockSpec(memory_space=pltpu.SMEM)
F32 = jnp.float32


def lanes(shape):
    return lax.broadcasted_iota(jnp.int32, shape, 1)


def rows(shape):
    return lax.broadcasted_iota(jnp.int32, shape, 0)


def left_of(x, k=1):
    return pltpu.roll(x, k, 1)


def right_of(x, k=1):
    return pltpu.roll(x, x.shape[1] - k, 1)


def group_sum(x):
    lane = lanes(x.shape)
    x = x + jnp.where(lane % 2 == 0, right_of(x), left_of(x))
    return x + jnp.where(lane % 4 < 2, right_of(x, 2), left_of(x, 2))


def ld(ref, start, count=8, step=1):
    rows_of = pl.ds(start, count, stride=step) if step > 1 else slice(start, start + count)
    return jnp.concatenate([ref[j, rows_of, :] for j in range(ref.shape[0])], axis=1)


def st(ref, start, value, step=1):
    count = value.shape[0]
    rows_of = pl.ds(start, count, stride=step) if step > 1 else slice(start, start + count)
    for j in range(ref.shape[0]):
        ref[j, rows_of, :] = value[:, j * 128 : (j + 1) * 128]


def four_rows(ref, start, count):
    parts = [ld(ref, start + k, count, 4) for k in range(4)]
    return (parts[0] + parts[1]) + (parts[2] + parts[3])


def pack_columns(flags, gx, gy, wx, wy, an, pr, out):
    n = gx.shape[0]
    last = flags[0] == 1
    shape = gx.shape
    row, lane = rows(shape), lanes(shape)
    w_x = wx[...]
    w_y = jnp.where((row == n - 1) & (flags[1] == 1), F32(0.0), wy[...])
    fx = w_x * gx[...]
    fy = w_y * gy[...]
    a = an[...]
    before_x = jnp.where(lane == 0, F32(0.0), left_of(fx))
    before_y = jnp.where(row == 0, F32(0.0), pltpu.roll(fy, 1, 0))
    src = a * pr[...] + before_x - fx + before_y - fy

    def pair(x, y):
        low = jnp.where(lane < HC, x, left_of(y, HC))
        high = jnp.where(lane < HC, left_of(x, HC), y)
        return jnp.where(last, high, low)

    first = pair(src, w_x)
    edge = jnp.broadcast_to(fx[:, 127:128], shape)
    out[0:n, 0:128] = jnp.where((lane == 0) & last, edge, first)
    out[0:n, 128:256] = pair(w_y, a)
    tail = jnp.broadcast_to(pair(fy, fy)[n - 1 : n, :], (8, 128))
    out[n : n + 8, 0:128] = tail
    out[n : n + 8, 128:256] = tail


def pack_rows(has_outer, flags, gx, gy, wx, wy, an, pr, *refs):
    inner, refs = refs[0], refs[1:]
    outer = None
    if has_outer:
        outer, refs = refs[0], refs[1:]
    msg_in, msg_out, r_o, wx_o, wy_o, an_o, fy_o, u_s, t_s, tops = refs
    n, width = gx.shape
    ext = width + 2 * HC
    odd = flags[0] == 1
    end_col = flags[1] == 1
    end_row = flags[2] == 1
    row_odd = flags[3] == 1
    lane = lanes((8, width))
    elane = lanes((8, ext))
    row = rows((8, width))
    zero = F32(0.0)

    def sides(r, c):
        x = inner[r : r + 8, c : c + 128]
        y = outer[r : r + 8, c : c + 128] if has_outer else jnp.zeros_like(x)
        return jnp.where(odd, x, y), jnp.where(odd, y, x)

    carry = jnp.zeros((1, width), F32)
    for r in range(0, n, 8):
        w_x = jnp.where((lane == width - 1) & end_col, zero, wx[r : r + 8, :])
        w_y = wy[r : r + 8, :]
        if r == n - 8:
            w_y = jnp.where((row == 7) & end_row, zero, w_y)
        fx = w_x * gx[r : r + 8, :]
        fy = w_y * gy[r : r + 8, :]
        a = an[r : r + 8, :]
        before_x = jnp.where(lane == 0, zero, left_of(fx))
        before_y = jnp.where(row == 0, jnp.broadcast_to(carry, fy.shape), pltpu.roll(fy, 1, 0))
        carry = fy[7:8, :]
        src = a * pr[r : r + 8, :] + before_x - fx + before_y - fy
        left_a, right_a = sides(r, 0)
        left_b, right_b = sides(r, 128)
        src_e = jnp.concatenate([left_a[:, :HC], src, right_a[:, :HC]], axis=1)
        incoming = jnp.broadcast_to(left_a[:, 0:1], src_e.shape)
        outgoing = jnp.broadcast_to(fx[:, width - 1 : width], src_e.shape)
        src_e = src_e + jnp.where(elane == HC, incoming, jnp.where(elane == HC + width, outgoing, zero))
        st(r_o, r, jnp.where(elane == 0, zero, src_e))
        st(wx_o, r, jnp.concatenate([left_a[:, HC:], w_x, right_a[:, HC:]], axis=1))
        st(wy_o, r, jnp.concatenate([left_b[:, :HC], w_y, right_b[:, :HC]], axis=1))
        st(an_o, r, jnp.concatenate([left_b[:, HC:], a, right_b[:, HC:]], axis=1))
    left_f, right_f = sides(n, 0)
    tail = jnp.broadcast_to(carry, (8, width))
    fy_e = jnp.concatenate([left_f[:, :HC], tail, right_f[:, :HC]], axis=1)
    st(fy_o, 0, fy_e)

    lo, hi = 16, n - 32
    for base in (lo, hi):
        for r in range(base - 8, base + 24, 8):
            w_x, w_y = ld(wx_o, r), ld(wy_o, r)
            diag = ld(an_o, r) + w_x + left_of(w_x) + w_y + ld(wy_o, r - 1)
            st(u_s, r, jnp.where(diag > zero, ld(r_o, r) / diag, zero))
        for r in range(base, base + 16, 8):
            st(t_s, r, apply_a(u_s, wx_o, wy_o, an_o, r))
    four = lanes((4, ext)) % 4
    packed_s = []
    for base in (lo, hi):
        s = group_sum(four_rows(t_s, base, 4))
        keep = jnp.where(four == rows((4, ext)), s, zero)
        packed_s.append((keep[0:1] + keep[1:2]) + (keep[2:3] + keep[3:4]))
    count = (n - 2 * lo) // 4
    four = lanes((count, ext)) % 4
    c_r = group_sum(jnp.where(four == 3, four_rows(wx_o, lo, count), zero))
    c_d = group_sum(ld(wy_o, lo + 3, count, 4))
    c_a = group_sum(four_rows(an_o, lo, count))
    g = group_sum(four_rows(r_o, lo, count))
    packed = jnp.where(four < 2, jnp.where(four == 0, g, c_r), jnp.where(four == 2, c_d, c_a))

    top, bottom = tops.at[0], tops.at[1]
    for k, ref in enumerate((r_o, wx_o, wy_o, an_o)):
        top[:, k * HR : (k + 1) * HR, :] = ref[:, 0:HR, :]
        bottom[:, k * HR : (k + 1) * HR, :] = ref[:, n - HR : n, :]
    st(top, HR - 1, packed_s[0])
    st(bottom, 0, packed_s[1])
    st(bottom, HR, c_d[count - 9 : count - 8, :])
    st(bottom, 3 * HR, fy_e[0:1, :])
    st(top, 4 * HR, packed[0:8, :])
    st(bottom, 4 * HR, packed[count - 8 :, :])

    @pl.when(row_odd)
    def _():
        msg_in[...] = top[...]
        msg_out[...] = bottom[...]

    @pl.when(jnp.logical_not(row_odd))
    def _():
        msg_in[...] = bottom[...]
        msg_out[...] = top[...]


def apply_a(v, w_x, w_y, an, r):
    x = ld(v, r)
    flow = ld(w_x, r) * (x - right_of(x))
    down = ld(w_y, r) * (x - ld(v, r + 1))
    up = ld(w_y, r - 1) * (x - ld(v, r - 1))
    return (ld(an, r) * x + (flow - left_of(flow))) + (down + up)


def main(flags, r_i, wx_i, wy_i, an_i, fy_i, msg_in, msg_out, mom, p0, p1, p2, q0, q1, q2, r0,
         R, WX, WY, AN, DI, SP, PA, PB, QA, C_L, C_R, C_D, C_A, C_I, EA, EB, GC):
    blocks, n, _ = r_i.shape
    ext = blocks * 128
    fine = n + 2 * FG
    coarse = fine // 4 + 12
    zero = F32(0.0)
    odd = flags[3] == 1
    B = GUARD

    def sides(a, b):
        x, y = ld(msg_in, a, b - a), ld(msg_out, a, b - a)
        return jnp.where(odd, x, y), jnp.where(odd, y, x)

    zeros = jnp.zeros((B, ext), F32)
    for ref in (R, WX, WY, AN, PA, PB):
        st(ref, 0, zeros)
        st(ref, B + fine, zeros)
    for k, (ref, own) in enumerate(((R, r_i), (WX, wx_i), (WY, wy_i), (AN, an_i))):
        up, down = sides(k * HR, (k + 1) * HR)
        st(ref, B, zeros[: FG - HR])
        st(ref, B + FG + n + HR, zeros[: FG - HR])
        st(ref, B + FG - HR, up)
        st(ref, B + FG + n, down)
        for r in range(0, n, 8):
            st(ref, B + FG + r, ld(own, r))
    flux_up, _ = sides(3 * HR, 3 * HR + 1)
    st(R, B + FG, ld(R, B + FG, 1) + flux_up)
    st(R, B + FG + n, ld(R, B + FG + n, 1) + ld(fy_i, 0, 1))

    for r in range(B, B + fine, 8):
        w_x, w_y = ld(WX, r), ld(WY, r)
        diag = ld(AN, r) + w_x + left_of(w_x) + w_y + ld(WY, r - 1)
        st(DI, r, jnp.where(diag > zero, F32(1.0) / diag, zero))

    for ref in (EA, EB, C_D):
        st(ref, 0, zeros)
        st(ref, B + coarse, zeros)
    up, down = sides(4 * HR, 4 * HR + 8)
    four = lanes((8, ext)) % 4
    for k, ref in enumerate((GC, C_R, C_D, C_A)):
        st(ref, B, group_sum(jnp.where(four == k, up, zero)))
        st(ref, B + coarse - 8, group_sum(jnp.where(four == k, down, zero)))
    beyond, _ = sides(HR, HR + 1)
    st(C_D, B - 1, beyond)
    for c in range(8, coarse - 8, 8):
        f = B + 4 * c - 24
        st(GC, B + c, group_sum(four_rows(R, f, 8)))
        st(C_R, B + c, group_sum(jnp.where(four == 3, four_rows(WX, f, 8), zero)))
        st(C_D, B + c, group_sum(ld(WY, f + 3, 8, 4)))
        st(C_A, B + c, group_sum(four_rows(AN, f, 8)))
    for c in range(B, B + coarse, 8):
        c_r = ld(C_R, c)
        c_l = left_of(c_r, 4)
        total = ld(C_A, c) + c_l + c_r + ld(C_D, c - 1) + ld(C_D, c)
        st(C_L, c, c_l)
        st(C_I, c, jnp.where(total > zero, F32(DAMP) / total, zero))

    def smooth(lo, hi):
        for c in range(lo, hi, 8):
            st(EA, B + c, ld(C_I, B + c) * ld(GC, B + c))
        if lo > 0:
            st(EA, B + lo - 8, zeros)
            st(EB, B + lo - 8, zeros)
        if hi < coarse:
            st(EA, B + hi, zeros)
            st(EB, B + hi, zeros)
        old, new = EA, EB
        for turn in range(3):
            for c in range(B + lo, B + hi, 8):
                e = ld(old, c)
                beside = ld(C_L, c) * left_of(e, 4) + ld(C_R, c) * right_of(e, 4)
                beside = beside + (ld(C_D, c - 1) * ld(old, c - 1) + ld(C_D, c) * ld(old, c + 1))
                st(new, c, F32(1.0 - DAMP) * e + ld(C_I, c) * (ld(GC, c) + beside))
            old, new = new, old
        first, last = max(lo, 6), min(hi, coarse - 6)
        count = last - first
        for k in range(4):
            st(SP, B + 4 * (first - 6) + k, ld(EB, B + first, count), 4)

    def restrict(q):
        for c in range(8, coarse - 8, 8):
            st(GC, B + c, group_sum(four_rows(q, B + 4 * c - 24, 8)))

    smooth(0, coarse)
    for r in range(B, B + fine, 8):
        st(PA, r, ld(DI, r) * ld(R, r) + ld(SP, r))
    for r in range(B, B + fine, 8):
        st(QA, r, apply_a(PA, WX, WY, AN, r))
    restrict(QA)
    s_up, _ = sides(0, 1)
    _, s_down = sides(HR - 1, HR)
    for c, s, off in ((0, s_up, 4), (coarse - 8, s_down, 0)):
        part = jnp.where(four == rows((8, ext)) - off, jnp.broadcast_to(s, (8, ext)), zero)
        c = B + c
        e = ld(EB, c)
        image = ld(C_A, c) * e + ld(C_L, c) * (e - left_of(e, 4)) + ld(C_R, c) * (e - right_of(e, 4))
        image = image + ld(C_D, c - 1) * (e - ld(EB, c - 1))
        image = image + ld(C_D, c) * (e - ld(EB, c + 1))
        st(GC, c, group_sum(part) + image)
    for r in range(0, n, 8):
        f = B + FG + r
        st(p0, r, ld(PA, f))
        st(q0, r, ld(QA, f))
        st(r0, r, ld(R, f))
    smooth(0, coarse)
    for r in range(B, B + fine, 8):
        st(PB, r, (ld(DI, r) * ld(QA, r) + ld(SP, r)) - F32(SHIFT) * ld(PA, r))
    for r in range(B + 8, B + fine - 8, 8):
        st(QA, r, apply_a(PB, WX, WY, AN, r))
    restrict(QA)
    for r in range(0, n, 8):
        f = B + FG + r
        st(p1, r, ld(PB, f))
        st(q1, r, ld(QA, f))
    smooth(8, coarse - 8)
    for r in range(B + FG - 8, B + FG + n + 8, 8):
        st(PA, r, (ld(DI, r) * ld(QA, r) + ld(SP, r)) - F32(SHIFT) * ld(PB, r))
    own = (lanes((8, ext)) >= HC) & (lanes((8, ext)) < ext - HC)
    acc = [jnp.zeros((8, 128), F32) for _ in range(9)]
    for r in range(0, n, 8):
        f = B + FG + r
        z2 = ld(PA, f)
        image = apply_a(PA, WX, WY, AN, f)
        st(p2, r, z2)
        st(q2, r, image)
        z0, z1 = ld(p0, r), ld(p1, r)
        i0, i1, i2, res = [jnp.where(own, x, zero) for x in (ld(q0, r), ld(q1, r), image, ld(r0, r))]
        pairs = ((z0, i0), (z1, i0), (z1, i1), (z2, i0), (z2, i1), (z2, i2), (z0, res), (z1, res), (z2, res))
        for k, (x, y) in enumerate(pairs):
            prod = x * y
            parts = [prod[:, j : j + 128] for j in range(0, ext, 128)]
            while len(parts) > 1:
                parts = [sum(parts[j : j + 2][1:], parts[j]) for j in range(0, len(parts), 2)]
            acc[k] = acc[k] + parts[0]
    lane = lanes((8, 128))
    line = jnp.zeros((8, 128), F32)
    for k in range(9):
        total = jnp.sum(jnp.sum(acc[k], axis=0, keepdims=True), axis=1, keepdims=True)
        line = jnp.where(lane == k, jnp.broadcast_to(total, (8, 128)), line)
    for j in range(mom.shape[0]):
        mom[j] = line


def combine(mom, p0, p1, p2, q0, q1, q2, r0, heights, residual):
    blocks, n, _ = p0.shape
    ext = blocks * 128
    parts = [mom[j] for j in range(mom.shape[0])]
    while len(parts) > 1:
        parts = [sum(parts[j : j + 2][1:], parts[j]) for j in range(0, len(parts), 2)]
    tot = parts[0]
    m = [jnp.broadcast_to(tot[:, k : k + 1], (8, 128)) for k in range(9)]
    g00, g10, g11, g20, g21, g22, b0, b1, b2 = m
    l10, l20 = g10 / g00, g20 / g00
    d1 = g11 - l10 * g10
    t21 = g21 - l20 * g10
    l21 = t21 / d1
    d2 = g22 - l20 * g20 - l21 * t21
    y1 = b1 - l10 * b0
    y2 = b2 - l20 * b0 - l21 * y1
    x2 = y2 / d2
    x1 = y1 / d1 - l21 * x2
    x0 = b0 / g00 - l10 * x1 - l20 * x2
    reps = ext // 128
    x0, x1, x2 = [jnp.concatenate([x] * reps, axis=1) for x in (x0, x1, x2)]
    for r in range(0, n, 8):
        at = slice(r, r + 8)
        h = x0 * ld(p0, r) + x1 * ld(p1, r) + x2 * ld(p2, r)
        s = ld(r0, r) - (x0 * ld(q0, r) + x1 * ld(q1, r) + x2 * ld(q2, r))
        heights[at, :] = h[:, HC : ext - HC]
        residual[at, :] = s[:, HC : ext - HC]


def swap(x, axis, size, inner):
    if inner:
        pairs = [(i, i ^ 1) for i in range(size) if i ^ 1 < size]
    else:
        pairs = [(i, j) for i in range(size) for j in [((i + 1) ^ 1) - 1] if 0 <= j < size]
    return lax.ppermute(x, axis, pairs)


def local(nrow, ncol, gx, gy, wx, wy, an, pr):
    n, width = gx.shape
    ext = width + 2 * HC
    row, col = lax.axis_index("row"), lax.axis_index("col")
    flags = jnp.stack([col % 2, jnp.int32(col == ncol - 1), jnp.int32(row == nrow - 1), row % 2]).astype(jnp.int32)
    fields = (gx, gy, wx, wy, an, pr)
    blocks = width // 128

    def edge_columns(last):
        edge = jnp.stack([jnp.int32(last), jnp.int32(row == nrow - 1)])
        spec = pl.BlockSpec((n, 128), lambda i, s: (0, s[0] * (blocks - 1)))
        return pl.pallas_call(
            pack_columns,
            grid_spec=pltpu.PrefetchScalarGridSpec(
                num_scalar_prefetch=1,
                grid=(1,),
                in_specs=[spec] * 6,
                out_specs=pl.BlockSpec((n + 8, 256), lambda i, s: (0, 0)),
            ),
            out_shape=jax.ShapeDtypeStruct((n + 8, 256), F32),
            name="edge_columns",
        )(edge, *fields)

    halos = [swap(edge_columns(col % 2 == 0), "col", ncol, True)]
    if ncol > 2:
        halos.append(swap(edge_columns(col % 2 == 1), "col", ncol, False))
    depth = 4 * HR + 8
    nb = ext // 128
    tile = jax.ShapeDtypeStruct((nb, n, 128), F32)
    msg = jax.ShapeDtypeStruct((nb, depth, 128), F32)
    line = jax.ShapeDtypeStruct((nb, 8, 128), F32)
    limit = pltpu.CompilerParams(vmem_limit_bytes=48 * 1024 * 1024)
    to_in, to_out, *ext_fields = pl.pallas_call(
        functools.partial(pack_rows, len(halos) > 1),
        in_specs=[SMEM] + [VMEM] * (6 + len(halos)),
        out_specs=[VMEM] * 7,
        out_shape=[msg, msg, tile, tile, tile, tile, line],
        scratch_shapes=[pltpu.VMEM((nb, n, 128), F32)] * 2 + [pltpu.VMEM((2, nb, depth, 128), F32)],
        compiler_params=limit,
        name="edge_rows",
    )(flags, *fields, *halos)
    from_in = swap(to_in, "row", nrow, True)
    from_out = swap(to_out, "row", nrow, False)
    fine = n + 2 * FG
    coarse = fine // 4 + 12
    big = pltpu.VMEM((nb, fine + 2 * GUARD, 128), F32)
    small = pltpu.VMEM((nb, coarse + 2 * GUARD, 128), F32)
    devices = nrow * ncol
    mom, *vectors = pl.pallas_call(
        main,
        in_specs=[SMEM] + [VMEM] * 7,
        out_specs=[VMEM] * 8,
        out_shape=[jax.ShapeDtypeStruct((devices, 8, 128), F32)] + [tile] * 7,
        scratch_shapes=[big] * 9 + [small] * 8,
        compiler_params=limit,
        name="basis",
    )(flags, *ext_fields, from_in, from_out)
    mom = lax.all_to_all(mom, ("row", "col"), 0, 0, tiled=True)
    out = jax.ShapeDtypeStruct((n, width), F32)
    return tuple(
        pl.pallas_call(
            combine,
            in_specs=[VMEM] * 8,
            out_specs=[VMEM] * 2,
            out_shape=[out, out],
            compiler_params=limit,
            name="combine",
        )(mom, *vectors)
    )


def solution(mesh):
    spec = P("row", "col")
    return jax.shard_map(
        functools.partial(local, mesh.shape["row"], mesh.shape["col"]),
        mesh=mesh,
        in_specs=(spec,) * 6,
        out_specs=(spec, spec),
        check_vma=False,
    )
```

time: 451 us -> 44.6 us (0.10)
  blocking collectives: 129 us -> 21.9 us
  local copies, waits for them, and re-layouts: 94.5 us -> 0.03 us
  starting transfers between devices: 90.6 us -> 3.68 us
  waiting for transfers between devices: 90.8 us -> 3.89 us
  other arithmetic: 33.2 us -> 0.66 us
  Pallas kernels: 0 us -> 13.5 us
  between operations: 11 us -> 0.73 us
    psum x3 -> x0, blocking collectives: 129 us -> none  [paired_total(): lax.psum((jnp.sum(resid * smooth), jnp.sum(smooth * image)), ('row', 'col'))]
    ppermute x50 -> x3, starting transfers between devices: 90.6 us -> 3.68 us  [swap(): return lax.ppermute(x, axis, pairs)]
    ppermute x50 -> x3, waiting for transfers between devices: 90.8 us -> 3.89 us  [swap(): return lax.ppermute(x, axis, pairs)]
    reshape x11 -> x0, local copies, waits for them, and re-layouts: 82.9 us -> none  [the longest x8 63 us: block_view(): return field.reshape(field.shape[0] // 4, 4, field.shape[1] // 4, 4)]
    reduce_sum x11 -> x0, other arithmetic: 27.8 us -> none  [the longest x3 9.84 us: precondition(): coarse = block_view(resid).sum((1, 3))]
    all_to_all x0 -> x1, blocking collectives: none -> 21.9 us  [local(): mom = lax.all_to_all(mom, ('row', 'col'), 0, 0, tiled=True)]
    pallas_call x0 -> x4, Pallas kernels: none -> 13.5 us  [the longest x1 7.25 us: local(): pl.pallas_call(main, in_specs=[SMEM] + [VMEM] * 7, out_specs=[VMEM] * 8,...]
    broadcast_in_dim x3 -> x0, local copies, waits for them, and re-layouts: 10.4 us -> none  [precondition(): jnp.broadcast_to(level[:, None, :, None], (level.shape[0], 4, level.shape...]
  transfers between devices with their start and end apart: 50 -> 3, of which waited for: 35 -> 2; matrix products, arithmetic and copies ran while one was open for 10% -> 0% of each run, Pallas kernels for 0% -> 0%
where the time goes in v1:
time: 44.6 us; the launch traced here: 44.4 us
  blocking collectives  21.9 us (49%)
  Pallas kernels  13.5 us (30%)
  waiting for transfers between devices  3.89 us (9%)
  starting transfers between devices  3.68 us (8%)
  between operations  0.73 us (2%)
  other arithmetic  0.66 us (1%)
    all_to_all x1, blocking collectives, local(): mom = lax.all_to_all(mom, ('row', 'col'), 0, 0, tiled=True)  21.9 us
    pallas_call x1, Pallas kernels, local(): pl.pallas_call(main, in_specs=[SMEM] + [VMEM] * 7, out_specs=[VMEM] * 8,...  7.25 us
    ppermute x3, waiting for transfers between devices, swap(): return lax.ppermute(x, axis, pairs)  3.89 us
    ppermute x3, starting transfers between devices, swap(): return lax.ppermute(x, axis, pairs)  3.68 us
    pallas_call x1, Pallas kernels, local(): pl.pallas_call(functools.partial(pack_rows, len(halos) > 1), in_specs=[SM...  2.73 us
    pallas_call x1, Pallas kernels, edge_columns(): pl.pallas_call(pack_columns, grid_spec=pltpu.PrefetchScalarGridSpec(num_s...  2.52 us
    pallas_call x1, Pallas kernels, local(): pl.pallas_call(combine, in_specs=[VMEM] * 8, out_specs=[VMEM] * 2, out_sh...  1.04 us
  transfers between devices with their start and end apart: 3, of which 2 were waited for; matrix products, arithmetic and copies ran while one was open for 0% of the time, Pallas kernels for 0%

profile of v1, /device:TPU:0, one launch (start us, length us, event | category | flops | bytes accessed | tf_op | source)
XLA Modules:
  0.0 44.4 jit_solution(14568746175118641750)
XLA Ops:
  0.6 0.6 %pad_add_fusion.1.flags = s32[2]{0:T(128)} fusion(s32[1]{0:T(128)} %bitcast.2, s32[1]{0:T(128)} %bitcast.4), kind=kLoop, calls=%fused_computation.1 | loop fusion | flops 2 | bytes 16 | tf_op jit(solution)/shard_map/stack | solution.py:380
  1.2 0.0 copy-start
  1.2 0.0 copy-start.1
  1.2 0.0 copy-start.2
  1.2 0.0 copy-start.4
  1.3 0.0 copy-start.5
  1.3 2.5 %edge_columns.1 = f32[104,256]{1,0:T(8,128)} custom-call(s32[2]{0:T(128)} %pad_add_fusion.1.flags, f32[96,512]{1,0:T(8,128)} %gx.3, f32[96,512]{1,0:T(8,128)} %gy.3, f32[96,512]{1,0:T(8,128)} %wx.3, f32[96,512]{1,0:T(8,128)} %wy.3, f32[96,512]{1,0:T(8,128)} %an.3, f32[96,512]{1,0:T(8,128)} %pr.3), custom_call_target="tpu_custom_call" | custom-call | tf_op jit(solution)/shard_map/edge_columns/pallas_call | solution.py:382
  3.8 2.9 %collective-permute-start = (f32[104,256]{1,0:T(8,128)}, f32[104,256]{1,0:T(8,128)S(1)}, u32[]{:S(2)}, u32[]{:S(2)}) collective-permute-start(f32[104,256]{1,0:T(8,128)} %edge_columns.1), channel_id=1, source_target_pairs={{0,1},{1,0},{2,3},{3,2},{4,5},{5,4},{6,7},{7,6},{8,9},{9,8},{10,11... | collective-permute-start | bytes 319496 | tf_op jit(solution)/shard_map/ppermute | solution.py:368
  6.7 0.1 pad_add_fusion.flags
  6.8 3.1 %collective-permute-done.refs_0_ = f32[104,256]{1,0:T(8,128)S(1)} collective-permute-done((f32[104,256]{1,0:T(8,128)}, f32[104,256]{1,0:T(8,128)S(1)}, u32[]{:S(2)}, u32[]{:S(2)}) %collective-permute-start) | collective-permute-done | bytes 106528 | tf_op jit(solution)/shard_map/ppermute | solution.py:368
  9.9 0.0 copy-done
  9.9 0.0 copy-done.1
  9.9 0.0 copy-done.2
  9.9 0.0 copy-done.3
  9.9 0.0 copy-done.4
  9.9 0.0 copy-done.5
  9.9 2.7 %edge_rows.1 = (f32[5,88,128]{2,1,0:T(8,128)S(1)}, f32[5,88,128]{2,1,0:T(8,128)S(1)}, f32[5,96,128]{2,1,0:T(8,128)S(1)}, f32[5,96,128]{2,1,0:T(8,128)S(1)}, f32[...) custom-call(s32[4]{0:T(128)S(1)} %pad_add_fusion.flags, f32[96,512]{1,0:T(8,128)S(1)} %copy-done, ...), custom_call_target="tpu_custom_call" | custom-call | tf_op jit(solution)/shard_map/edge_rows/pallas_call | solution.py:403
  12.7 0.1 collective-permute-start.1
  12.8 0.7 %collective-permute-start.2 = (f32[5,88,128]{2,1,0:T(8,128)S(1)}, f32[5,88,128]{2,1,0:T(8,128)S(1)}, u32[]{:S(2)}, u32[]{:S(2)}) collective-permute-start(f32[5,88,128]{2,1,0:T(8,128)S(1)} %get-tuple-element.23), channel_id=1, source_target_pairs={{2,4},{4,2},{6,8},{8,6},{10,12},{12,10},{14,16},{16,14},{18,20},{2... | collective-permute-start | bytes 675848 | tf_op jit(solution)/shard_map/ppermute | solution.py:368
  13.5 0.8 %collective-permute-done.1.msg_in = f32[5,88,128]{2,1,0:T(8,128)S(1)} collective-permute-done((f32[5,88,128]{2,1,0:T(8,128)S(1)}, f32[5,88,128]{2,1,0:T(8,128)S(1)}, u32[]{:S(2)}, u32[]{:S(2)}) %collective-permute-start.1) | collective-permute-done | bytes 225312 | tf_op jit(solution)/shard_map/ppermute | solution.py:368
  14.2 0.0 collective-permute-done.2.msg_out
  14.2 7.3 %basis.1 = (f32[32,8,128]{2,1,0:T(8,128)S(1)}, f32[5,96,128]{2,1,0:T(8,128)S(1)}, f32[5,96,128]{2,1,0:T(8,128)S(1)}, f32[5,96,128]{2,1,0:T(8,128)S(1)}, f32[5,96...) custom-call(s32[4]{0:T(128)S(1)} %pad_add_fusion.flags, ...), custom_call_target="tpu_custom_call" | custom-call | tf_op jit(solution)/shard_map/basis/pallas_call | solution.py:419
  21.5 21.9 %all_to_all.5.mom = f32[32,8,128]{2,1,0:T(8,128)S(1)} all-to-all(f32[32,8,128]{2,1,0:T(8,128)S(1)} %get-tuple-element.24), channel_id=1, replica_groups=mesh['row'=16,'col'=2] {'row','col'}, dimensions={0} | all-to-all | bytes 262144 | tf_op jit(solution)/shard_map/all_to_all | solution.py:428
  43.4 1.0 %combine.1 = (f32[96,512]{1,0:T(8,128)}, f32[96,512]{1,0:T(8,128)}) custom-call(f32[32,8,128]{2,1,0:T(8,128)S(1)} %all_to_all.5.mom, f32[5,96,128]{2,1,0:T(8,128)S(1)} %get-tuple-element.25.p0, f32[5,96,128]{2,1,0:T(8,128)S(1)} %get-tuple-element.26.p1, f32[5,96,128]{2,1,0:T(8,128)S(1)} %get-tuple-element.27.p2, f32[5,96,128]{2,1,0:T(8,128)S(1)} %get-tuple-element.28.q0, ...), custom_call_target="tpu_custom_call" | custom-call | tf_op jit(solution)/shard_map/combine/pallas_call | solution.py:431
  (1 shorter events, 0.0 us)
Async XLA Ops:
  1.2 8.7 %copy-start = (f32[96,512]{1,0:T(8,128)S(1)}, f32[96,512]{1,0:T(8,128)}, u32[]{:S(2)}) copy-start(f32[96,512]{1,0:T(8,128)} %gx.3) | copy-start | bytes 589828
  1.2 8.7 %copy-start.1 = (f32[96,512]{1,0:T(8,128)S(1)}, f32[96,512]{1,0:T(8,128)}, u32[]{:S(2)}) copy-start(f32[96,512]{1,0:T(8,128)} %gy.3) | copy-start | bytes 589828
  1.2 8.7 %copy-start.2 = (f32[96,512]{1,0:T(8,128)S(1)}, f32[96,512]{1,0:T(8,128)}, u32[]{:S(2)}) copy-start(f32[96,512]{1,0:T(8,128)} %wx.3) | copy-start | bytes 589828
  1.2 8.7 %copy-start.3 = (f32[96,512]{1,0:T(8,128)S(1)}, f32[96,512]{1,0:T(8,128)}, u32[]{:S(2)}) copy-start(f32[96,512]{1,0:T(8,128)} %wy.3) | copy-start | bytes 589828
  1.2 8.7 %copy-start.4 = (f32[96,512]{1,0:T(8,128)S(1)}, f32[96,512]{1,0:T(8,128)}, u32[]{:S(2)}) copy-start(f32[96,512]{1,0:T(8,128)} %an.3) | copy-start | bytes 589828
  1.3 8.7 %copy-start.5 = (f32[96,512]{1,0:T(8,128)S(1)}, f32[96,512]{1,0:T(8,128)}, u32[]{:S(2)}) copy-start(f32[96,512]{1,0:T(8,128)} %pr.3) | copy-start | bytes 589828
  3.8 6.1 %collective-permute-start = (f32[104,256]{1,0:T(8,128)}, f32[104,256]{1,0:T(8,128)S(1)}, u32[]{:S(2)}, u32[]{:S(2)}) collective-permute-start(f32[104,256]{1,0:T(8,128)} %edge_columns.1), channel_id=1, source_target_pairs={{0,1},{1,0},{2,3},{3,2},{4,5},{5,4},{6,7},{7,6},{8,9},{9,8},{10,11... | collective-permute-start | bytes 319496 | tf_op jit(solution)/shard_map/ppermute | solution.py:368
  12.7 1.5 %collective-permute-start.1 = (f32[5,88,128]{2,1,0:T(8,128)S(1)}, f32[5,88,128]{2,1,0:T(8,128)S(1)}, u32[]{:S(2)}, u32[]{:S(2)}) collective-permute-start(f32[5,88,128]{2,1,0:T(8,128)S(1)} %get-tuple-element.22), channel_id=1, source_target_pairs={{0,2},{2,0},{4,6},{6,4},{8,10},{10,8},{12,14},{14,12},{16,18},{18,... | collective-permute-start | bytes 675848 | tf_op jit(solution)/shard_map/ppermute | solution.py:368
  12.8 1.5 %collective-permute-start.2 = (f32[5,88,128]{2,1,0:T(8,128)S(1)}, f32[5,88,128]{2,1,0:T(8,128)S(1)}, u32[]{:S(2)}, u32[]{:S(2)}) collective-permute-start(f32[5,88,128]{2,1,0:T(8,128)S(1)} %get-tuple-element.23), channel_id=1, source_target_pairs={{2,4},{4,2},{6,8},{8,6},{10,12},{12,10},{14,16},{16,14},{18,20},{2... | collective-permute-start | bytes 675848 | tf_op jit(solution)/shard_map/ppermute | solution.py:368

commit v2 on v1

v2 whole, which is shorter than its diff:
```python
import functools

import jax
import jax.numpy as jnp
from jax import lax
from jax.experimental import pallas as pl
from jax.experimental.pallas import tpu as pltpu
from jax.sharding import PartitionSpec as P

DAMP = 2.0 / 3.0
SHIFT = 1.0
HC = 64
HR = 20
FG = 24
GUARD = 8
VMEM = pl.BlockSpec(memory_space=pltpu.VMEM)
HBM = pl.BlockSpec(memory_space=pltpu.HBM)
F32 = jnp.float32


def lanes(shape):
    return lax.broadcasted_iota(jnp.int32, shape, 1)


def rows(shape):
    return lax.broadcasted_iota(jnp.int32, shape, 0)


def left_of(x, k=1):
    return pltpu.roll(x, k, 1)


def right_of(x, k=1):
    return pltpu.roll(x, x.shape[1] - k, 1)


def group_sum(x):
    lane = lanes(x.shape)
    x = x + jnp.where(lane % 2 == 0, right_of(x), left_of(x))
    return x + jnp.where(lane % 4 < 2, right_of(x, 2), left_of(x, 2))


def ld(ref, start, count=8, step=1):
    rows_of = pl.ds(start, count, stride=step) if step > 1 else slice(start, start + count)
    return jnp.concatenate([ref[j, rows_of, :] for j in range(ref.shape[0])], axis=1)


def st(ref, start, value, step=1):
    count = value.shape[0]
    rows_of = pl.ds(start, count, stride=step) if step > 1 else slice(start, start + count)
    for j in range(ref.shape[0]):
        ref[j, rows_of, :] = value[:, j * 128 : (j + 1) * 128]


def tree(parts):
    while len(parts) > 1:
        parts = [sum(parts[j + 1 : j + 2], parts[j]) for j in range(0, len(parts), 2)]
    return parts[0]


def four_rows(ref, start, count):
    parts = [ld(ref, start + k, count, 4) for k in range(4)]
    return (parts[0] + parts[1]) + (parts[2] + parts[3])


def position():
    row, col = lax.axis_index("row"), lax.axis_index("col")
    end_row = row == lax.axis_size("row") - 1
    end_col = col == lax.axis_size("col") - 1
    return lax.rem(row, 2) == 1, lax.rem(col, 2) == 1, end_row, end_col


def fetch(sources, targets, sems):
    copies = [pltpu.make_async_copy(x, y, sems.at[k]) for k, (x, y) in enumerate(zip(sources, targets))]
    for copy in copies:
        copy.start()
    for copy in copies:
        copy.wait()


def edge_columns(inner, *refs):
    fields, (out, *held, sems) = refs[:6], refs[6:]
    n, width = fields[0].shape
    _, col_odd, end_row, _ = position()
    last = jnp.logical_not(col_odd) if inner else col_odd
    offset = pl.multiple_of(jnp.where(last, width - 128, 0), 128)
    row, lane = rows((8, 128)), lanes((8, 128))
    zero = F32(0.0)
    fetch([f.at[:, pl.ds(offset, 128)] for f in fields], held, sems)

    def pair(x, y):
        low = jnp.where(lane < HC, x, left_of(y, HC))
        high = jnp.where(lane < HC, left_of(x, HC), y)
        return jnp.where(last, high, low)

    carry = jnp.zeros((1, 128), F32)
    for r in range(0, n, 8):
        g_x, g_y, w_x, w_y, a, p = [f[r : r + 8, :] for f in held]
        if r == n - 8:
            w_y = jnp.where((row == 7) & end_row, zero, w_y)
        fx = w_x * g_x
        fy = w_y * g_y
        before_x = jnp.where(lane == 0, zero, left_of(fx))
        before_y = jnp.where(row == 0, jnp.broadcast_to(carry, fy.shape), pltpu.roll(fy, 1, 0))
        carry = fy[7:8, :]
        src = a * p + before_x - fx + before_y - fy
        edge = jnp.broadcast_to(fx[:, 127:128], fx.shape)
        out[r : r + 8, 0:128] = jnp.where((lane == 0) & last, edge, pair(src, w_x))
        out[r : r + 8, 128:256] = pair(w_y, a)
    tail = jnp.broadcast_to(carry, (8, 128))
    tail = pair(tail, tail)
    out[n : n + 8, 0:128] = tail
    out[n : n + 8, 128:256] = tail


def tile_fields(*refs):
    fields, (r_o, wx_o, wy_o, an_o, fx_o, fy_o, *held, sems) = refs[:6], refs[6:]
    gx, gy, wx, wy, an, pr = held
    n, width = gx.shape
    fetch(fields, held, sems)
    _, _, end_row, end_col = position()
    row, lane = rows((8, width)), lanes((8, width))
    zero = F32(0.0)
    carry = jnp.zeros((1, width), F32)
    for r in range(0, n, 8):
        w_x = jnp.where((lane == width - 1) & end_col, zero, wx[r : r + 8, :])
        w_y = wy[r : r + 8, :]
        if r == n - 8:
            w_y = jnp.where((row == 7) & end_row, zero, w_y)
        fx = w_x * gx[r : r + 8, :]
        fy = w_y * gy[r : r + 8, :]
        a = an[r : r + 8, :]
        before_x = jnp.where(lane == 0, zero, left_of(fx))
        before_y = jnp.where(row == 0, jnp.broadcast_to(carry, fy.shape), pltpu.roll(fy, 1, 0))
        carry = fy[7:8, :]
        st(r_o, r, a * pr[r : r + 8, :] + before_x - fx + before_y - fy)
        st(wx_o, r, w_x)
        st(wy_o, r, w_y)
        st(an_o, r, a)
        fx_o[r : r + 8, :] = jnp.broadcast_to(fx[:, width - 1 : width], (8, 128))
    st(fy_o, 0, jnp.broadcast_to(carry, (8, width)))


def edge_rows(has_outer, r_t, wx_t, wy_t, an_t, fx_t, fy_t, *refs):
    inner, refs = refs[0], refs[1:]
    outer = None
    if has_outer:
        outer, refs = refs[0], refs[1:]
    msg_in, msg_out, r_o, wx_o, wy_o, an_o, fy_o, g_o, cr_o, cd_o, ca_o, u_s, t_s, tops = refs
    own, n, _ = r_t.shape
    ext = (own + 1) * 128
    row_odd, odd, _, _ = position()
    lane = lanes((8, 128))
    zero = F32(0.0)

    def halo(r, c):
        x = inner[r : r + 8, c : c + 128]
        y = outer[r : r + 8, c : c + 128] if has_outer else jnp.zeros_like(x)
        before, after = jnp.where(odd, x, y), jnp.where(odd, y, x)
        first = jnp.where(lane < HC, after, left_of(before, HC))
        second = jnp.where(lane < HC, left_of(after, HC), before)
        return first, second

    for r in range(0, n, 8):
        src_h, wx_h = halo(r, 0)
        wy_h, an_h = halo(r, 128)
        incoming = jnp.broadcast_to(src_h[:, HC : HC + 1], (8, 128))
        src_h = jnp.where(lane == 0, src_h + fx_t[r : r + 8, :], jnp.where(lane == HC, zero, src_h))
        for out, tile, h in ((r_o, r_t, src_h), (wx_o, wx_t, wx_h), (wy_o, wy_t, wy_h), (an_o, an_t, an_h)):
            for j in range(own):
                x = tile[j, r : r + 8, :]
                if out is r_o and j == 0:
                    x = jnp.where(lane == 0, x + incoming, x)
                out[j, r : r + 8, :] = x
            out[own, r : r + 8, :] = h
    for j in range(own):
        fy_o[j] = fy_t[j]
    fy_o[own] = halo(n, 0)[0]

    lo, hi = 16, n - 32
    for base in (lo, hi):
        for r in range(base - 8, base + 24, 8):
            w_x, w_y = ld(wx_o, r), ld(wy_o, r)
            diag = ld(an_o, r) + w_x + left_of(w_x) + w_y + ld(wy_o, r - 1)
            st(u_s, r, jnp.where(diag > zero, ld(r_o, r) / diag, zero))
        for r in range(base, base + 16, 8):
            st(t_s, r, apply_a(u_s, wx_o, wy_o, an_o, r))
    four = lanes((4, ext)) % 4
    packed_s = []
    for base in (lo, hi):
        s = group_sum(four_rows(t_s, base, 4))
        keep = jnp.where(four == rows((4, ext)), s, zero)
        packed_s.append((keep[0:1] + keep[1:2]) + (keep[2:3] + keep[3:4]))
    packed = []
    four = lanes((8, ext)) % 4
    for k, c in enumerate(range(lo, n - lo, 32)):
        c_r = group_sum(jnp.where(four == 3, four_rows(wx_o, c, 8), zero))
        c_d = group_sum(ld(wy_o, c + 3, 8, 4))
        c_a = group_sum(four_rows(an_o, c, 8))
        g = group_sum(four_rows(r_o, c, 8))
        packed.append(jnp.where(four < 2, jnp.where(four == 0, g, c_r), jnp.where(four == 2, c_d, c_a)))
        for out, x in ((g_o, g), (cr_o, c_r), (cd_o, c_d), (ca_o, c_a)):
            st(out, 8 * k, x)

    top, bottom = tops.at[0], tops.at[1]
    for k, ref in enumerate((r_o, wx_o, wy_o, an_o)):
        top[:, k * HR : (k + 1) * HR, :] = ref[:, 0:HR, :]
        bottom[:, k * HR : (k + 1) * HR, :] = ref[:, n - HR : n, :]
    st(top, HR - 1, packed_s[0])
    st(bottom, 0, packed_s[1])
    st(bottom, HR, ld(cd_o, cd_o.shape[1] - 9, 1))
    st(bottom, 3 * HR, ld(fy_o, 0, 1))
    st(top, 4 * HR, packed[0])
    st(bottom, 4 * HR, packed[-1])

    @pl.when(row_odd)
    def _():
        msg_in[...] = top[...]
        msg_out[...] = bottom[...]

    @pl.when(jnp.logical_not(row_odd))
    def _():
        msg_in[...] = bottom[...]
        msg_out[...] = top[...]


def inverse_diagonal(wx, wy, an, di):
    for r in range(8, wx.shape[1], 8):
        w_x, w_y = ld(wx, r), ld(wy, r)
        diag = ld(an, r) + w_x + left_of(w_x) + w_y + ld(wy, r - 1)
        st(di, r, jnp.where(diag > F32(0.0), F32(1.0) / diag, F32(0.0)))


def apply_a(v, w_x, w_y, an, r):
    x = ld(v, r)
    flow = ld(w_x, r) * (x - right_of(x))
    down = ld(w_y, r) * (x - ld(v, r + 1))
    up = ld(w_y, r - 1) * (x - ld(v, r - 1))
    return (ld(an, r) * x + (flow - left_of(flow))) + (down + up)


def basis(r_i, wx_i, wy_i, an_i, fy_i, g_i, cr_i, cd_i, ca_i, di_i, msg_in, msg_out, mom, p0, p1, p2, q0, q1, q2, r0,
         R, WX, WY, AN, DI, SP, PA, PB, QA, C_L, C_R, C_D, C_A, C_I, EA, EB, GC):
    blocks, n, _ = r_i.shape
    ext = blocks * 128
    fine = n + 2 * FG
    coarse = fine // 4 + 12
    zero = F32(0.0)
    odd, _, _, _ = position()
    own_blocks = blocks - 1
    B = GUARD

    def sides(a, b):
        x, y = ld(msg_in, a, b - a), ld(msg_out, a, b - a)
        return jnp.where(odd, x, y), jnp.where(odd, y, x)

    zeros = jnp.zeros((B, ext), F32)
    for ref in (R, WX, WY, AN, PA, PB):
        st(ref, 0, zeros)
        st(ref, B + fine, zeros)
    for k, (ref, own) in enumerate(((R, r_i), (WX, wx_i), (WY, wy_i), (AN, an_i))):
        up, down = sides(k * HR, (k + 1) * HR)
        st(ref, B, zeros[: FG - HR])
        st(ref, B + FG + n + HR, zeros[: FG - HR])
        st(ref, B + FG - HR, up)
        st(ref, B + FG + n, down)
        for r in range(0, n, 8):
            st(ref, B + FG + r, ld(own, r))
    flux_up, _ = sides(3 * HR, 3 * HR + 1)
    st(R, B + FG, ld(R, B + FG, 1) + flux_up)
    st(R, B + FG + n, ld(R, B + FG + n, 1) + ld(fy_i, 0, 1))

    for r in range(8, n, 8):
        st(DI, B + FG + r, ld(di_i, r))
    for r in [*range(B, B + FG + 8, 8), *range(B + FG + n, B + fine, 8)]:
        w_x, w_y = ld(WX, r), ld(WY, r)
        diag = ld(AN, r) + w_x + left_of(w_x) + w_y + ld(WY, r - 1)
        st(DI, r, jnp.where(diag > zero, F32(1.0) / diag, zero))

    for ref in (EA, EB, C_D):
        st(ref, 0, zeros)
        st(ref, B + coarse, zeros)
    up, down = sides(4 * HR, 4 * HR + 8)
    four = lanes((8, ext)) % 4
    for k, ref in enumerate((GC, C_R, C_D, C_A)):
        st(ref, B, group_sum(jnp.where(four == k, up, zero)))
        st(ref, B + coarse - 8, group_sum(jnp.where(four == k, down, zero)))
    beyond, _ = sides(HR, HR + 1)
    st(C_D, B - 1, beyond)
    for ref, own in ((GC, g_i), (C_R, cr_i), (C_D, cd_i), (C_A, ca_i)):
        for r in range(0, own.shape[1], 8):
            st(ref, B + 16 + r, ld(own, r))
    for c in (8, coarse - 16):
        f = B + 4 * c - 24
        st(GC, B + c, group_sum(four_rows(R, f, 8)))
        st(C_R, B + c, group_sum(jnp.where(four == 3, four_rows(WX, f, 8), zero)))
        st(C_D, B + c, group_sum(ld(WY, f + 3, 8, 4)))
        st(C_A, B + c, group_sum(four_rows(AN, f, 8)))
    for c in range(B, B + coarse, 8):
        c_r = ld(C_R, c)
        c_l = left_of(c_r, 4)
        total = ld(C_A, c) + c_l + c_r + ld(C_D, c - 1) + ld(C_D, c)
        st(C_L, c, c_l)
        st(C_I, c, jnp.where(total > zero, F32(DAMP) / total, zero))

    def smooth(lo, hi):
        for c in range(lo, hi, 8):
            st(EA, B + c, ld(C_I, B + c) * ld(GC, B + c))
        if lo > 0:
            st(EA, B + lo - 8, zeros)
            st(EB, B + lo - 8, zeros)
        if hi < coarse:
            st(EA, B + hi, zeros)
            st(EB, B + hi, zeros)
        old, new = EA, EB
        for turn in range(3):
            for c in range(B + lo, B + hi, 8):
                e = ld(old, c)
                beside = ld(C_L, c) * left_of(e, 4) + ld(C_R, c) * right_of(e, 4)
                beside = beside + (ld(C_D, c - 1) * ld(old, c - 1) + ld(C_D, c) * ld(old, c + 1))
                st(new, c, F32(1.0 - DAMP) * e + ld(C_I, c) * (ld(GC, c) + beside))
            old, new = new, old
        first, last = max(lo, 6), min(hi, coarse - 6)
        count = last - first
        for k in range(4):
            st(SP, B + 4 * (first - 6) + k, ld(EB, B + first, count), 4)

    def restrict(q):
        for c in range(8, coarse - 8, 8):
            st(GC, B + c, group_sum(four_rows(q, B + 4 * c - 24, 8)))

    smooth(0, coarse)
    for r in range(B, B + fine, 8):
        st(PA, r, ld(DI, r) * ld(R, r) + ld(SP, r))
    for r in range(B, B + fine, 8):
        st(QA, r, apply_a(PA, WX, WY, AN, r))
    restrict(QA)
    s_up, _ = sides(0, 1)
    _, s_down = sides(HR - 1, HR)
    for c, s, off in ((0, s_up, 4), (coarse - 8, s_down, 0)):
        part = jnp.where(four == rows((8, ext)) - off, jnp.broadcast_to(s, (8, ext)), zero)
        c = B + c
        e = ld(EB, c)
        image = ld(C_A, c) * e + ld(C_L, c) * (e - left_of(e, 4)) + ld(C_R, c) * (e - right_of(e, 4))
        image = image + ld(C_D, c - 1) * (e - ld(EB, c - 1))
        image = image + ld(C_D, c) * (e - ld(EB, c + 1))
        st(GC, c, group_sum(part) + image)
    for r in range(0, n, 8):
        f = B + FG + r
        for out, ref in ((p0, PA), (q0, QA), (r0, R)):
            out[:, r : r + 8, :] = ref[:own_blocks, f : f + 8, :]
    smooth(0, coarse)
    for r in range(B, B + fine, 8):
        st(PB, r, (ld(DI, r) * ld(QA, r) + ld(SP, r)) - F32(SHIFT) * ld(PA, r))
    for r in range(B + 8, B + fine - 8, 8):
        st(QA, r, apply_a(PB, WX, WY, AN, r))
    restrict(QA)
    for r in range(0, n, 8):
        f = B + FG + r
        for out, ref in ((p1, PB), (q1, QA)):
            out[:, r : r + 8, :] = ref[:own_blocks, f : f + 8, :]
    smooth(8, coarse - 8)
    for r in range(B + FG - 8, B + FG + n + 8, 8):
        st(PA, r, (ld(DI, r) * ld(QA, r) + ld(SP, r)) - F32(SHIFT) * ld(PB, r))
    acc = [jnp.zeros((8, 128), F32) for _ in range(9)]
    for r in range(0, n, 8):
        f = B + FG + r
        image = apply_a(PA, WX, WY, AN, f)
        sums = [[] for _ in acc]
        for j in range(own_blocks):
            z2, i2 = PA[j, f : f + 8, :], image[:, j * 128 : (j + 1) * 128]
            p2[j, r : r + 8, :] = z2
            q2[j, r : r + 8, :] = i2
            z0, z1, i0, i1, res = [x[j, r : r + 8, :] for x in (p0, p1, q0, q1, r0)]
            pairs = ((z0, i0), (z1, i0), (z1, i1), (z2, i0), (z2, i1), (z2, i2), (z0, res), (z1, res), (z2, res))
            for k, (x, y) in enumerate(pairs):
                sums[k].append(x * y)
        for k, parts in enumerate(sums):
            acc[k] = acc[k] + tree(parts)
    lane = lanes((8, 128))
    line = jnp.zeros((8, 128), F32)
    for k in range(9):
        total = jnp.sum(jnp.sum(acc[k], axis=0, keepdims=True), axis=1, keepdims=True)
        line = jnp.where(lane == k, jnp.broadcast_to(total, (8, 128)), line)
    for j in range(mom.shape[0]):
        mom[j] = line


def combine(mom, p0, p1, p2, q0, q1, q2, r0, heights, residual):
    blocks, n, _ = p0.shape
    tot = tree([mom[j] for j in range(mom.shape[0])])
    m = [jnp.broadcast_to(tot[:, k : k + 1], (8, 128)) for k in range(9)]
    g00, g10, g11, g20, g21, g22, b0, b1, b2 = m
    l10, l20 = g10 / g00, g20 / g00
    d1 = g11 - l10 * g10
    t21 = g21 - l20 * g10
    l21 = t21 / d1
    d2 = g22 - l20 * g20 - l21 * t21
    y1 = b1 - l10 * b0
    y2 = b2 - l20 * b0 - l21 * y1
    x2 = y2 / d2
    x1 = y1 / d1 - l21 * x2
    x0 = b0 / g00 - l10 * x1 - l20 * x2
    for r in range(0, n, 8):
        for j in range(blocks):
            at = (slice(r, r + 8), slice(j * 128, (j + 1) * 128))
            z0, z1, z2, i0, i1, i2, res = [x[j, r : r + 8, :] for x in (p0, p1, p2, q0, q1, q2, r0)]
            heights[at] = x0 * z0 + x1 * z1 + x2 * z2
            residual[at] = res - (x0 * i0 + x1 * i1 + x2 * i2)


def swap(x, axis, size, inner):
    if inner:
        pairs = [(i, i ^ 1) for i in range(size) if i ^ 1 < size]
    else:
        pairs = [(i, j) for i in range(size) for j in [((i + 1) ^ 1) - 1] if 0 <= j < size]
    return lax.ppermute(x, axis, pairs)


def local(nrow, ncol, gx, gy, wx, wy, an, pr):
    n, width = gx.shape
    ext = width + 2 * HC
    fields = tuple(pltpu.with_memory_space_constraint(f, pltpu.HBM) for f in (gx, gy, wx, wy, an, pr))
    nb = ext // 128
    shape = lambda *dims: jax.ShapeDtypeStruct(dims, F32)
    params = pltpu.CompilerParams(vmem_limit_bytes=48 * 1024 * 1024)

    def call(kernel, name, args, outs, scratch=(), us=1, fetches=0):
        sems = [pltpu.SemaphoreType.DMA((fetches,))] if fetches else []
        return pl.pallas_call(
            kernel,
            in_specs=[HBM if fetches else VMEM] * len(args),
            out_specs=[VMEM] * len(outs),
            out_shape=outs,
            scratch_shapes=[pltpu.VMEM(dims, F32) for dims in scratch] + sems,
            compiler_params=params,
            cost_estimate=pl.CostEstimate(flops=us * 2_000_000, bytes_accessed=us * 2_000_000, transcendentals=0),
            name=name,
        )(*args)

    halos = []
    for inner in (True, False) if ncol > 2 else (True,):
        (edge,) = call(functools.partial(edge_columns, inner), "edge_columns", fields, [shape(n + 8, 256)], [(n, 128)] * 6, 1, 6)
        halos.append(swap(edge, "col", ncol, inner))
    tile = shape(nb - 1, n, 128)
    own = call(tile_fields, "tile_fields", fields, [tile] * 4 + [shape(n, 128), shape(nb - 1, 8, 128)], [(n, width)] * 6, 1, 6)
    depth = 4 * HR + 8
    lo = 16
    far = shape(nb, (n - 2 * lo) // 4, 128)
    msg = shape(nb, depth, 128)
    field = shape(nb, n, 128)
    to_in, to_out, r_e, wx_e, wy_e, an_e, *rest = call(
        functools.partial(edge_rows, len(halos) > 1),
        "edge_rows",
        (*own, *halos),
        [msg, msg] + [field] * 4 + [shape(nb, 8, 128)] + [far] * 4,
        [(nb, n, 128), (nb, n, 128), (2, nb, depth, 128)],
    )
    from_out = swap(to_out, "row", nrow, False)
    from_in = swap(to_in, "row", nrow, True)
    (di,) = call(inverse_diagonal, "inverse_diagonal", (wx_e, wy_e, an_e), [field])
    fine = n + 2 * FG
    coarse = fine // 4 + 12
    mom, *vectors = call(
        basis,
        "basis",
        (r_e, wx_e, wy_e, an_e, *rest, di, from_in, from_out),
        [shape(nrow * ncol, 8, 128)] + [tile] * 7,
        [(nb, fine + 2 * GUARD, 128)] * 9 + [(nb, coarse + 2 * GUARD, 128)] * 8,
    )
    mom = lax.all_to_all(mom, ("row", "col"), 0, 0, tiled=True)
    out = shape(n, width)
    return tuple(call(combine, "combine", (mom, *vectors), [out, out]))


def solution(mesh):
    spec = P("row", "col")
    return jax.shard_map(
        functools.partial(local, mesh.shape["row"], mesh.shape["col"]),
        mesh=mesh,
        in_specs=(spec,) * 6,
        out_specs=(spec, spec),
        check_vma=False,
    )
```

time: 44.6 us -> 39.1 us (0.88)
  Pallas kernels: 13.5 us -> 10.5 us
  waiting for transfers between devices: 3.89 us -> 2.08 us
  other arithmetic: 0.66 us -> 0 us
    pallas_call x4 -> x6, Pallas kernels: 13.5 us -> 10.5 us  [call(): pl.pallas_call(kernel, in_specs=[HBM if fetches else VMEM] * len(args), o...]
    ppermute x3, waiting for transfers between devices: 3.89 us -> 2.08 us  [swap(): return lax.ppermute(x, axis, pairs)]
    another operation x2 -> x0, other arithmetic: 0.66 us -> none  [the longest x1 0.59 us: edge_columns(): edge = jnp.stack([jnp.int32(last), jnp.int32(row == nrow - 1)])]
  transfers between devices with their start and end apart: 3 -> 3, of which waited for: 2 -> 2; matrix products, arithmetic and copies ran while one was open for 0% -> 0% of each run, Pallas kernels for 0% -> 4%
where the time goes in v2:
time: 39.1 us; the launch traced here: 38.9 us
  blocking collectives  21.9 us (56%)
  Pallas kernels  10.5 us (27%)
  starting transfers between devices  3.75 us (10%)
  waiting for transfers between devices  2.08 us (5%)
  between operations  0.69 us (2%)
    all_to_all x1, blocking collectives, local(): mom = lax.all_to_all(mom, ('row', 'col'), 0, 0, tiled=True)  21.9 us
    pallas_call x6, Pallas kernels, call(): pl.pallas_call(kernel, in_specs=[HBM if fetches else VMEM] * len(args), o...  10.5 us
    ppermute x3, starting transfers between devices, swap(): return lax.ppermute(x, axis, pairs)  3.75 us
    ppermute x3, waiting for transfers between devices, swap(): return lax.ppermute(x, axis, pairs)  2.08 us
  transfers between devices with their start and end apart: 3, of which 2 were waited for; matrix products, arithmetic and copies ran while one was open for 0% of the time, Pallas kernels for 4%

profile of v2, /device:TPU:0, one launch (start us, length us, event | category | flops | bytes accessed | tf_op | source)
XLA Modules:
  0.0 38.9 jit_solution(6521319104119695903)
XLA Ops:
  0.6 1.2 %edge_columns.1 = f32[104,256]{1,0:T(8,128)S(1)} custom-call(f32[96,512]{1,0:T(8,128)} %refs_0_.3, f32[96,512]{1,0:T(8,128)} %refs_1_.3, f32[96,512]{1,0:T(8,128)} %refs_2_.3, f32[96,512]{1,0:T(8,128)} %refs_3_.3, f32[96,512]{1,0:T(8,128)} %refs_4_.3, f32[96,512]{1,0:T(8,128)} %refs_5_.3), custom_call_target="tpu_custom_call" | custom-call | flops 2000000 | bytes 2000000 | tf_op jit(solution)/shard_map/edge_columns/pallas_call | solution.py:430
  1.8 3.0 %collective-permute-start = (f32[104,256]{1,0:T(8,128)S(1)}, f32[104,256]{1,0:T(8,128)S(1)}, u32[]{:S(2)}, u32[]{:S(2)}) collective-permute-start(f32[104,256]{1,0:T(8,128)S(1)} %edge_columns.1), channel_id=1, source_target_pairs={{0,1},{1,0},{2,3},{3,2},{4,5},{5,4},{6,7},{7,6},{8,9},{9,8},{10,11... | collective-permute-start | bytes 319496 | tf_op jit(solution)/shard_map/ppermute | solution.py:417
  4.8 1.5 %tile_fields.1 = (f32[4,96,128]{2,1,0:T(8,128)S(1)}, f32[4,96,128]{2,1,0:T(8,128)S(1)}, f32[4,96,128]{2,1,0:T(8,128)S(1)}, f32[4,96,128]{2,1,0:T(8,128)S(1)}, f3...) custom-call(f32[96,512]{1,0:T(8,128)} %refs_0_.3, f32[96,512]{1,0:T(8,128)} %refs_1_.3, f32[96,512]{1,0:T(8,128)} %refs_2_.3, ...), custom_call_target="tpu_custom_call" | custom-call | flops 2000000 | bytes 2000000 | tf_op jit(solution)/shard_map/tile_fields/pallas_call | solution.py:430
  6.3 1.4 %collective-permute-done.refs_0_ = f32[104,256]{1,0:T(8,128)S(1)} collective-permute-done((f32[104,256]{1,0:T(8,128)S(1)}, f32[104,256]{1,0:T(8,128)S(1)}, u32[]{:S(2)}, u32[]{:S(2)}) %collective-permute-start) | collective-permute-done | bytes 106528 | tf_op jit(solution)/shard_map/ppermute | solution.py:417
  7.8 1.0 %edge_rows.1 = (f32[5,88,128]{2,1,0:T(8,128)S(1)}, f32[5,88,128]{2,1,0:T(8,128)S(1)}, f32[5,96,128]{2,1,0:T(8,128)S(1)}, f32[5,96,128]{2,1,0:T(8,128)S(1)}, f32[...) custom-call(f32[4,96,128]{2,1,0:T(8,128)S(1)} %get-tuple-element.27., ...), custom_call_target="tpu_custom_call" | custom-call | flops 2000000 | bytes 2000000 | tf_op jit(solution)/shard_map/edge_rows/pallas_call | solution.py:430
  8.8 0.1 collective-permute-start.1
  8.8 0.7 %collective-permute-start.2 = (f32[5,88,128]{2,1,0:T(8,128)S(1)}, f32[5,88,128]{2,1,0:T(8,128)S(1)}, u32[]{:S(2)}, u32[]{:S(2)}) collective-permute-start(f32[5,88,128]{2,1,0:T(8,128)S(1)} %get-tuple-element.43), channel_id=1, source_target_pairs={{2,4},{4,2},{6,8},{8,6},{10,12},{12,10},{14,16},{16,14},{18,20},{2... | collective-permute-start | bytes 675848 | tf_op jit(solution)/shard_map/ppermute | solution.py:417
  9.5 0.1 inverse_diagonal.1.di_i
  9.7 0.6 %collective-permute-done.1.msg_in = f32[5,88,128]{2,1,0:T(8,128)S(1)} collective-permute-done((f32[5,88,128]{2,1,0:T(8,128)S(1)}, f32[5,88,128]{2,1,0:T(8,128)S(1)}, u32[]{:S(2)}, u32[]{:S(2)}) %collective-permute-start.1) | collective-permute-done | bytes 225312 | tf_op jit(solution)/shard_map/ppermute | solution.py:417
  10.3 0.0 collective-permute-done.2.msg_out
  10.3 5.8 %basis.1 = (f32[32,8,128]{2,1,0:T(8,128)S(1)}, f32[4,96,128]{2,1,0:T(8,128)S(1)}, f32[4,96,128]{2,1,0:T(8,128)S(1)}, f32[4,96,128]{2,1,0:T(8,128)S(1)}, f32[4,96...) custom-call(f32[5,96,128]{2,1,0:T(8,128)S(1)} %get-tuple-element.33.r_i, ...), custom_call_target="tpu_custom_call" | custom-call | flops 2000000 | bytes 2000000 | tf_op jit(solution)/shard_map/basis/pallas_call | solution.py:430
  16.1 21.9 %all_to_all.5.mom = f32[32,8,128]{2,1,0:T(8,128)S(1)} all-to-all(f32[32,8,128]{2,1,0:T(8,128)S(1)} %get-tuple-element.44), channel_id=1, replica_groups=mesh['row'=16,'col'=2] {'row','col'}, dimensions={0} | all-to-all | bytes 262144 | tf_op jit(solution)/shard_map/all_to_all | solution.py:471
  38.0 0.9 %combine.1 = (f32[96,512]{1,0:T(8,128)}, f32[96,512]{1,0:T(8,128)}) custom-call(f32[32,8,128]{2,1,0:T(8,128)S(1)} %all_to_all.5.mom, f32[4,96,128]{2,1,0:T(8,128)S(1)} %get-tuple-element.45.p0, f32[4,96,128]{2,1,0:T(8,128)S(1)} %get-tuple-element.46.p1, f32[4,96,128]{2,1,0:T(8,128)S(1)} %get-tuple-element.47.p2, f32[4,96,128]{2,1,0:T(8,128)S(1)} %get-tuple-element.48.q0, ...), custom_call_target="tpu_custom_call" | custom-call | flops 2000000 | bytes 2000000 | tf_op jit(solution)/shard_map/combine/pallas_call | solution.py:430
Async XLA Ops:
  1.8 6.0 %collective-permute-start = (f32[104,256]{1,0:T(8,128)S(1)}, f32[104,256]{1,0:T(8,128)S(1)}, u32[]{:S(2)}, u32[]{:S(2)}) collective-permute-start(f32[104,256]{1,0:T(8,128)S(1)} %edge_columns.1), channel_id=1, source_target_pairs={{0,1},{1,0},{2,3},{3,2},{4,5},{5,4},{6,7},{7,6},{8,9},{9,8},{10,11... | collective-permute-start | bytes 319496 | tf_op jit(solution)/shard_map/ppermute | solution.py:417
  8.8 1.5 %collective-permute-start.1 = (f32[5,88,128]{2,1,0:T(8,128)S(1)}, f32[5,88,128]{2,1,0:T(8,128)S(1)}, u32[]{:S(2)}, u32[]{:S(2)}) collective-permute-start(f32[5,88,128]{2,1,0:T(8,128)S(1)} %get-tuple-element.42), channel_id=1, source_target_pairs={{0,2},{2,0},{4,6},{6,4},{8,10},{10,8},{12,14},{14,12},{16,18},{18,... | collective-permute-start | bytes 675848 | tf_op jit(solution)/shard_map/ppermute | solution.py:417
  8.8 1.5 %collective-permute-start.2 = (f32[5,88,128]{2,1,0:T(8,128)S(1)}, f32[5,88,128]{2,1,0:T(8,128)S(1)}, u32[]{:S(2)}, u32[]{:S(2)}) collective-permute-start(f32[5,88,128]{2,1,0:T(8,128)S(1)} %get-tuple-element.43), channel_id=1, source_target_pairs={{2,4},{4,2},{6,8},{8,6},{10,12},{12,10},{14,16},{16,14},{18,20},{2... | collective-permute-start | bytes 675848 | tf_op jit(solution)/shard_map/ppermute | solution.py:417

commit v3 on v2

--- a/solution.py
+++ b/solution.py
@@ -26,18 +26,148 @@
     return lax.broadcasted_iota(jnp.int32, shape, 0)
 
 
-def left_of(x, k=1):
+def roll_right(x, k=1):
     return pltpu.roll(x, k, 1)
 
 
-def right_of(x, k=1):
+def roll_left(x, k=1):
     return pltpu.roll(x, x.shape[1] - k, 1)
 
 
 def group_sum(x):
     lane = lanes(x.shape)
-    x = x + jnp.where(lane % 2 == 0, right_of(x), left_of(x))
-    return x + jnp.where(lane % 4 < 2, right_of(x, 2), left_of(x, 2))
+    x = x + jnp.where(lane % 2 == 0, roll_left(x), roll_right(x))
+    return x + jnp.where(lane % 4 < 2, roll_left(x, 2), roll_right(x, 2))
+
+
+def split(x):
+    return [x[:, j : j + 128] for j in range(0, x.shape[1], 128)]
+
+
+def join(parts):
+    return jnp.concatenate(parts, axis=1)
+
+
+class Wide:
+    def __init__(self, width):
+        self.coarse_blocks = width // 128 + 1
+
+    left, right = staticmethod(roll_right), staticmethod(roll_left)
+    total = staticmethod(group_sum)
+    spread = take = staticmethod(lambda x: x)
+    steps_in = steps_out = ()
+
+    def coarse_left(self, e):
+        return roll_right(e, 4)
+
+    def coarse_right(self, e):
+        return roll_left(e, 4)
+
+    def last_column(self, x):
+        return group_sum(jnp.where(lanes(x.shape) % 4 == 3, x, F32(0.0)))
+
+    def pack(self, a, b, c, d):
+        four = lanes(a.shape) % 4
+        return jnp.where(four < 2, jnp.where(four == 0, a, b), jnp.where(four == 2, c, d))
+
+    def unpack(self, m, k):
+        return group_sum(jnp.where(lanes(m.shape) % 4 == k, m, F32(0.0)))
+
+
+class Planes:
+    coarse_blocks = 2
+
+    def left(self, x):
+        a, b, c, d, h = split(x)
+        first = lanes(h.shape) == 0
+        d, h = roll_right(d), roll_right(h)
+        return join([jnp.where(first, h, d), a, b, c, jnp.where(first, d, h)])
+
+    def right(self, x):
+        a, b, c, d, h = split(x)
+        last = lanes(h.shape) == 127
+        a, h = roll_left(a), roll_left(h)
+        return join([b, c, d, jnp.where(last, h, a), jnp.where(last, a, h)])
+
+    def coarse_left(self, e):
+        o, h = split(e)
+        lane = lanes(h.shape)
+        end = jnp.broadcast_to(o[:, 127:128], h.shape)
+        return join([jnp.where(lane == 0, roll_right(h), roll_right(o)), jnp.where(lane < 4, end, roll_right(h, 4))])
+
+    def coarse_right(self, e):
+        o, h = split(e)
+        lane = lanes(h.shape)
+        end = jnp.broadcast_to(o[:, 0:1], h.shape)
+        return join([jnp.where(lane == 127, roll_left(h), roll_left(o)), jnp.where(lane >= 124, end, roll_left(h, 4))])
+
+    def total(self, x):
+        a, b, c, d, h = split(x)
+        return join([(a + b) + (c + d), group_sum(h)])
+
+    def last_column(self, x):
+        h = x[:, 512:640]
+        return join([x[:, 384:512], group_sum(jnp.where(lanes(h.shape) % 4 == 3, h, F32(0.0)))])
+
+    def spread(self, e):
+        o, h = split(e)
+        return join([o, o, o, o, h])
+
+    def take(self, x):
+        return join([x[:, 0:128], x[:, 512:640]])
+
+    def pack(self, *fields):
+        own, halo = zip(*[split(f) for f in fields])
+        a, b, c, d = halo
+        four = lanes(a.shape) % 4
+        mixed = jnp.where(four < 2, jnp.where(four == 0, a, b), jnp.where(four == 2, c, d))
+        return join([*own, mixed])
+
+    def unpack(self, m, k):
+        h = m[:, 512:640]
+        return join([m[:, k * 128 : k * 128 + 128], group_sum(jnp.where(lanes(h.shape) % 4 == k, h, F32(0.0)))])
+
+    def gather_in(self, parts):
+        lane = lanes(parts[0].shape)
+        index = (lane % 32) * 4 + lane // 32
+        return [jnp.take_along_axis(p, index, axis=1) for p in parts]
+
+    def gather_out(self, parts):
+        lane = lanes(parts[0].shape)
+        index = (lane % 4) * 32 + lane // 4
+        return [jnp.take_along_axis(p, index, axis=1) for p in parts]
+
+    def swap_halves(self, parts):
+        a, b, c, d = parts
+        low = lanes(a.shape) < 64
+        return [
+            jnp.where(low, a, roll_right(c, 64)),
+            jnp.where(low, b, roll_right(d, 64)),
+            jnp.where(low, roll_right(a, 64), c),
+            jnp.where(low, roll_right(b, 64), d),
+        ]
+
+    def swap_quarters(self, parts):
+        a, b, c, d = parts
+        low = lanes(a.shape) % 64 < 32
+        return [
+            jnp.where(low, a, roll_right(b, 32)),
+            jnp.where(low, roll_left(a, 32), b),
+            jnp.where(low, c, roll_right(d, 32)),
+            jnp.where(low, roll_left(c, 32), d),
+        ]
+
+    @property
+    def steps_in(self):
+        return self.gather_in, self.swap_halves, self.swap_quarters
+
+    @property
+    def steps_out(self):
+        return self.swap_halves, self.swap_quarters, self.gather_out
+
+
+def layout(blocks):
+    return Planes() if blocks == 5 else Wide(128 * (blocks - 1))
 
 
 def ld(ref, start, count=8, step=1):
@@ -68,6 +198,20 @@
     end_row = row == lax.axis_size("row") - 1
     end_col = col == lax.axis_size("col") - 1
     return lax.rem(row, 2) == 1, lax.rem(col, 2) == 1, end_row, end_col
+
+
+def reorder(steps, sources, targets, spare):
+    pairs = list(zip(sources, spare))
+    for k, step in enumerate(steps):
+        for (x, y), target in zip(pairs, targets):
+            x, y = (y, x) if k % 2 else (x, y)
+            y = target if k == len(steps) - 1 else y
+            for r in range(0, x.shape[1], 8):
+                for j, block in enumerate(step([x[j, r : r + 8, :] for j in range(x.shape[0])])):
+                    y[j, r : r + 8, :] = block
+    if not steps:
+        for x, target in zip(sources, targets):
+            target[...] = x[...]
 
 
 def fetch(sources, targets, sems):
@@ -89,8 +233,8 @@
     fetch([f.at[:, pl.ds(offset, 128)] for f in fields], held, sems)
 
     def pair(x, y):
-        low = jnp.where(lane < HC, x, left_of(y, HC))
-        high = jnp.where(lane < HC, left_of(x, HC), y)
+        low = jnp.where(lane < HC, x, roll_right(y, HC))
+        high = jnp.where(lane < HC, roll_right(x, HC), y)
         return jnp.where(last, high, low)
 
     carry = jnp.zeros((1, 128), F32)
@@ -100,7 +244,7 @@
             w_y = jnp.where((row == 7) & end_row, zero, w_y)
         fx = w_x * g_x
         fy = w_y * g_y
-        before_x = jnp.where(lane == 0, zero, left_of(fx))
+        before_x = jnp.where(lane == 0, zero, roll_right(fx))
         before_y = jnp.where(row == 0, jnp.broadcast_to(carry, fy.shape), pltpu.roll(fy, 1, 0))
         carry = fy[7:8, :]
         src = a * p + before_x - fx + before_y - fy
@@ -114,9 +258,10 @@
 
 
 def tile_fields(*refs):
-    fields, (r_o, wx_o, wy_o, an_o, fx_o, fy_o, *held, sems) = refs[:6], refs[6:]
+    fields, (r_o, wx_o, wy_o, an_o, fx_o, fy_o, *held, raw, spare, tail, sems) = refs[:6], refs[6:]
     gx, gy, wx, wy, an, pr = held
     n, width = gx.shape
+    form = layout(width // 128 + 1)
     fetch(fields, held, sems)
     _, _, end_row, end_col = position()
     row, lane = rows((8, width)), lanes((8, width))
@@ -130,15 +275,16 @@
         fx = w_x * gx[r : r + 8, :]
         fy = w_y * gy[r : r + 8, :]
         a = an[r : r + 8, :]
-        before_x = jnp.where(lane == 0, zero, left_of(fx))
+        before_x = jnp.where(lane == 0, zero, roll_right(fx))
         before_y = jnp.where(row == 0, jnp.broadcast_to(carry, fy.shape), pltpu.roll(fy, 1, 0))
         carry = fy[7:8, :]
-        st(r_o, r, a * pr[r : r + 8, :] + before_x - fx + before_y - fy)
-        st(wx_o, r, w_x)
-        st(wy_o, r, w_y)
-        st(an_o, r, a)
+        src = a * pr[r : r + 8, :] + before_x - fx + before_y - fy
+        for k, x in enumerate((src, w_x, w_y, a)):
+            st(raw.at[k], r, x)
         fx_o[r : r + 8, :] = jnp.broadcast_to(fx[:, width - 1 : width], (8, 128))
-    st(fy_o, 0, jnp.broadcast_to(carry, (8, width)))
+    st(tail.at[0], 0, jnp.broadcast_to(carry, (8, width)))
+    pick = lambda ref: [ref.at[k] for k in range(4)]
+    reorder(form.steps_in, [*pick(raw), tail.at[0]], [r_o, wx_o, wy_o, an_o, fy_o], [*pick(spare), tail.at[1]])
 
 
 def edge_rows(has_outer, r_t, wx_t, wy_t, an_t, fx_t, fy_t, *refs):
@@ -146,9 +292,9 @@
     outer = None
     if has_outer:
         outer, refs = refs[0], refs[1:]
-    msg_in, msg_out, r_o, wx_o, wy_o, an_o, fy_o, g_o, cr_o, cd_o, ca_o, u_s, t_s, tops = refs
+    msg_in, msg_out, r_o, wx_o, wy_o, an_o, fy_o, g_o, cr_o, cd_o, ca_o, u_s, t_s, f_s, tops = refs
     own, n, _ = r_t.shape
-    ext = (own + 1) * 128
+    form = layout(own + 1)
     row_odd, odd, _, _ = position()
     lane = lanes((8, 128))
     zero = F32(0.0)
@@ -157,8 +303,8 @@
         x = inner[r : r + 8, c : c + 128]
         y = outer[r : r + 8, c : c + 128] if has_outer else jnp.zeros_like(x)
         before, after = jnp.where(odd, x, y), jnp.where(odd, y, x)
-        first = jnp.where(lane < HC, after, left_of(before, HC))
-        second = jnp.where(lane < HC, left_of(after, HC), before)
+        first = jnp.where(lane < HC, after, roll_right(before, HC))
+        second = jnp.where(lane < HC, roll_right(after, HC), before)
         return first, second
 
     for r in range(0, n, 8):
@@ -181,24 +327,24 @@
     for base in (lo, hi):
         for r in range(base - 8, base + 24, 8):
             w_x, w_y = ld(wx_o, r), ld(wy_o, r)
-            diag = ld(an_o, r) + w_x + left_of(w_x) + w_y + ld(wy_o, r - 1)
+            diag = ld(an_o, r) + w_x + form.left(w_x) + w_y + ld(wy_o, r - 1)
             st(u_s, r, jnp.where(diag > zero, ld(r_o, r) / diag, zero))
+    for base in (lo, hi):
+        flows(form, u_s, wx_o, f_s, range(base, base + 16, 8))
+    for base in (lo, hi):
         for r in range(base, base + 16, 8):
-            st(t_s, r, apply_a(u_s, wx_o, wy_o, an_o, r))
-    four = lanes((4, ext)) % 4
+            st(t_s, r, apply_a(u_s, form.left, f_s, wy_o, an_o, r))
     packed_s = []
     for base in (lo, hi):
-        s = group_sum(four_rows(t_s, base, 4))
-        keep = jnp.where(four == rows((4, ext)), s, zero)
-        packed_s.append((keep[0:1] + keep[1:2]) + (keep[2:3] + keep[3:4]))
+        sums = form.total(four_rows(t_s, base, 4))
+        packed_s.append(form.pack(*[sums[k : k + 1] for k in range(4)]))
     packed = []
-    four = lanes((8, ext)) % 4
     for k, c in enumerate(range(lo, n - lo, 32)):
-        c_r = group_sum(jnp.where(four == 3, four_rows(wx_o, c, 8), zero))
-        c_d = group_sum(ld(wy_o, c + 3, 8, 4))
-        c_a = group_sum(four_rows(an_o, c, 8))
-        g = group_sum(four_rows(r_o, c, 8))
-        packed.append(jnp.where(four < 2, jnp.where(four == 0, g, c_r), jnp.where(four == 2, c_d, c_a)))
+        c_r = form.last_column(four_rows(wx_o, c, 8))
+        c_d = form.total(ld(wy_o, c + 3, 8, 4))
+        c_a = form.total(four_rows(an_o, c, 8))
+        g = form.total(four_rows(r_o, c, 8))
+        packed.append(form.pack(g, c_r, c_d, c_a))
         for out, x in ((g_o, g), (cr_o, c_r), (cd_o, c_d), (ca_o, c_a)):
             st(out, 8 * k, x)
 
@@ -208,7 +354,7 @@
         bottom[:, k * HR : (k + 1) * HR, :] = ref[:, n - HR : n, :]
     st(top, HR - 1, packed_s[0])
     st(bottom, 0, packed_s[1])
-    st(bottom, HR, ld(cd_o, cd_o.shape[1] - 9, 1))
+    st(bottom, HR, form.spread(ld(cd_o, cd_o.shape[1] - 9, 1)))
     st(bottom, 3 * HR, ld(fy_o, 0, 1))
     st(top, 4 * HR, packed[0])
     st(bottom, 4 * HR, packed[-1])
@@ -225,24 +371,30 @@
 
 
 def inverse_diagonal(wx, wy, an, di):
+    form = layout(wx.shape[0])
     for r in range(8, wx.shape[1], 8):
         w_x, w_y = ld(wx, r), ld(wy, r)
-        diag = ld(an, r) + w_x + left_of(w_x) + w_y + ld(wy, r - 1)
+        diag = ld(an, r) + w_x + form.left(w_x) + w_y + ld(wy, r - 1)
         st(di, r, jnp.where(diag > F32(0.0), F32(1.0) / diag, F32(0.0)))
 
 
-def apply_a(v, w_x, w_y, an, r):
+def flows(form, v, w_x, flow, starts):
+    for r in starts:
+        x = ld(v, r)
+        st(flow, r, ld(w_x, r) * (x - form.right(x)))
+
+
+def apply_a(v, flow_left, flow, w_y, an, r):
     x = ld(v, r)
-    flow = ld(w_x, r) * (x - right_of(x))
     down = ld(w_y, r) * (x - ld(v, r + 1))
     up = ld(w_y, r - 1) * (x - ld(v, r - 1))
-    return (ld(an, r) * x + (flow - left_of(flow))) + (down + up)
+    return (ld(an, r) * x + (ld(flow, r) - flow_left(ld(flow, r)))) + (down + up)
 
 
 def basis(r_i, wx_i, wy_i, an_i, fy_i, g_i, cr_i, cd_i, ca_i, di_i, msg_in, msg_out, mom, p0, p1, p2, q0, q1, q2, r0,
-         R, WX, WY, AN, DI, SP, PA, PB, QA, C_L, C_R, C_D, C_A, C_I, EA, EB, GC):
+         R, WX, WY, AN, DI, SP, PA, PB, QA, FL, C_L, C_R, C_D, C_A, C_I, EA, EB, GC):
     blocks, n, _ = r_i.shape
-    ext = blocks * 128
+    form = layout(blocks)
     fine = n + 2 * FG
     coarse = fine // 4 + 12
     zero = F32(0.0)
@@ -254,7 +406,8 @@
         x, y = ld(msg_in, a, b - a), ld(msg_out, a, b - a)
         return jnp.where(odd, x, y), jnp.where(odd, y, x)
 
-    zeros = jnp.zeros((B, ext), F32)
+    zeros = jnp.zeros((B, blocks * 128), F32)
+    coarse_zeros = jnp.zeros((B, form.coarse_blocks * 128), F32)
     for ref in (R, WX, WY, AN, PA, PB):
         st(ref, 0, zeros)
         st(ref, B + fine, zeros)
@@ -274,31 +427,30 @@
         st(DI, B + FG + r, ld(di_i, r))
     for r in [*range(B, B + FG + 8, 8), *range(B + FG + n, B + fine, 8)]:
         w_x, w_y = ld(WX, r), ld(WY, r)
-        diag = ld(AN, r) + w_x + left_of(w_x) + w_y + ld(WY, r - 1)
+        diag = ld(AN, r) + w_x + form.left(w_x) + w_y + ld(WY, r - 1)
         st(DI, r, jnp.where(diag > zero, F32(1.0) / diag, zero))
 
     for ref in (EA, EB, C_D):
-        st(ref, 0, zeros)
-        st(ref, B + coarse, zeros)
+        st(ref, 0, coarse_zeros)
+        st(ref, B + coarse, coarse_zeros)
     up, down = sides(4 * HR, 4 * HR + 8)
-    four = lanes((8, ext)) % 4
     for k, ref in enumerate((GC, C_R, C_D, C_A)):
-        st(ref, B, group_sum(jnp.where(four == k, up, zero)))
-        st(ref, B + coarse - 8, group_sum(jnp.where(four == k, down, zero)))
+        st(ref, B, form.unpack(up, k))
+        st(ref, B + coarse - 8, form.unpack(down, k))
     beyond, _ = sides(HR, HR + 1)
-    st(C_D, B - 1, beyond)
+    st(C_D, B - 1, form.take(beyond))
     for ref, own in ((GC, g_i), (C_R, cr_i), (C_D, cd_i), (C_A, ca_i)):
         for r in range(0, own.shape[1], 8):
             st(ref, B + 16 + r, ld(own, r))
     for c in (8, coarse - 16):
         f = B + 4 * c - 24
-        st(GC, B + c, group_sum(four_rows(R, f, 8)))
-        st(C_R, B + c, group_sum(jnp.where(four == 3, four_rows(WX, f, 8), zero)))
-        st(C_D, B + c, group_sum(ld(WY, f + 3, 8, 4)))
-        st(C_A, B + c, group_sum(four_rows(AN, f, 8)))
+        st(GC, B + c, form.total(four_rows(R, f, 8)))
+        st(C_R, B + c, form.last_column(four_rows(WX, f, 8)))
+        st(C_D, B + c, form.total(ld(WY, f + 3, 8, 4)))
+        st(C_A, B + c, form.total(four_rows(AN, f, 8)))
     for c in range(B, B + coarse, 8):
         c_r = ld(C_R, c)
-        c_l = left_of(c_r, 4)
+        c_l = form.coarse_left(c_r)
         total = ld(C_A, c) + c_l + c_r + ld(C_D, c - 1) + ld(C_D, c)
         st(C_L, c, c_l)
         st(C_I, c, jnp.where(total > zero, F32(DAMP) / total, zero))
@@ -307,44 +459,47 @@
         for c in range(lo, hi, 8):
             st(EA, B + c, ld(C_I, B + c) * ld(GC, B + c))
         if lo > 0:
-            st(EA, B + lo - 8, zeros)
-            st(EB, B + lo - 8, zeros)
+            st(EA, B + lo - 8, coarse_zeros)
+            st(EB, B + lo - 8, coarse_zeros)
         if hi < coarse:
-            st(EA, B + hi, zeros)
-            st(EB, B + hi, zeros)
+            st(EA, B + hi, coarse_zeros)
+            st(EB, B + hi, coarse_zeros)
         old, new = EA, EB
         for turn in range(3):
             for c in range(B + lo, B + hi, 8):
                 e = ld(old, c)
-                beside = ld(C_L, c) * left_of(e, 4) + ld(C_R, c) * right_of(e, 4)
+                beside = ld(C_L, c) * form.coarse_left(e) + ld(C_R, c) * form.coarse_right(e)
                 beside = beside + (ld(C_D, c - 1) * ld(old, c - 1) + ld(C_D, c) * ld(old, c + 1))
                 st(new, c, F32(1.0 - DAMP) * e + ld(C_I, c) * (ld(GC, c) + beside))
             old, new = new, old
         first, last = max(lo, 6), min(hi, coarse - 6)
         count = last - first
         for k in range(4):
-            st(SP, B + 4 * (first - 6) + k, ld(EB, B + first, count), 4)
+            st(SP, B + 4 * (first - 6) + k, form.spread(ld(EB, B + first, count)), 4)
 
     def restrict(q):
         for c in range(8, coarse - 8, 8):
-            st(GC, B + c, group_sum(four_rows(q, B + 4 * c - 24, 8)))
+            st(GC, B + c, form.total(four_rows(q, B + 4 * c - 24, 8)))
 
     smooth(0, coarse)
     for r in range(B, B + fine, 8):
         st(PA, r, ld(DI, r) * ld(R, r) + ld(SP, r))
+    flows(form, PA, WX, FL, range(B, B + fine, 8))
     for r in range(B, B + fine, 8):
-        st(QA, r, apply_a(PA, WX, WY, AN, r))
+        st(QA, r, apply_a(PA, form.left, FL, WY, AN, r))
     restrict(QA)
     s_up, _ = sides(0, 1)
     _, s_down = sides(HR - 1, HR)
     for c, s, off in ((0, s_up, 4), (coarse - 8, s_down, 0)):
-        part = jnp.where(four == rows((8, ext)) - off, jnp.broadcast_to(s, (8, ext)), zero)
         c = B + c
         e = ld(EB, c)
-        image = ld(C_A, c) * e + ld(C_L, c) * (e - left_of(e, 4)) + ld(C_R, c) * (e - right_of(e, 4))
+        part = jnp.zeros_like(e)
+        for k in range(4):
+            part = jnp.where(rows(e.shape) == off + k, jnp.broadcast_to(form.unpack(s, k), e.shape), part)
+        image = ld(C_A, c) * e + ld(C_L, c) * (e - form.coarse_left(e)) + ld(C_R, c) * (e - form.coarse_right(e))
         image = image + ld(C_D, c - 1) * (e - ld(EB, c - 1))
         image = image + ld(C_D, c) * (e - ld(EB, c + 1))
-        st(GC, c, group_sum(part) + image)
+        st(GC, c, part + image)
     for r in range(0, n, 8):
         f = B + FG + r
         for out, ref in ((p0, PA), (q0, QA), (r0, R)):
@@ -352,8 +507,9 @@
     smooth(0, coarse)
     for r in range(B, B + fine, 8):
         st(PB, r, (ld(DI, r) * ld(QA, r) + ld(SP, r)) - F32(SHIFT) * ld(PA, r))
+    flows(form, PB, WX, FL, range(B + 8, B + fine - 8, 8))
     for r in range(B + 8, B + fine - 8, 8):
-        st(QA, r, apply_a(PB, WX, WY, AN, r))
+        st(QA, r, apply_a(PB, form.left, FL, WY, AN, r))
     restrict(QA)
     for r in range(0, n, 8):
         f = B + FG + r
@@ -362,10 +518,11 @@
     smooth(8, coarse - 8)
     for r in range(B + FG - 8, B + FG + n + 8, 8):
         st(PA, r, (ld(DI, r) * ld(QA, r) + ld(SP, r)) - F32(SHIFT) * ld(PB, r))
+    flows(form, PA, WX, FL, range(B + FG, B + FG + n, 8))
     acc = [jnp.zeros((8, 128), F32) for _ in range(9)]
     for r in range(0, n, 8):
         f = B + FG + r
-        image = apply_a(PA, WX, WY, AN, f)
+        image = apply_a(PA, form.left, FL, WY, AN, f)
         sums = [[] for _ in acc]
         for j in range(own_blocks):
             z2, i2 = PA[j, f : f + 8, :], image[:, j * 128 : (j + 1) * 128]
@@ -386,8 +543,9 @@
         mom[j] = line
 
 
-def combine(mom, p0, p1, p2, q0, q1, q2, r0, heights, residual):
+def combine(mom, p0, p1, p2, q0, q1, q2, r0, heights, residual, work):
     blocks, n, _ = p0.shape
+    form = layout(blocks + 1)
     tot = tree([mom[j] for j in range(mom.shape[0])])
     m = [jnp.broadcast_to(tot[:, k : k + 1], (8, 128)) for k in range(9)]
     g00, g10, g11, g20, g21, g22, b0, b1, b2 = m
@@ -401,12 +559,16 @@
     x2 = y2 / d2
     x1 = y1 / d1 - l21 * x2
     x0 = b0 / g00 - l10 * x1 - l20 * x2
+    sums, spare, done = [[work.at[k], work.at[k + 1]] for k in (0, 2, 4)]
     for r in range(0, n, 8):
         for j in range(blocks):
-            at = (slice(r, r + 8), slice(j * 128, (j + 1) * 128))
             z0, z1, z2, i0, i1, i2, res = [x[j, r : r + 8, :] for x in (p0, p1, p2, q0, q1, q2, r0)]
-            heights[at] = x0 * z0 + x1 * z1 + x2 * z2
-            residual[at] = res - (x0 * i0 + x1 * i1 + x2 * i2)
+            sums[0][j, r : r + 8, :] = x0 * z0 + x1 * z1 + x2 * z2
+            sums[1][j, r : r + 8, :] = res - (x0 * i0 + x1 * i1 + x2 * i2)
+    reorder(form.steps_out, sums, done, spare)
+    for r in range(0, n, 8):
+        heights[r : r + 8, :] = ld(done[0], r)
+        residual[r : r + 8, :] = ld(done[1], r)
 
 
 def swap(x, axis, size, inner):
@@ -443,10 +605,11 @@
         (edge,) = call(functools.partial(edge_columns, inner), "edge_columns", fields, [shape(n + 8, 256)], [(n, 128)] * 6, 1, 6)
         halos.append(swap(edge, "col", ncol, inner))
     tile = shape(nb - 1, n, 128)
-    own = call(tile_fields, "tile_fields", fields, [tile] * 4 + [shape(n, 128), shape(nb - 1, 8, 128)], [(n, width)] * 6, 1, 6)
+    own = call(tile_fields, "tile_fields", fields, [tile] * 4 + [shape(n, 128), shape(nb - 1, 8, 128)], [(n, width)] * 6 + [(4, nb - 1, n, 128)] * 2 + [(2, nb - 1, 8, 128)], 1, 6)
     depth = 4 * HR + 8
     lo = 16
-    far = shape(nb, (n - 2 * lo) // 4, 128)
+    cb = layout(nb).coarse_blocks
+    far = shape(cb, (n - 2 * lo) // 4, 128)
     msg = shape(nb, depth, 128)
     field = shape(nb, n, 128)
     to_in, to_out, r_e, wx_e, wy_e, an_e, *rest = call(
@@ -454,7 +617,7 @@
         "edge_rows",
         (*own, *halos),
         [msg, msg] + [field] * 4 + [shape(nb, 8, 128)] + [far] * 4,
-        [(nb, n, 128), (nb, n, 128), (2, nb, depth, 128)],
+        [(nb, n, 128)] * 3 + [(2, nb, depth, 128)],
     )
     from_out = swap(to_out, "row", nrow, False)
     from_in = swap(to_in, "row", nrow, True)
@@ -466,11 +629,11 @@
         "basis",
         (r_e, wx_e, wy_e, an_e, *rest, di, from_in, from_out),
         [shape(nrow * ncol, 8, 128)] + [tile] * 7,
-        [(nb, fine + 2 * GUARD, 128)] * 9 + [(nb, coarse + 2 * GUARD, 128)] * 8,
+        [(nb, fine + 2 * GUARD, 128)] * 10 + [(cb, coarse + 2 * GUARD, 128)] * 8,
     )
     mom = lax.all_to_all(mom, ("row", "col"), 0, 0, tiled=True)
     out = shape(n, width)
-    return tuple(call(combine, "combine", (mom, *vectors), [out, out]))
+    return tuple(call(combine, "combine", (mom, *vectors), [out, out], [(6, nb - 1, n, 128)]))
 
 
 def solution(mesh):

time: 39.1 us -> 35.6 us (0.910)
  Pallas kernels: 10.5 us -> 7.6 us
  waiting for transfers between devices: 2.08 us -> 1.48 us
    pallas_call x6, Pallas kernels: 10.5 us -> 7.6 us  [call(): pl.pallas_call(kernel, in_specs=[HBM if fetches else VMEM] * len(args), o...]
    ppermute x3, waiting for transfers between devices: 2.08 us -> 1.48 us  [swap(): return lax.ppermute(x, axis, pairs)]
  transfers between devices with their start and end apart: 3 -> 3, of which waited for: 2 -> 2; matrix products, arithmetic and copies ran while one was open for 0% -> 0% of each run, Pallas kernels for 4% -> 6%
where the time goes in v3:
time: 35.6 us; the launch traced here: 35.4 us
  blocking collectives  21.9 us (62%)
  Pallas kernels  7.6 us (21%)
  starting transfers between devices  3.75 us (11%)
  waiting for transfers between devices  1.48 us (4%)
  between operations  0.69 us (2%)
    all_to_all x1, blocking collectives, local(): mom = lax.all_to_all(mom, ('row', 'col'), 0, 0, tiled=True)  21.9 us
    pallas_call x6, Pallas kernels, call(): pl.pallas_call(kernel, in_specs=[HBM if fetches else VMEM] * len(args), o...  7.6 us
    ppermute x3, starting transfers between devices, swap(): return lax.ppermute(x, axis, pairs)  3.75 us
    ppermute x3, waiting for transfers between devices, swap(): return lax.ppermute(x, axis, pairs)  1.48 us
  transfers between devices with their start and end apart: 3, of which 2 were waited for; matrix products, arithmetic and copies ran while one was open for 0% of the time, Pallas kernels for 6%

profile of v3, /device:TPU:0, one launch (start us, length us, event | category | flops | bytes accessed | tf_op | source)
XLA Modules:
  0.0 35.4 jit_solution(18432211377456482098)
XLA Ops:
  0.6 1.2 %edge_columns.1 = f32[104,256]{1,0:T(8,128)S(1)} custom-call(f32[96,512]{1,0:T(8,128)} %refs_0_.3, f32[96,512]{1,0:T(8,128)} %refs_1_.3, f32[96,512]{1,0:T(8,128)} %refs_2_.3, f32[96,512]{1,0:T(8,128)} %refs_3_.3, f32[96,512]{1,0:T(8,128)} %refs_4_.3, f32[96,512]{1,0:T(8,128)} %refs_5_.3), custom_call_target="tpu_custom_call" | custom-call | flops 2000000 | bytes 2000000 | tf_op jit(solution)/shard_map/edge_columns/pallas_call | solution.py:592
  1.8 3.0 %collective-permute-start = (f32[104,256]{1,0:T(8,128)S(1)}, f32[104,256]{1,0:T(8,128)S(1)}, u32[]{:S(2)}, u32[]{:S(2)}) collective-permute-start(f32[104,256]{1,0:T(8,128)S(1)} %edge_columns.1), channel_id=1, source_target_pairs={{0,1},{1,0},{2,3},{3,2},{4,5},{5,4},{6,7},{7,6},{8,9},{9,8},{10,11... | collective-permute-start | bytes 319496 | tf_op jit(solution)/shard_map/ppermute | solution.py:579
  4.8 2.2 %tile_fields.1 = (f32[4,96,128]{2,1,0:T(8,128)S(1)}, f32[4,96,128]{2,1,0:T(8,128)S(1)}, f32[4,96,128]{2,1,0:T(8,128)S(1)}, f32[4,96,128]{2,1,0:T(8,128)S(1)}, f3...) custom-call(f32[96,512]{1,0:T(8,128)} %refs_0_.3, f32[96,512]{1,0:T(8,128)} %refs_1_.3, f32[96,512]{1,0:T(8,128)} %refs_2_.3, ...), custom_call_target="tpu_custom_call" | custom-call | flops 2000000 | bytes 2000000 | tf_op jit(solution)/shard_map/tile_fields/pallas_call | solution.py:592
  7.0 0.8 %collective-permute-done.refs_0_ = f32[104,256]{1,0:T(8,128)S(1)} collective-permute-done((f32[104,256]{1,0:T(8,128)S(1)}, f32[104,256]{1,0:T(8,128)S(1)}, u32[]{:S(2)}, u32[]{:S(2)}) %collective-permute-start) | collective-permute-done | bytes 106528 | tf_op jit(solution)/shard_map/ppermute | solution.py:579
  7.8 0.5 %edge_rows.1 = (f32[5,88,128]{2,1,0:T(8,128)S(1)}, f32[5,88,128]{2,1,0:T(8,128)S(1)}, f32[5,96,128]{2,1,0:T(8,128)S(1)}, f32[5,96,128]{2,1,0:T(8,128)S(1)}, f32[...) custom-call(f32[4,96,128]{2,1,0:T(8,128)S(1)} %get-tuple-element.27., ...), custom_call_target="tpu_custom_call" | custom-call | flops 2000000 | bytes 2000000 | tf_op jit(solution)/shard_map/edge_rows/pallas_call | solution.py:592
  8.3 0.1 collective-permute-start.1
  8.4 0.7 %collective-permute-start.2 = (f32[5,88,128]{2,1,0:T(8,128)S(1)}, f32[5,88,128]{2,1,0:T(8,128)S(1)}, u32[]{:S(2)}, u32[]{:S(2)}) collective-permute-start(f32[5,88,128]{2,1,0:T(8,128)S(1)} %get-tuple-element.43), channel_id=1, source_target_pairs={{2,4},{4,2},{6,8},{8,6},{10,12},{12,10},{14,16},{16,14},{18,20},{2... | collective-permute-start | bytes 675848 | tf_op jit(solution)/shard_map/ppermute | solution.py:579
  9.1 0.1 inverse_diagonal.1.di_i
  9.2 0.7 %collective-permute-done.1.msg_in = f32[5,88,128]{2,1,0:T(8,128)S(1)} collective-permute-done((f32[5,88,128]{2,1,0:T(8,128)S(1)}, f32[5,88,128]{2,1,0:T(8,128)S(1)}, u32[]{:S(2)}, u32[]{:S(2)}) %collective-permute-start.1) | collective-permute-done | bytes 225312 | tf_op jit(solution)/shard_map/ppermute | solution.py:579
  9.9 0.0 collective-permute-done.2.msg_out
  9.9 2.5 %basis.1 = (f32[32,8,128]{2,1,0:T(8,128)S(1)}, f32[4,96,128]{2,1,0:T(8,128)S(1)}, f32[4,96,128]{2,1,0:T(8,128)S(1)}, f32[4,96,128]{2,1,0:T(8,128)S(1)}, f32[4,96...) custom-call(f32[5,96,128]{2,1,0:T(8,128)S(1)} %get-tuple-element.33.r_i, ...), custom_call_target="tpu_custom_call" | custom-call | flops 2000000 | bytes 2000000 | tf_op jit(solution)/shard_map/basis/pallas_call | solution.py:592
  12.3 21.9 %all_to_all.5.mom = f32[32,8,128]{2,1,0:T(8,128)S(1)} all-to-all(f32[32,8,128]{2,1,0:T(8,128)S(1)} %get-tuple-element.44), channel_id=1, replica_groups=mesh['row'=16,'col'=2] {'row','col'}, dimensions={0} | all-to-all | bytes 262144 | tf_op jit(solution)/shard_map/all_to_all | solution.py:634
  34.2 1.2 %combine.1 = (f32[96,512]{1,0:T(8,128)}, f32[96,512]{1,0:T(8,128)}) custom-call(f32[32,8,128]{2,1,0:T(8,128)S(1)} %all_to_all.5.mom, f32[4,96,128]{2,1,0:T(8,128)S(1)} %get-tuple-element.45.p0, f32[4,96,128]{2,1,0:T(8,128)S(1)} %get-tuple-element.46.p1, f32[4,96,128]{2,1,0:T(8,128)S(1)} %get-tuple-element.47.p2, f32[4,96,128]{2,1,0:T(8,128)S(1)} %get-tuple-element.48.q0, ...), custom_call_target="tpu_custom_call" | custom-call | flops 2000000 | bytes 2000000 | tf_op jit(solution)/shard_map/combine/pallas_call | solution.py:592
Async XLA Ops:
  1.8 6.0 %collective-permute-start = (f32[104,256]{1,0:T(8,128)S(1)}, f32[104,256]{1,0:T(8,128)S(1)}, u32[]{:S(2)}, u32[]{:S(2)}) collective-permute-start(f32[104,256]{1,0:T(8,128)S(1)} %edge_columns.1), channel_id=1, source_target_pairs={{0,1},{1,0},{2,3},{3,2},{4,5},{5,4},{6,7},{7,6},{8,9},{9,8},{10,11... | collective-permute-start | bytes 319496 | tf_op jit(solution)/shard_map/ppermute | solution.py:579
  8.3 1.5 %collective-permute-start.1 = (f32[5,88,128]{2,1,0:T(8,128)S(1)}, f32[5,88,128]{2,1,0:T(8,128)S(1)}, u32[]{:S(2)}, u32[]{:S(2)}) collective-permute-start(f32[5,88,128]{2,1,0:T(8,128)S(1)} %get-tuple-element.42), channel_id=1, source_target_pairs={{0,2},{2,0},{4,6},{6,4},{8,10},{10,8},{12,14},{14,12},{16,18},{18,... | collective-permute-start | bytes 675848 | tf_op jit(solution)/shard_map/ppermute | solution.py:579
  8.4 1.5 %collective-permute-start.2 = (f32[5,88,128]{2,1,0:T(8,128)S(1)}, f32[5,88,128]{2,1,0:T(8,128)S(1)}, u32[]{:S(2)}, u32[]{:S(2)}) collective-permute-start(f32[5,88,128]{2,1,0:T(8,128)S(1)} %get-tuple-element.43), channel_id=1, source_target_pairs={{2,4},{4,2},{6,8},{8,6},{10,12},{12,10},{14,16},{16,14},{18,20},{2... | collective-permute-start | bytes 675848 | tf_op jit(solution)/shard_map/ppermute | solution.py:579

commit v4 on v3

--- a/solution.py
+++ b/solution.py
@@ -171,13 +171,13 @@
 
 
 def ld(ref, start, count=8, step=1):
-    rows_of = pl.ds(start, count, stride=step) if step > 1 else slice(start, start + count)
+    rows_of = pl.ds(start, count, stride=step) if step > 1 else pl.ds(start, count)
     return jnp.concatenate([ref[j, rows_of, :] for j in range(ref.shape[0])], axis=1)
 
 
 def st(ref, start, value, step=1):
     count = value.shape[0]
-    rows_of = pl.ds(start, count, stride=step) if step > 1 else slice(start, start + count)
+    rows_of = pl.ds(start, count, stride=step) if step > 1 else pl.ds(start, count)
     for j in range(ref.shape[0]):
         ref[j, rows_of, :] = value[:, j * 128 : (j + 1) * 128]
 
@@ -292,7 +292,7 @@
     outer = None
     if has_outer:
         outer, refs = refs[0], refs[1:]
-    msg_in, msg_out, r_o, wx_o, wy_o, an_o, fy_o, g_o, cr_o, cd_o, ca_o, u_s, t_s, f_s, tops = refs
+    r_o, wx_o, wy_o, an_o, fy_o, *rest = refs
     own, n, _ = r_t.shape
     form = layout(own + 1)
     row_odd, odd, _, _ = position()
@@ -323,59 +323,60 @@
         fy_o[j] = fy_t[j]
     fy_o[own] = halo(n, 0)[0]
 
-    lo, hi = 16, n - 32
-    for base in (lo, hi):
-        for r in range(base - 8, base + 24, 8):
-            w_x, w_y = ld(wx_o, r), ld(wy_o, r)
-            diag = ld(an_o, r) + w_x + form.left(w_x) + w_y + ld(wy_o, r - 1)
-            st(u_s, r, jnp.where(diag > zero, ld(r_o, r) / diag, zero))
-    for base in (lo, hi):
-        flows(form, u_s, wx_o, f_s, range(base, base + 16, 8))
-    for base in (lo, hi):
-        for r in range(base, base + 16, 8):
-            st(t_s, r, apply_a(u_s, form.left, f_s, wy_o, an_o, r))
-    packed_s = []
-    for base in (lo, hi):
-        sums = form.total(four_rows(t_s, base, 4))
-        packed_s.append(form.pack(*[sums[k : k + 1] for k in range(4)]))
-    packed = []
-    for k, c in enumerate(range(lo, n - lo, 32)):
-        c_r = form.last_column(four_rows(wx_o, c, 8))
-        c_d = form.total(ld(wy_o, c + 3, 8, 4))
-        c_a = form.total(four_rows(an_o, c, 8))
-        g = form.total(four_rows(r_o, c, 8))
-        packed.append(form.pack(g, c_r, c_d, c_a))
-        for out, x in ((g_o, g), (cr_o, c_r), (cd_o, c_d), (ca_o, c_a)):
-            st(out, 8 * k, x)
-
-    top, bottom = tops.at[0], tops.at[1]
+    message(form, row_odd, r_o, wx_o, wy_o, an_o, fy_o, *rest)
+
+
+def near_rows(r_i, wx_i, wy_i, an_i, fy_i, di, *rest):
+    form = layout(wx_i.shape[0])
+    row_odd, _, _, _ = position()
+    message(form, jnp.logical_not(row_odd), r_i, wx_i, wy_i, an_i, fy_i, *rest)
+    for r in range(8, wx_i.shape[1], 8):
+        w_x, w_y = ld(wx_i, r), ld(wy_i, r)
+        diag = ld(an_i, r) + w_x + form.left(w_x) + w_y + ld(wy_i, r - 1)
+        st(di, r, jnp.where(diag > F32(0.0), F32(1.0) / diag, F32(0.0)))
+
+
+def message(form, bottom, r_o, wx_o, wy_o, an_o, fy_o, msg, g_o, cr_o, cd_o, ca_o, u_s, t_s, f_s):
+    n = r_o.shape[1]
+    zero = F32(0.0)
+
+    def pick(low, high):
+        return jnp.where(bottom, high, low)
+
+    base = pl.multiple_of(pick(16, n - 32), 8)
+    for r in range(0, 32, 8):
+        at = pl.multiple_of(base - 8 + r, 8)
+        w_x, w_y = ld(wx_o, at), ld(wy_o, at)
+        diag = ld(an_o, at) + w_x + form.left(w_x) + w_y + ld(wy_o, base - 9 + r)
+        st(u_s, 8 + r, jnp.where(diag > zero, ld(r_o, at) / diag, zero))
+    for r in (0, 8):
+        x = ld(u_s, 16 + r)
+        st(f_s, r, ld(wx_o, pl.multiple_of(base + r, 8)) * (x - form.right(x)))
+    for r in (0, 8):
+        at = pl.multiple_of(base + r, 8)
+        x, flow = ld(u_s, 16 + r), ld(f_s, r)
+        down = ld(wy_o, at) * (x - ld(u_s, 17 + r))
+        up = ld(wy_o, base + r - 1) * (x - ld(u_s, 15 + r))
+        st(t_s, r, (ld(an_o, at) * x + (flow - form.left(flow))) + (down + up))
+    sums = form.total(four_rows(t_s, 0, 4))
+    c = pl.multiple_of(pick(16, n - 48), 8)
+    coarse = (
+        form.total(four_rows(r_o, c, 8)),
+        form.last_column(four_rows(wx_o, c, 8)),
+        form.total(ld(wy_o, c + 3, 8, 4)),
+        form.total(four_rows(an_o, c, 8)),
+    )
+    for out, x in zip((g_o, cr_o, cd_o, ca_o), coarse):
+        st(out, 0, x)
+    start = pick(0, n - HR)
     for k, ref in enumerate((r_o, wx_o, wy_o, an_o)):
-        top[:, k * HR : (k + 1) * HR, :] = ref[:, 0:HR, :]
-        bottom[:, k * HR : (k + 1) * HR, :] = ref[:, n - HR : n, :]
-    st(top, HR - 1, packed_s[0])
-    st(bottom, 0, packed_s[1])
-    st(bottom, HR, form.spread(ld(cd_o, cd_o.shape[1] - 9, 1)))
-    st(bottom, 3 * HR, ld(fy_o, 0, 1))
-    st(top, 4 * HR, packed[0])
-    st(bottom, 4 * HR, packed[-1])
-
-    @pl.when(row_odd)
-    def _():
-        msg_in[...] = top[...]
-        msg_out[...] = bottom[...]
-
-    @pl.when(jnp.logical_not(row_odd))
-    def _():
-        msg_in[...] = bottom[...]
-        msg_out[...] = top[...]
-
-
-def inverse_diagonal(wx, wy, an, di):
-    form = layout(wx.shape[0])
-    for r in range(8, wx.shape[1], 8):
-        w_x, w_y = ld(wx, r), ld(wy, r)
-        diag = ld(an, r) + w_x + form.left(w_x) + w_y + ld(wy, r - 1)
-        st(di, r, jnp.where(diag > F32(0.0), F32(1.0) / diag, F32(0.0)))
+        for r in range(0, HR, 4):
+            st(msg, k * HR + r, ld(ref, start + r, 4))
+    outer = pick(HR - 1, 0)
+    st(msg, outer, form.pack(*[sums[k : k + 1] for k in range(4)]))
+    st(msg, HR + outer, form.spread(form.total(ld(wy_o, n - 49, 1))))
+    st(msg, 3 * HR + outer, ld(fy_o, 0, 1))
+    st(msg, 4 * HR, form.pack(*coarse))
 
 
 def flows(form, v, w_x, flow, starts):
@@ -391,7 +392,7 @@
     return (ld(an, r) * x + (ld(flow, r) - flow_left(ld(flow, r)))) + (down + up)
 
 
-def basis(r_i, wx_i, wy_i, an_i, fy_i, g_i, cr_i, cd_i, ca_i, di_i, msg_in, msg_out, mom, p0, p1, p2, q0, q1, q2, r0,
+def basis(r_i, wx_i, wy_i, an_i, fy_i, g_a, cr_a, cd_a, ca_a, di_i, g_b, cr_b, cd_b, ca_b, msg_in, msg_out, mom, p0, p1, p2, q0, q1, q2, r0,
          R, WX, WY, AN, DI, SP, PA, PB, QA, FL, C_L, C_R, C_D, C_A, C_I, EA, EB, GC):
     blocks, n, _ = r_i.shape
     form = layout(blocks)
@@ -439,9 +440,10 @@
         st(ref, B + coarse - 8, form.unpack(down, k))
     beyond, _ = sides(HR, HR + 1)
     st(C_D, B - 1, form.take(beyond))
-    for ref, own in ((GC, g_i), (C_R, cr_i), (C_D, cd_i), (C_A, ca_i)):
-        for r in range(0, own.shape[1], 8):
-            st(ref, B + 16 + r, ld(own, r))
+    for ref, a, b in ((GC, g_a, g_b), (C_R, cr_a, cr_b), (C_D, cd_a, cd_b), (C_A, ca_a, ca_b)):
+        x, y = ld(a, 0), ld(b, 0)
+        st(ref, B + 16, jnp.where(odd, y, x))
+        st(ref, B + 24, jnp.where(odd, x, y))
     for c in (8, coarse - 16):
         f = B + 4 * c - 24
         st(GC, B + c, form.total(four_rows(R, f, 8)))
@@ -540,13 +542,13 @@
         total = jnp.sum(jnp.sum(acc[k], axis=0, keepdims=True), axis=1, keepdims=True)
         line = jnp.where(lane == k, jnp.broadcast_to(total, (8, 128)), line)
     for j in range(mom.shape[0]):
-        mom[j] = line
+        mom[j] = line[0:1]
 
 
 def combine(mom, p0, p1, p2, q0, q1, q2, r0, heights, residual, work):
     blocks, n, _ = p0.shape
     form = layout(blocks + 1)
-    tot = tree([mom[j] for j in range(mom.shape[0])])
+    tot = jnp.broadcast_to(tree([mom[j] for j in range(mom.shape[0])]), (8, 128))
     m = [jnp.broadcast_to(tot[:, k : k + 1], (8, 128)) for k in range(9)]
     g00, g10, g11, g20, g21, g22, b0, b1, b2 = m
     l10, l20 = g10 / g00, g20 / g00
@@ -607,28 +609,28 @@
     tile = shape(nb - 1, n, 128)
     own = call(tile_fields, "tile_fields", fields, [tile] * 4 + [shape(n, 128), shape(nb - 1, 8, 128)], [(n, width)] * 6 + [(4, nb - 1, n, 128)] * 2 + [(2, nb - 1, 8, 128)], 1, 6)
     depth = 4 * HR + 8
-    lo = 16
     cb = layout(nb).coarse_blocks
-    far = shape(cb, (n - 2 * lo) // 4, 128)
+    far = shape(cb, 8, 128)
     msg = shape(nb, depth, 128)
     field = shape(nb, n, 128)
-    to_in, to_out, r_e, wx_e, wy_e, an_e, *rest = call(
+    work = [(nb, 48, 128), (nb, 16, 128), (nb, 16, 128)]
+    *fields, to_out, g_a, cr_a, cd_a, ca_a = call(
         functools.partial(edge_rows, len(halos) > 1),
         "edge_rows",
         (*own, *halos),
-        [msg, msg] + [field] * 4 + [shape(nb, 8, 128)] + [far] * 4,
-        [(nb, n, 128)] * 3 + [(2, nb, depth, 128)],
+        [field] * 4 + [shape(nb, 8, 128), msg] + [far] * 4,
+        work,
     )
     from_out = swap(to_out, "row", nrow, False)
+    di, to_in, *far_b = call(near_rows, "near_rows", fields, [field, msg] + [far] * 4, work)
     from_in = swap(to_in, "row", nrow, True)
-    (di,) = call(inverse_diagonal, "inverse_diagonal", (wx_e, wy_e, an_e), [field])
     fine = n + 2 * FG
     coarse = fine // 4 + 12
     mom, *vectors = call(
         basis,
         "basis",
-        (r_e, wx_e, wy_e, an_e, *rest, di, from_in, from_out),
-        [shape(nrow * ncol, 8, 128)] + [tile] * 7,
+        (*fields, g_a, cr_a, cd_a, ca_a, di, *far_b, from_in, from_out),
+        [shape(nrow * ncol, 1, 128)] + [tile] * 7,
         [(nb, fine + 2 * GUARD, 128)] * 10 + [(cb, coarse + 2 * GUARD, 128)] * 8,
     )
     mom = lax.all_to_all(mom, ("row", "col"), 0, 0, tiled=True)

time: 35.6 us -> 33.9 us (0.952)
  blocking collectives: 21.9 us -> 16.4 us
  starting transfers between devices: 3.75 us -> 6.83 us
  waiting for transfers between devices: 1.48 us -> 1.91 us
    all_to_all x1, blocking collectives: 21.9 us -> 16.4 us  [local(): mom = lax.all_to_all(mom, ('row', 'col'), 0, 0, tiled=True)]
    ppermute x3, starting transfers between devices: 3.75 us -> 6.83 us  [swap(): return lax.ppermute(x, axis, pairs)]
    ppermute x3, waiting for transfers between devices: 1.48 us -> 1.91 us  [swap(): return lax.ppermute(x, axis, pairs)]
  transfers between devices with their start and end apart: 3 -> 3, of which waited for: 2 -> 2; matrix products, arithmetic and copies ran while one was open for 0% -> 0% of each run, Pallas kernels for 6% -> 8%
where the time goes in v4:
time: 33.9 us; the launch traced here: 33.7 us
  blocking collectives  16.4 us (48%)
  Pallas kernels  7.83 us (23%)
  starting transfers between devices  6.83 us (20%)
  waiting for transfers between devices  1.91 us (6%)
  between operations  0.67 us (2%)
    all_to_all x1, blocking collectives, local(): mom = lax.all_to_all(mom, ('row', 'col'), 0, 0, tiled=True)  16.4 us
    pallas_call x6, Pallas kernels, call(): pl.pallas_call(kernel, in_specs=[HBM if fetches else VMEM] * len(args), o...  7.83 us
    ppermute x3, starting transfers between devices, swap(): return lax.ppermute(x, axis, pairs)  6.83 us
    ppermute x3, waiting for transfers between devices, swap(): return lax.ppermute(x, axis, pairs)  1.91 us
  transfers between devices with their start and end apart: 3, of which 2 were waited for; matrix products, arithmetic and copies ran while one was open for 0% of the time, Pallas kernels for 8%

profile of v4, /device:TPU:0, one launch (start us, length us, event | category | flops | bytes accessed | tf_op | source)
XLA Modules:
  0.0 33.7 jit_solution(16650482976847816709)
XLA Ops:
  0.6 1.2 %edge_columns.1 = f32[104,256]{1,0:T(8,128)S(1)} custom-call(f32[96,512]{1,0:T(8,128)} %refs_0_.3, f32[96,512]{1,0:T(8,128)} %refs_1_.3, f32[96,512]{1,0:T(8,128)} %refs_2_.3, f32[96,512]{1,0:T(8,128)} %refs_3_.3, f32[96,512]{1,0:T(8,128)} %refs_4_.3, f32[96,512]{1,0:T(8,128)} %refs_5_.3), custom_call_target="tpu_custom_call" | custom-call | flops 2000000 | bytes 2000000 | tf_op jit(solution)/shard_map/edge_columns/pallas_call | solution.py:594
  1.8 3.0 %collective-permute-start = (f32[104,256]{1,0:T(8,128)S(1)}, f32[104,256]{1,0:T(8,128)S(1)}, u32[]{:S(2)}, u32[]{:S(2)}) collective-permute-start(f32[104,256]{1,0:T(8,128)S(1)} %edge_columns.1), channel_id=1, source_target_pairs={{0,1},{1,0},{2,3},{3,2},{4,5},{5,4},{6,7},{7,6},{8,9},{9,8},{10,11... | collective-permute-start | bytes 319496 | tf_op jit(solution)/shard_map/ppermute | solution.py:581
  4.8 2.2 %tile_fields.1 = (f32[4,96,128]{2,1,0:T(8,128)S(1)}, f32[4,96,128]{2,1,0:T(8,128)S(1)}, f32[4,96,128]{2,1,0:T(8,128)S(1)}, f32[4,96,128]{2,1,0:T(8,128)S(1)}, f3...) custom-call(f32[96,512]{1,0:T(8,128)} %refs_0_.3, f32[96,512]{1,0:T(8,128)} %refs_1_.3, f32[96,512]{1,0:T(8,128)} %refs_2_.3, ...), custom_call_target="tpu_custom_call" | custom-call | flops 2000000 | bytes 2000000 | tf_op jit(solution)/shard_map/tile_fields/pallas_call | solution.py:594
  7.0 0.8 %collective-permute-done.refs_0_ = f32[104,256]{1,0:T(8,128)S(1)} collective-permute-done((f32[104,256]{1,0:T(8,128)S(1)}, f32[104,256]{1,0:T(8,128)S(1)}, u32[]{:S(2)}, u32[]{:S(2)}) %collective-permute-start) | collective-permute-done | bytes 106528 | tf_op jit(solution)/shard_map/ppermute | solution.py:581
  7.8 0.5 %edge_rows.1 = (f32[5,96,128]{2,1,0:T(8,128)S(1)}, f32[5,96,128]{2,1,0:T(8,128)S(1)}, f32[5,96,128]{2,1,0:T(8,128)S(1)}, f32[5,96,128]{2,1,0:T(8,128)S(1)}, f32[...) custom-call(f32[4,96,128]{2,1,0:T(8,128)S(1)} %get-tuple-element.32., ...), custom_call_target="tpu_custom_call" | custom-call | flops 2000000 | bytes 2000000 | tf_op jit(solution)/shard_map/edge_rows/pallas_call | solution.py:594
  8.3 0.7 %collective-permute-start.2 = (f32[5,88,128]{2,1,0:T(8,128)S(1)}, f32[5,88,128]{2,1,0:T(8,128)S(1)}, u32[]{:S(2)}, u32[]{:S(2)}) collective-permute-start(f32[5,88,128]{2,1,0:T(8,128)S(1)} %get-tuple-element.53), channel_id=1, source_target_pairs={{2,4},{4,2},{6,8},{8,6},{10,12},{12,10},{14,16},{16,14},{18,20},{2... | collective-permute-start | bytes 675848 | tf_op jit(solution)/shard_map/ppermute | solution.py:581
  8.9 0.4 %near_rows.1 = (f32[5,96,128]{2,1,0:T(8,128)S(1)}, f32[5,88,128]{2,1,0:T(8,128)S(1)}, f32[2,8,128]{2,1,0:T(8,128)S(1)}, f32[2,8,128]{2,1,0:T(8,128)S(1)}, f32[2,...) custom-call(f32[5,96,128]{2,1,0:T(8,128)S(1)} %get-tuple-element.38.r_i, f32[5,96,128]{2,1,0:T(8,128)S(1)} %get-tuple-element.39.wx_i, ...), custom_call_target="tpu_custom_call" | custom-call | flops 2000000 | bytes 2000000 | tf_op jit(solution)/shard_map/near_rows/pallas_call | solution.py:594
  9.4 3.2 %collective-permute-start.1 = (f32[5,88,128]{2,1,0:T(8,128)S(1)}, f32[5,88,128]{2,1,0:T(8,128)S(1)}, u32[]{:S(2)}, u32[]{:S(2)}) collective-permute-start(f32[5,88,128]{2,1,0:T(8,128)S(1)} %get-tuple-element.52), channel_id=1, source_target_pairs={{0,2},{2,0},{4,6},{6,4},{8,10},{10,8},{12,14},{14,12},{16,18},{18,... | collective-permute-start | bytes 675848 | tf_op jit(solution)/shard_map/ppermute | solution.py:581
  12.5 0.0 collective-permute-done.2.msg_out
  12.5 1.1 %collective-permute-done.1.msg_in = f32[5,88,128]{2,1,0:T(8,128)S(1)} collective-permute-done((f32[5,88,128]{2,1,0:T(8,128)S(1)}, f32[5,88,128]{2,1,0:T(8,128)S(1)}, u32[]{:S(2)}, u32[]{:S(2)}) %collective-permute-start.1) | collective-permute-done | bytes 225312 | tf_op jit(solution)/shard_map/ppermute | solution.py:581
  13.6 2.4 %basis.1 = (f32[32,1,128]{2,1,0:T(1,128)S(1)}, f32[4,96,128]{2,1,0:T(8,128)S(1)}, f32[4,96,128]{2,1,0:T(8,128)S(1)}, f32[4,96,128]{2,1,0:T(8,128)S(1)}, f32[4,96...) custom-call(f32[5,96,128]{2,1,0:T(8,128)S(1)} %get-tuple-element.38.r_i, ...), custom_call_target="tpu_custom_call" | custom-call | flops 2000000 | bytes 2000000 | tf_op jit(solution)/shard_map/basis/pallas_call | solution.py:594
  16.1 16.4 %all_to_all.5.mom = f32[32,1,128]{2,1,0:T(1,128)S(1)} all-to-all(f32[32,1,128]{2,1,0:T(1,128)S(1)} %get-tuple-element.54), channel_id=1, replica_groups=mesh['row'=16,'col'=2] {'row','col'}, dimensions={0} | all-to-all | bytes 32768 | tf_op jit(solution)/shard_map/all_to_all | solution.py:636
  32.5 1.2 %combine.1 = (f32[96,512]{1,0:T(8,128)}, f32[96,512]{1,0:T(8,128)}) custom-call(f32[32,1,128]{2,1,0:T(1,128)S(1)} %all_to_all.5.mom, f32[4,96,128]{2,1,0:T(8,128)S(1)} %get-tuple-element.55.p0, f32[4,96,128]{2,1,0:T(8,128)S(1)} %get-tuple-element.56.p1, f32[4,96,128]{2,1,0:T(8,128)S(1)} %get-tuple-element.57.p2, f32[4,96,128]{2,1,0:T(8,128)S(1)} %get-tuple-element.58.q0, ...), custom_call_target="tpu_custom_call" | custom-call | flops 2000000 | bytes 2000000 | tf_op jit(solution)/shard_map/combine/pallas_call | solution.py:594
Async XLA Ops:
  1.8 6.0 %collective-permute-start = (f32[104,256]{1,0:T(8,128)S(1)}, f32[104,256]{1,0:T(8,128)S(1)}, u32[]{:S(2)}, u32[]{:S(2)}) collective-permute-start(f32[104,256]{1,0:T(8,128)S(1)} %edge_columns.1), channel_id=1, source_target_pairs={{0,1},{1,0},{2,3},{3,2},{4,5},{5,4},{6,7},{7,6},{8,9},{9,8},{10,11... | collective-permute-start | bytes 319496 | tf_op jit(solution)/shard_map/ppermute | solution.py:581
  8.3 4.3 %collective-permute-start.2 = (f32[5,88,128]{2,1,0:T(8,128)S(1)}, f32[5,88,128]{2,1,0:T(8,128)S(1)}, u32[]{:S(2)}, u32[]{:S(2)}) collective-permute-start(f32[5,88,128]{2,1,0:T(8,128)S(1)} %get-tuple-element.53), channel_id=1, source_target_pairs={{2,4},{4,2},{6,8},{8,6},{10,12},{12,10},{14,16},{16,14},{18,20},{2... | collective-permute-start | bytes 675848 | tf_op jit(solution)/shard_map/ppermute | solution.py:581
  9.4 4.3 %collective-permute-start.1 = (f32[5,88,128]{2,1,0:T(8,128)S(1)}, f32[5,88,128]{2,1,0:T(8,128)S(1)}, u32[]{:S(2)}, u32[]{:S(2)}) collective-permute-start(f32[5,88,128]{2,1,0:T(8,128)S(1)} %get-tuple-element.52), channel_id=1, source_target_pairs={{0,2},{2,0},{4,6},{6,4},{8,10},{10,8},{12,14},{14,12},{16,18},{18,... | collective-permute-start | bytes 675848 | tf_op jit(solution)/shard_map/ppermute | solution.py:581

commit v5 on v4

--- a/solution.py
+++ b/solution.py
@@ -10,8 +10,9 @@
 DAMP = 2.0 / 3.0
 SHIFT = 1.0
 HC = 64
-HR = 20
-FG = 24
+HR = 8
+FAR = 12
+DEPTH = 4 * HR + FAR - 1 + 5
 GUARD = 8
 VMEM = pl.BlockSpec(memory_space=pltpu.VMEM)
 HBM = pl.BlockSpec(memory_space=pltpu.HBM)
@@ -72,6 +73,15 @@
 
     def unpack(self, m, k):
         return group_sum(jnp.where(lanes(m.shape) % 4 == k, m, F32(0.0)))
+
+    def unpack_rows(self, m):
+        return group_sum(jnp.where(lanes(m.shape) % 4 == rows(m.shape) % 4, m, F32(0.0)))
+
+    def first_only(self, x):
+        return jnp.where(lanes(x.shape) % 4 == 0, x, F32(0.0))
+
+    def last_only(self, x):
+        return jnp.where(lanes(x.shape) % 4 == 3, x, F32(0.0))
 
 
 class Planes:
@@ -126,6 +136,22 @@
     def unpack(self, m, k):
         h = m[:, 512:640]
         return join([m[:, k * 128 : k * 128 + 128], group_sum(jnp.where(lanes(h.shape) % 4 == k, h, F32(0.0)))])
+
+    def unpack_rows(self, m):
+        a, b, c, d, h = split(m)
+        key = rows(h.shape) % 4
+        own = jnp.where(key < 2, jnp.where(key == 0, a, b), jnp.where(key == 2, c, d))
+        return join([own, group_sum(jnp.where(lanes(h.shape) % 4 == key, h, F32(0.0)))])
+
+    def first_only(self, x):
+        a, _, _, _, h = split(x)
+        none = jnp.zeros_like(h)
+        return join([a, none, none, none, jnp.where(lanes(h.shape) % 4 == 0, h, none)])
+
+    def last_only(self, x):
+        _, _, _, d, h = split(x)
+        none = jnp.zeros_like(h)
+        return join([none, none, none, d, jnp.where(lanes(h.shape) % 4 == 3, h, none)])
 
     def gather_in(self, parts):
         lane = lanes(parts[0].shape)
@@ -313,12 +339,14 @@
         incoming = jnp.broadcast_to(src_h[:, HC : HC + 1], (8, 128))
         src_h = jnp.where(lane == 0, src_h + fx_t[r : r + 8, :], jnp.where(lane == HC, zero, src_h))
         for out, tile, h in ((r_o, r_t, src_h), (wx_o, wx_t, wx_h), (wy_o, wy_t, wy_h), (an_o, an_t, an_h)):
+            top = GUARD if out is wy_o else 0
             for j in range(own):
                 x = tile[j, r : r + 8, :]
                 if out is r_o and j == 0:
                     x = jnp.where(lane == 0, x + incoming, x)
-                out[j, r : r + 8, :] = x
-            out[own, r : r + 8, :] = h
+                out[j, top + r : top + r + 8, :] = x
+            out[own, top + r : top + r + 8, :] = h
+    st(wy_o, 0, jnp.zeros((GUARD, (own + 1) * 128), F32))
     for j in range(own):
         fy_o[j] = fy_t[j]
     fy_o[own] = halo(n, 0)[0]
@@ -331,52 +359,113 @@
     row_odd, _, _, _ = position()
     message(form, jnp.logical_not(row_odd), r_i, wx_i, wy_i, an_i, fy_i, *rest)
     for r in range(8, wx_i.shape[1], 8):
-        w_x, w_y = ld(wx_i, r), ld(wy_i, r)
-        diag = ld(an_i, r) + w_x + form.left(w_x) + w_y + ld(wy_i, r - 1)
+        w_x, w_y = ld(wx_i, r), ld(wy_i, GUARD + r)
+        diag = ld(an_i, r) + w_x + form.left(w_x) + w_y + ld(wy_i, GUARD + r - 1)
         st(di, r, jnp.where(diag > F32(0.0), F32(1.0) / diag, F32(0.0)))
 
 
-def message(form, bottom, r_o, wx_o, wy_o, an_o, fy_o, msg, g_o, cr_o, cd_o, ca_o, u_s, t_s, f_s):
+def message(form, bottom, r_o, wx_o, wy_o, an_o, fy_o, msg, g_o, cr_o, cd_o, ca_o, U, DI, V, FL, T, H, K):
     n = r_o.shape[1]
     zero = F32(0.0)
+    G = GUARD
 
     def pick(low, high):
         return jnp.where(bottom, high, low)
 
-    base = pl.multiple_of(pick(16, n - 32), 8)
-    for r in range(0, 32, 8):
-        at = pl.multiple_of(base - 8 + r, 8)
-        w_x, w_y = ld(wx_o, at), ld(wy_o, at)
-        diag = ld(an_o, at) + w_x + form.left(w_x) + w_y + ld(wy_o, base - 9 + r)
-        st(u_s, 8 + r, jnp.where(diag > zero, ld(r_o, at) / diag, zero))
-    for r in (0, 8):
-        x = ld(u_s, 16 + r)
-        st(f_s, r, ld(wx_o, pl.multiple_of(base + r, 8)) * (x - form.right(x)))
-    for r in (0, 8):
-        at = pl.multiple_of(base + r, 8)
-        x, flow = ld(u_s, 16 + r), ld(f_s, r)
-        down = ld(wy_o, at) * (x - ld(u_s, 17 + r))
-        up = ld(wy_o, base + r - 1) * (x - ld(u_s, 15 + r))
-        st(t_s, r, (ld(an_o, at) * x + (flow - form.left(flow))) + (down + up))
-    sums = form.total(four_rows(t_s, 0, 4))
-    c = pl.multiple_of(pick(16, n - 48), 8)
+    def align(x):
+        return pl.multiple_of(x, 8)
+
+    base = align(pick(0, n - 40))
+    for r in range(0, 40, 8):
+        at = align(base + r)
+        w_x = ld(wx_o, at)
+        diag = ld(an_o, at) + w_x + form.left(w_x) + ld(wy_o, align(at + G)) + ld(wy_o, base + (r + G - 1))
+        inverse = jnp.where(diag > zero, F32(1.0) / diag, zero)
+        st(DI, G + r, inverse)
+        st(U, G + r, ld(r_o, at) * inverse)
+    for source, image in ((U, T), (V, U)):
+        for r in range(0, 40, 8):
+            x = ld(source, G + r)
+            st(FL, G + r, ld(wx_o, align(base + r)) * (x - form.right(x)))
+        for r in range(0, 40, 8):
+            at = align(base + r)
+            x, flow = ld(source, G + r), ld(FL, G + r)
+            down = ld(wy_o, align(at + G)) * (x - ld(source, G + r + 1))
+            up = ld(wy_o, base + (r + G - 1)) * (x - ld(source, G + r - 1))
+            y = (ld(an_o, at) * x + (flow - form.left(flow))) + (down + up)
+            st(image, G + r, y)
+            if image is T:
+                st(V, G + r, ld(DI, G + r) * y)
+    near = align(pick(0, 8))
+    sums = form.total(four_rows(T, align(near + G), 8))
+    sums_2 = form.total(four_rows(U, pick(0, 20) + G, 4))
+    parts = {}
+
+    def add(name, x):
+        parts[name] = parts[name] + x if name in parts else x
+
+    for k in range(4):
+        at = base + (near + k)
+        w_x = ld(wx_o, at, 8, 4)
+        first, last = form.first_only(form.left(w_x)), form.last_only(w_x)
+        a = ld(an_o, at, 8, 4) + first + last
+        inverse = ld(DI, near + (G + k), 8, 4)
+        sides = []
+        if k == 0:
+            w = ld(wy_o, at + (G - 1), 8, 4)
+            sides.append(("u", w))
+            a = a + w
+        if k == 3:
+            w = ld(wy_o, at + G, 8, 4)
+            sides.append(("d", w))
+            a = a + w
+        weighted = inverse * a
+        add("aa", weighted * a)
+        for name, w in (("l", first), ("r", last)):
+            add("a" + name, weighted * w)
+            scaled = inverse * w
+            add(name + name, scaled * w)
+            for other, v in sides:
+                add(name + other, scaled * v)
+        for name, w in sides:
+            add("a" + name, weighted * w)
+            add(name + name, inverse * w * w)
+    parts = {name: form.total(x) for name, x in parts.items()}
+    for k, name in enumerate(("uu", "dd", "au", "ru", "lu")):
+        st(H.at[k], G, parts[name])
+    uu, au, ru, lu = [ld(H.at[k], G + 1) for k in (0, 2, 3, 4)]
+    dd = ld(H.at[1], G - 1)
+    centre = parts["aa"] + form.coarse_right(parts["ll"]) + form.coarse_left(parts["rr"]) + uu + dd
+    east = -(parts["ar"] + form.coarse_right(parts["al"]))
+    south = -(parts["ad"] + au)
+    south_east = form.coarse_right(parts["ld"]) + ru
+    south_west = form.coarse_left(parts["rd"]) + lu
+    for k, x in enumerate((centre, east, south, south_east, south_west)):
+        st(K.at[k], 0, x)
+
+    c = align(pick(0, n - 4 * FAR))
     coarse = (
-        form.total(four_rows(r_o, c, 8)),
-        form.last_column(four_rows(wx_o, c, 8)),
-        form.total(ld(wy_o, c + 3, 8, 4)),
-        form.total(four_rows(an_o, c, 8)),
+        form.total(four_rows(r_o, c, FAR)),
+        form.last_column(four_rows(wx_o, c, FAR)),
+        form.total(ld(wy_o, c + (G + 3), FAR, 4)),
+        form.total(four_rows(an_o, c, FAR)),
     )
     for out, x in zip((g_o, cr_o, cd_o, ca_o), coarse):
         st(out, 0, x)
-    start = pick(0, n - HR)
-    for k, ref in enumerate((r_o, wx_o, wy_o, an_o)):
-        for r in range(0, HR, 4):
-            st(msg, k * HR + r, ld(ref, start + r, 4))
-    outer = pick(HR - 1, 0)
+    start = align(pick(0, n - HR))
+    for k, (ref, top) in enumerate(((r_o, 0), (wx_o, 0), (wy_o, G), (an_o, 0))):
+        st(msg, k * HR, ld(ref, align(start + top), HR))
+    outer, inner = pick(HR - 1, 0), pick(HR - 2, 1)
     st(msg, outer, form.pack(*[sums[k : k + 1] for k in range(4)]))
-    st(msg, HR + outer, form.spread(form.total(ld(wy_o, n - 49, 1))))
+    st(msg, inner, form.pack(*[sums[k : k + 1] for k in range(4, 8)]))
+    st(msg, HR + outer, form.spread(form.total(ld(wy_o, n - 4 * FAR - 1 + G, 1))))
+    st(msg, HR + inner, form.pack(*[sums_2[k : k + 1] for k in range(4)]))
     st(msg, 3 * HR + outer, ld(fy_o, 0, 1))
-    st(msg, 4 * HR, form.pack(*coarse))
+    packed = form.pack(*coarse)
+    st(msg, 4 * HR, jnp.where(bottom, packed[: FAR - 1], packed[1:]))
+    for k in range(5):
+        four = [ld(K.at[k], pick(0, 3) + i, 1) for i in range(4)]
+        st(msg, 4 * HR + FAR - 1 + k, form.pack(*four))
 
 
 def flows(form, v, w_x, flow, starts):
@@ -393,11 +482,11 @@
 
 
 def basis(r_i, wx_i, wy_i, an_i, fy_i, g_a, cr_a, cd_a, ca_a, di_i, g_b, cr_b, cd_b, ca_b, msg_in, msg_out, mom, p0, p1, p2, q0, q1, q2, r0,
-         R, WX, WY, AN, DI, SP, PA, PB, QA, FL, C_L, C_R, C_D, C_A, C_I, EA, EB, GC):
+         R, WX, WY, AN, DI, SP, PA, PB, QA, FL, C_L, C_R, C_D, C_A, C_I, EA, EB, GC, KF, KV):
     blocks, n, _ = r_i.shape
     form = layout(blocks)
-    fine = n + 2 * FG
-    coarse = fine // 4 + 12
+    fine = n + 2 * HR
+    coarse = n // 4 + 2 * FAR
     zero = F32(0.0)
     odd, _, _, _ = position()
     own_blocks = blocks - 1
@@ -412,21 +501,19 @@
     for ref in (R, WX, WY, AN, PA, PB):
         st(ref, 0, zeros)
         st(ref, B + fine, zeros)
-    for k, (ref, own) in enumerate(((R, r_i), (WX, wx_i), (WY, wy_i), (AN, an_i))):
+    for k, (ref, own, top) in enumerate(((R, r_i, 0), (WX, wx_i, 0), (WY, wy_i, GUARD), (AN, an_i, 0))):
         up, down = sides(k * HR, (k + 1) * HR)
-        st(ref, B, zeros[: FG - HR])
-        st(ref, B + FG + n + HR, zeros[: FG - HR])
-        st(ref, B + FG - HR, up)
-        st(ref, B + FG + n, down)
+        st(ref, B, up)
+        st(ref, B + HR + n, down)
         for r in range(0, n, 8):
-            st(ref, B + FG + r, ld(own, r))
+            st(ref, B + HR + r, ld(own, top + r))
     flux_up, _ = sides(3 * HR, 3 * HR + 1)
-    st(R, B + FG, ld(R, B + FG, 1) + flux_up)
-    st(R, B + FG + n, ld(R, B + FG + n, 1) + ld(fy_i, 0, 1))
+    st(R, B + HR, ld(R, B + HR, 1) + flux_up)
+    st(R, B + HR + n, ld(R, B + HR + n, 1) + ld(fy_i, 0, 1))
 
     for r in range(8, n, 8):
-        st(DI, B + FG + r, ld(di_i, r))
-    for r in [*range(B, B + FG + 8, 8), *range(B + FG + n, B + fine, 8)]:
+        st(DI, B + HR + r, ld(di_i, r))
+    for r in [*range(B, B + HR + 8, 8), *range(B + HR + n, B + fine, 8)]:
         w_x, w_y = ld(WX, r), ld(WY, r)
         diag = ld(AN, r) + w_x + form.left(w_x) + w_y + ld(WY, r - 1)
         st(DI, r, jnp.where(diag > zero, F32(1.0) / diag, zero))
@@ -434,22 +521,22 @@
     for ref in (EA, EB, C_D):
         st(ref, 0, coarse_zeros)
         st(ref, B + coarse, coarse_zeros)
-    up, down = sides(4 * HR, 4 * HR + 8)
-    for k, ref in enumerate((GC, C_R, C_D, C_A)):
+    up, down = sides(4 * HR, 4 * HR + FAR - 1)
+    for k, (ref, a, b) in enumerate(((GC, g_a, g_b), (C_R, cr_a, cr_b), (C_D, cd_a, cd_b), (C_A, ca_a, ca_b))):
         st(ref, B, form.unpack(up, k))
-        st(ref, B + coarse - 8, form.unpack(down, k))
+        st(ref, B + coarse - FAR + 1, form.unpack(down, k))
+        x, y = ld(a, 0, FAR), ld(b, 0, FAR)
+        st(ref, B + FAR, jnp.where(odd, y, x))
+        st(ref, B + 2 * FAR, jnp.where(odd, x, y))
+    st(GC, B + FAR, ld(GC, B + FAR, 1) + form.total(flux_up))
     beyond, _ = sides(HR, HR + 1)
     st(C_D, B - 1, form.take(beyond))
-    for ref, a, b in ((GC, g_a, g_b), (C_R, cr_a, cr_b), (C_D, cd_a, cd_b), (C_A, ca_a, ca_b)):
-        x, y = ld(a, 0), ld(b, 0)
-        st(ref, B + 16, jnp.where(odd, y, x))
-        st(ref, B + 24, jnp.where(odd, x, y))
-    for c in (8, coarse - 16):
-        f = B + 4 * c - 24
-        st(GC, B + c, form.total(four_rows(R, f, 8)))
-        st(C_R, B + c, form.last_column(four_rows(WX, f, 8)))
-        st(C_D, B + c, form.total(ld(WY, f + 3, 8, 4)))
-        st(C_A, B + c, form.total(four_rows(AN, f, 8)))
+    for c in (FAR - 1, coarse - FAR):
+        f = B + 4 * c - 40
+        st(GC, B + c, form.total(four_rows(R, f, 1)))
+        st(C_R, B + c, form.last_column(four_rows(WX, f, 1)))
+        st(C_D, B + c, form.total(ld(WY, f + 3, 1)))
+        st(C_A, B + c, form.total(four_rows(AN, f, 1)))
     for c in range(B, B + coarse, 8):
         c_r = ld(C_R, c)
         c_l = form.coarse_left(c_r)
@@ -474,14 +561,38 @@
                 beside = beside + (ld(C_D, c - 1) * ld(old, c - 1) + ld(C_D, c) * ld(old, c + 1))
                 st(new, c, F32(1.0 - DAMP) * e + ld(C_I, c) * (ld(GC, c) + beside))
             old, new = new, old
-        first, last = max(lo, 6), min(hi, coarse - 6)
-        count = last - first
         for k in range(4):
-            st(SP, B + 4 * (first - 6) + k, form.spread(ld(EB, B + first, count)), 4)
+            st(SP, B + k, form.spread(ld(EB, B + 10, fine // 4)), 4)
 
     def restrict(q):
-        for c in range(8, coarse - 8, 8):
-            st(GC, B + c, form.total(four_rows(q, B + 4 * c - 24, 8)))
+        for c in range(FAR - 1, coarse - FAR + 1, 8):
+            count = min(8, coarse - FAR + 1 - c)
+            st(GC, B + c, form.total(four_rows(q, B + 4 * c - 40, count)))
+
+    def coarse_image(c, count):
+        e = ld(EB, B + c, count)
+        c_l, c_r = ld(C_L, B + c, count), ld(C_R, B + c, count)
+        image = ld(C_A, B + c, count) * e + c_l * (e - form.coarse_left(e)) + c_r * (e - form.coarse_right(e))
+        image = image + ld(C_D, B + c - 1, count) * (e - ld(EB, B + c - 1, count))
+        return image + ld(C_D, B + c, count) * (e - ld(EB, B + c + 1, count))
+
+    def stretch(a, b):
+        shape = (8, a.shape[1])
+        return form.unpack_rows(jnp.where(rows(shape) < 4, jnp.broadcast_to(a, shape), jnp.broadcast_to(b, shape)))
+
+    def second_sums(side, c, sums):
+        for k in range(5):
+            at = 4 * HR + FAR - 1 + k
+            row = sides(at, at + 1)[side]
+            st(KF.at[k], 8, form.unpack_rows(jnp.broadcast_to(row, (4, row.shape[1]))))
+        centre, east, south, south_east, south_west = [ld(KF.at[k], 8, 4) for k in range(5)]
+        north, north_west, north_east = [ld(KF.at[k], 7, 4) for k in (2, 3, 4)]
+        e, below, above = [ld(EB, B + c + d, 4) for d in (0, 1, -1)]
+        image = centre * e + east * form.coarse_right(e) + form.coarse_left(east * e)
+        image = image + south * below + north * above
+        image = image + south_east * form.coarse_right(below) + form.coarse_left(north_west * above)
+        image = image + south_west * form.coarse_left(below) + form.coarse_right(north_east * above)
+        st(KV.at[side], 0, image + form.unpack_rows(jnp.broadcast_to(sums, (4, sums.shape[1]))))
 
     smooth(0, coarse)
     for r in range(B, B + fine, 8):
@@ -490,40 +601,45 @@
     for r in range(B, B + fine, 8):
         st(QA, r, apply_a(PA, form.left, FL, WY, AN, r))
     restrict(QA)
-    s_up, _ = sides(0, 1)
-    _, s_down = sides(HR - 1, HR)
-    for c, s, off in ((0, s_up, 4), (coarse - 8, s_down, 0)):
-        c = B + c
-        e = ld(EB, c)
-        part = jnp.zeros_like(e)
-        for k in range(4):
-            part = jnp.where(rows(e.shape) == off + k, jnp.broadcast_to(form.unpack(s, k), e.shape), part)
-        image = ld(C_A, c) * e + ld(C_L, c) * (e - form.coarse_left(e)) + ld(C_R, c) * (e - form.coarse_right(e))
-        image = image + ld(C_D, c - 1) * (e - ld(EB, c - 1))
-        image = image + ld(C_D, c) * (e - ld(EB, c + 1))
-        st(GC, c, part + image)
+    far_up, _ = sides(0, 1)
+    near_up, _ = sides(1, 2)
+    _, near_down = sides(HR - 1, HR)
+    _, far_down = sides(HR - 2, HR - 1)
+    up = stretch(far_up, near_up)
+    down = stretch(near_down, far_down)
+    image = coarse_image(0, FAR - 1)
+    st(GC, B, image[0:4])
+    st(GC, B + 4, image[4:] + up[0 : FAR - 5])
+    image = coarse_image(coarse - FAR + 1, FAR - 1)
+    st(GC, B + coarse - FAR + 1, image[0:7] + down[1:])
+    st(GC, B + coarse - 4, image[7:])
+    second_sums(0, 7, sides(HR + 1, HR + 2)[0])
+    second_sums(1, coarse - FAR, sides(2 * HR - 2, 2 * HR - 1)[1])
     for r in range(0, n, 8):
-        f = B + FG + r
+        f = B + HR + r
         for out, ref in ((p0, PA), (q0, QA), (r0, R)):
             out[:, r : r + 8, :] = ref[:own_blocks, f : f + 8, :]
     smooth(0, coarse)
     for r in range(B, B + fine, 8):
         st(PB, r, (ld(DI, r) * ld(QA, r) + ld(SP, r)) - F32(SHIFT) * ld(PA, r))
-    flows(form, PB, WX, FL, range(B + 8, B + fine - 8, 8))
-    for r in range(B + 8, B + fine - 8, 8):
+    flows(form, PB, WX, FL, range(B, B + fine, 8))
+    for r in range(B, B + fine, 8):
         st(QA, r, apply_a(PB, form.left, FL, WY, AN, r))
     restrict(QA)
+    for c, side, first in ((8, 0, 1), (coarse - FAR + 1, 1, 1)):
+        image = coarse_image(c, 3) + ld(KV.at[side], first, 3)
+        st(GC, B + c, image - F32(SHIFT) * ld(GC, B + c, 3))
     for r in range(0, n, 8):
-        f = B + FG + r
+        f = B + HR + r
         for out, ref in ((p1, PB), (q1, QA)):
             out[:, r : r + 8, :] = ref[:own_blocks, f : f + 8, :]
     smooth(8, coarse - 8)
-    for r in range(B + FG - 8, B + FG + n + 8, 8):
+    for r in range(B + HR - 8, B + HR + n + 8, 8):
         st(PA, r, (ld(DI, r) * ld(QA, r) + ld(SP, r)) - F32(SHIFT) * ld(PB, r))
-    flows(form, PA, WX, FL, range(B + FG, B + FG + n, 8))
+    flows(form, PA, WX, FL, range(B + HR, B + HR + n, 8))
     acc = [jnp.zeros((8, 128), F32) for _ in range(9)]
     for r in range(0, n, 8):
-        f = B + FG + r
+        f = B + HR + r
         image = apply_a(PA, form.left, FL, WY, AN, f)
         sums = [[] for _ in acc]
         for j in range(own_blocks):
@@ -608,30 +724,29 @@
         halos.append(swap(edge, "col", ncol, inner))
     tile = shape(nb - 1, n, 128)
     own = call(tile_fields, "tile_fields", fields, [tile] * 4 + [shape(n, 128), shape(nb - 1, 8, 128)], [(n, width)] * 6 + [(4, nb - 1, n, 128)] * 2 + [(2, nb - 1, 8, 128)], 1, 6)
-    depth = 4 * HR + 8
     cb = layout(nb).coarse_blocks
-    far = shape(cb, 8, 128)
-    msg = shape(nb, depth, 128)
+    far = shape(cb, FAR, 128)
+    msg = shape(nb, DEPTH, 128)
     field = shape(nb, n, 128)
-    work = [(nb, 48, 128), (nb, 16, 128), (nb, 16, 128)]
+    work = [(nb, 40 + 2 * GUARD, 128)] * 5 + [(5, cb, 24, 128), (5, cb, 8, 128)]
     *fields, to_out, g_a, cr_a, cd_a, ca_a = call(
         functools.partial(edge_rows, len(halos) > 1),
         "edge_rows",
         (*own, *halos),
-        [field] * 4 + [shape(nb, 8, 128), msg] + [far] * 4,
+        [field, field, shape(nb, GUARD + n, 128), field, shape(nb, 8, 128), msg] + [far] * 4,
         work,
     )
     from_out = swap(to_out, "row", nrow, False)
     di, to_in, *far_b = call(near_rows, "near_rows", fields, [field, msg] + [far] * 4, work)
     from_in = swap(to_in, "row", nrow, True)
-    fine = n + 2 * FG
-    coarse = fine // 4 + 12
+    fine = n + 2 * HR
+    coarse = n // 4 + 2 * FAR
     mom, *vectors = call(
         basis,
         "basis",
         (*fields, g_a, cr_a, cd_a, ca_a, di, *far_b, from_in, from_out),
         [shape(nrow * ncol, 1, 128)] + [tile] * 7,
-        [(nb, fine + 2 * GUARD, 128)] * 10 + [(cb, coarse + 2 * GUARD, 128)] * 8,
+        [(nb, fine + 2 * GUARD, 128)] * 10 + [(cb, coarse + 2 * GUARD, 128)] * 8 + [(5, cb, 16, 128), (2, cb, 8, 128)],
     )
     mom = lax.all_to_all(mom, ("row", "col"), 0, 0, tiled=True)
     out = shape(n, width)

time: 33.9 us -> 32.5 us (0.959)
  blocking collectives: 16.4 us -> 14 us
  Pallas kernels: 7.83 us -> 8.99 us
    all_to_all x1, blocking collectives: 16.4 us -> 14 us  [local(): mom = lax.all_to_all(mom, ('row', 'col'), 0, 0, tiled=True)]
    pallas_call x6, Pallas kernels: 7.83 us -> 8.99 us  [call(): pl.pallas_call(kernel, in_specs=[HBM if fetches else VMEM] * len(args), o...]
  transfers between devices with their start and end apart: 3 -> 3, of which waited for: 2 -> 2; matrix products, arithmetic and copies ran while one was open for 0% -> 0% of each run, Pallas kernels for 8% -> 9%
where the time goes in v5:
time: 32.5 us; the launch traced here: 32.2 us
  blocking collectives  14 us (43%)
  Pallas kernels  8.99 us (28%)
  starting transfers between devices  6.83 us (21%)
  waiting for transfers between devices  1.77 us (5%)
  between operations  0.66 us (2%)
    all_to_all x1, blocking collectives, local(): mom = lax.all_to_all(mom, ('row', 'col'), 0, 0, tiled=True)  14 us
    pallas_call x6, Pallas kernels, call(): pl.pallas_call(kernel, in_specs=[HBM if fetches else VMEM] * len(args), o...  8.99 us
    ppermute x3, starting transfers between devices, swap(): return lax.ppermute(x, axis, pairs)  6.83 us
    ppermute x3, waiting for transfers between devices, swap(): return lax.ppermute(x, axis, pairs)  1.77 us
  transfers between devices with their start and end apart: 3, of which 2 were waited for; matrix products, arithmetic and copies ran while one was open for 0% of the time, Pallas kernels for 9%

profile of v5, /device:TPU:0, one launch (start us, length us, event | category | flops | bytes accessed | tf_op | source)
XLA Modules:
  0.0 32.2 jit_solution(13233169779551001826)
XLA Ops:
  0.6 1.2 %edge_columns.1 = f32[104,256]{1,0:T(8,128)S(1)} custom-call(f32[96,512]{1,0:T(8,128)} %refs_0_.3, f32[96,512]{1,0:T(8,128)} %refs_1_.3, f32[96,512]{1,0:T(8,128)} %refs_2_.3, f32[96,512]{1,0:T(8,128)} %refs_3_.3, f32[96,512]{1,0:T(8,128)} %refs_4_.3, f32[96,512]{1,0:T(8,128)} %refs_5_.3), custom_call_target="tpu_custom_call" | custom-call | flops 2000000 | bytes 2000000 | tf_op jit(solution)/shard_map/edge_columns/pallas_call | solution.py:710
  1.8 3.0 %collective-permute-start = (f32[104,256]{1,0:T(8,128)S(1)}, f32[104,256]{1,0:T(8,128)S(1)}, u32[]{:S(2)}, u32[]{:S(2)}) collective-permute-start(f32[104,256]{1,0:T(8,128)S(1)} %edge_columns.1), channel_id=1, source_target_pairs={{0,1},{1,0},{2,3},{3,2},{4,5},{5,4},{6,7},{7,6},{8,9},{9,8},{10,11... | collective-permute-start | bytes 319496 | tf_op jit(solution)/shard_map/ppermute | solution.py:697
  4.8 2.2 %tile_fields.1 = (f32[4,96,128]{2,1,0:T(8,128)S(1)}, f32[4,96,128]{2,1,0:T(8,128)S(1)}, f32[4,96,128]{2,1,0:T(8,128)S(1)}, f32[4,96,128]{2,1,0:T(8,128)S(1)}, f3...) custom-call(f32[96,512]{1,0:T(8,128)} %refs_0_.3, f32[96,512]{1,0:T(8,128)} %refs_1_.3, f32[96,512]{1,0:T(8,128)} %refs_2_.3, ...), custom_call_target="tpu_custom_call" | custom-call | flops 2000000 | bytes 2000000 | tf_op jit(solution)/shard_map/tile_fields/pallas_call | solution.py:710
  7.0 0.8 %collective-permute-done.refs_0_ = f32[104,256]{1,0:T(8,128)S(1)} collective-permute-done((f32[104,256]{1,0:T(8,128)S(1)}, f32[104,256]{1,0:T(8,128)S(1)}, u32[]{:S(2)}, u32[]{:S(2)}) %collective-permute-start) | collective-permute-done | bytes 106528 | tf_op jit(solution)/shard_map/ppermute | solution.py:697
  7.8 1.0 %edge_rows.1 = (f32[5,96,128]{2,1,0:T(8,128)S(1)}, f32[5,96,128]{2,1,0:T(8,128)S(1)}, f32[5,104,128]{2,1,0:T(8,128)S(1)}, f32[5,96,128]{2,1,0:T(8,128)S(1)}, f32...) custom-call(f32[4,96,128]{2,1,0:T(8,128)S(1)} %get-tuple-element.32., ...), custom_call_target="tpu_custom_call" | custom-call | flops 2000000 | bytes 2000000 | tf_op jit(solution)/shard_map/edge_rows/pallas_call | solution.py:710
  8.8 0.7 %collective-permute-start.2 = (f32[5,48,128]{2,1,0:T(8,128)S(1)}, f32[5,48,128]{2,1,0:T(8,128)S(1)}, u32[]{:S(2)}, u32[]{:S(2)}) collective-permute-start(f32[5,48,128]{2,1,0:T(8,128)S(1)} %get-tuple-element.53), channel_id=1, source_target_pairs={{2,4},{4,2},{6,8},{8,6},{10,12},{12,10},{14,16},{16,14},{18,20},{2... | collective-permute-start | bytes 368648 | tf_op jit(solution)/shard_map/ppermute | solution.py:697
  9.5 0.8 %near_rows.1 = (f32[5,96,128]{2,1,0:T(8,128)S(1)}, f32[5,48,128]{2,1,0:T(8,128)S(1)}, f32[2,12,128]{2,1,0:T(8,128)S(1)}, f32[2,12,128]{2,1,0:T(8,128)S(1)}, f32[...) custom-call(f32[5,96,128]{2,1,0:T(8,128)S(1)} %get-tuple-element.38.r_i, f32[5,96,128]{2,1,0:T(8,128)S(1)} %get-tuple-element.39.wx_i, ...), custom_call_target="tpu_custom_call" | custom-call | flops 2000000 | bytes 2000000 | tf_op jit(solution)/shard_map/near_rows/pallas_call | solution.py:710
  10.3 3.2 %collective-permute-start.1 = (f32[5,48,128]{2,1,0:T(8,128)S(1)}, f32[5,48,128]{2,1,0:T(8,128)S(1)}, u32[]{:S(2)}, u32[]{:S(2)}) collective-permute-start(f32[5,48,128]{2,1,0:T(8,128)S(1)} %get-tuple-element.52), channel_id=1, source_target_pairs={{0,2},{2,0},{4,6},{6,4},{8,10},{10,8},{12,14},{14,12},{16,18},{18,... | collective-permute-start | bytes 368648 | tf_op jit(solution)/shard_map/ppermute | solution.py:697
  13.4 0.0 collective-permute-done.2.msg_out
  13.4 1.0 %collective-permute-done.1.msg_in = f32[5,48,128]{2,1,0:T(8,128)S(1)} collective-permute-done((f32[5,48,128]{2,1,0:T(8,128)S(1)}, f32[5,48,128]{2,1,0:T(8,128)S(1)}, u32[]{:S(2)}, u32[]{:S(2)}) %collective-permute-start.1) | collective-permute-done | bytes 122912 | tf_op jit(solution)/shard_map/ppermute | solution.py:697
  14.4 2.7 %basis.1 = (f32[32,1,128]{2,1,0:T(1,128)S(1)}, f32[4,96,128]{2,1,0:T(8,128)S(1)}, f32[4,96,128]{2,1,0:T(8,128)S(1)}, f32[4,96,128]{2,1,0:T(8,128)S(1)}, f32[4,96...) custom-call(f32[5,96,128]{2,1,0:T(8,128)S(1)} %get-tuple-element.38.r_i, ...), custom_call_target="tpu_custom_call" | custom-call | flops 2000000 | bytes 2000000 | tf_op jit(solution)/shard_map/basis/pallas_call | solution.py:710
  17.1 14.0 %all_to_all.5.mom = f32[32,1,128]{2,1,0:T(1,128)S(1)} all-to-all(f32[32,1,128]{2,1,0:T(1,128)S(1)} %get-tuple-element.54), channel_id=1, replica_groups=mesh['row'=16,'col'=2] {'row','col'}, dimensions={0} | all-to-all | bytes 32768 | tf_op jit(solution)/shard_map/all_to_all | solution.py:751
  31.1 1.2 %combine.1 = (f32[96,512]{1,0:T(8,128)}, f32[96,512]{1,0:T(8,128)}) custom-call(f32[32,1,128]{2,1,0:T(1,128)S(1)} %all_to_all.5.mom, f32[4,96,128]{2,1,0:T(8,128)S(1)} %get-tuple-element.55.p0, f32[4,96,128]{2,1,0:T(8,128)S(1)} %get-tuple-element.56.p1, f32[4,96,128]{2,1,0:T(8,128)S(1)} %get-tuple-element.57.p2, f32[4,96,128]{2,1,0:T(8,128)S(1)} %get-tuple-element.58.q0, ...), custom_call_target="tpu_custom_call" | custom-call | flops 2000000 | bytes 2000000 | tf_op jit(solution)/shard_map/combine/pallas_call | solution.py:710
Async XLA Ops:
  1.8 6.0 %collective-permute-start = (f32[104,256]{1,0:T(8,128)S(1)}, f32[104,256]{1,0:T(8,128)S(1)}, u32[]{:S(2)}, u32[]{:S(2)}) collective-permute-start(f32[104,256]{1,0:T(8,128)S(1)} %edge_columns.1), channel_id=1, source_target_pairs={{0,1},{1,0},{2,3},{3,2},{4,5},{5,4},{6,7},{7,6},{8,9},{9,8},{10,11... | collective-permute-start | bytes 319496 | tf_op jit(solution)/shard_map/ppermute | solution.py:697
  8.8 4.7 %collective-permute-start.2 = (f32[5,48,128]{2,1,0:T(8,128)S(1)}, f32[5,48,128]{2,1,0:T(8,128)S(1)}, u32[]{:S(2)}, u32[]{:S(2)}) collective-permute-start(f32[5,48,128]{2,1,0:T(8,128)S(1)} %get-tuple-element.53), channel_id=1, source_target_pairs={{2,4},{4,2},{6,8},{8,6},{10,12},{12,10},{14,16},{16,14},{18,20},{2... | collective-permute-start | bytes 368648 | tf_op jit(solution)/shard_map/ppermute | solution.py:697
  10.3 4.1 %collective-permute-start.1 = (f32[5,48,128]{2,1,0:T(8,128)S(1)}, f32[5,48,128]{2,1,0:T(8,128)S(1)}, u32[]{:S(2)}, u32[]{:S(2)}) collective-permute-start(f32[5,48,128]{2,1,0:T(8,128)S(1)} %get-tuple-element.52), channel_id=1, source_target_pairs={{0,2},{2,0},{4,6},{6,4},{8,10},{10,8},{12,14},{14,12},{16,18},{18,... | collective-permute-start | bytes 368648 | tf_op jit(solution)/shard_map/ppermute | solution.py:697

commit v6 on v5

--- a/solution.py
+++ b/solution.py
@@ -36,9 +36,11 @@
 
 
 def group_sum(x):
-    lane = lanes(x.shape)
-    x = x + jnp.where(lane % 2 == 0, roll_left(x), roll_right(x))
-    return x + jnp.where(lane % 4 < 2, roll_left(x, 2), roll_right(x, 2))
+    four = lanes(x.shape) % 4
+    one = jnp.where(four < 3, roll_left(x), roll_right(x, 3))
+    two = jnp.where(four < 2, roll_left(x, 2), roll_right(x, 2))
+    three = jnp.where(four < 1, roll_left(x, 3), roll_right(x))
+    return (x + two) + (one + three)
 
 
 def split(x):
@@ -56,7 +58,7 @@
     left, right = staticmethod(roll_right), staticmethod(roll_left)
     total = staticmethod(group_sum)
     spread = take = staticmethod(lambda x: x)
-    steps_in = steps_out = ()
+    steps_in = steps_out = (lambda parts: parts,)
 
     def coarse_left(self, e):
         return roll_right(e, 4)
@@ -192,6 +194,17 @@
         return self.swap_halves, self.swap_quarters, self.gather_out
 
 
+class Rows:
+    def __init__(self, own, ends):
+        self.own, self.ends = own, ends
+
+    def chunk(self, start):
+        start -= GUARD + HR
+        if 0 <= start < self.own.shape[1]:
+            return ld(self.own, start)
+        return ld(self.ends.at[int(start >= 0)], 0)
+
+
 def layout(blocks):
     return Planes() if blocks == 5 else Wide(128 * (blocks - 1))
 
@@ -234,10 +247,10 @@
             y = target if k == len(steps) - 1 else y
             for r in range(0, x.shape[1], 8):
                 for j, block in enumerate(step([x[j, r : r + 8, :] for j in range(x.shape[0])])):
-                    y[j, r : r + 8, :] = block
-    if not steps:
-        for x, target in zip(sources, targets):
-            target[...] = x[...]
+                    if len(y.shape) == 2:
+                        y[r : r + 8, j * 128 : j * 128 + 128] = block
+                    else:
+                        y[j, r : r + 8, :] = block
 
 
 def fetch(sources, targets, sems):
@@ -354,17 +367,19 @@
     message(form, row_odd, r_o, wx_o, wy_o, an_o, fy_o, *rest)
 
 
-def near_rows(r_i, wx_i, wy_i, an_i, fy_i, di, *rest):
+def near_rows(r_i, wx_i, wy_i, an_i, fy_i, di, wl, *rest):
     form = layout(wx_i.shape[0])
     row_odd, _, _, _ = position()
     message(form, jnp.logical_not(row_odd), r_i, wx_i, wy_i, an_i, fy_i, *rest)
-    for r in range(8, wx_i.shape[1], 8):
+    for r in range(0, wx_i.shape[1], 8):
         w_x, w_y = ld(wx_i, r), ld(wy_i, GUARD + r)
-        diag = ld(an_i, r) + w_x + form.left(w_x) + w_y + ld(wy_i, GUARD + r - 1)
+        w_l = form.left(w_x)
+        st(wl, r, w_l)
+        diag = ld(an_i, r) + w_x + w_l + w_y + ld(wy_i, GUARD + r - 1)
         st(di, r, jnp.where(diag > F32(0.0), F32(1.0) / diag, F32(0.0)))
 
 
-def message(form, bottom, r_o, wx_o, wy_o, an_o, fy_o, msg, g_o, cr_o, cd_o, ca_o, U, DI, V, FL, T, H, K):
+def message(form, bottom, r_o, wx_o, wy_o, an_o, fy_o, msg, g_o, cr_o, cd_o, ca_o, U, DI, V, WL, T, H, K):
     n = r_o.shape[1]
     zero = F32(0.0)
     G = GUARD
@@ -379,20 +394,20 @@
     for r in range(0, 40, 8):
         at = align(base + r)
         w_x = ld(wx_o, at)
-        diag = ld(an_o, at) + w_x + form.left(w_x) + ld(wy_o, align(at + G)) + ld(wy_o, base + (r + G - 1))
+        w_l = form.left(w_x)
+        st(WL, G + r, w_l)
+        diag = ld(an_o, at) + w_x + w_l + ld(wy_o, align(at + G)) + ld(wy_o, base + (r + G - 1))
         inverse = jnp.where(diag > zero, F32(1.0) / diag, zero)
         st(DI, G + r, inverse)
         st(U, G + r, ld(r_o, at) * inverse)
     for source, image in ((U, T), (V, U)):
         for r in range(0, 40, 8):
+            at = align(base + r)
             x = ld(source, G + r)
-            st(FL, G + r, ld(wx_o, align(base + r)) * (x - form.right(x)))
-        for r in range(0, 40, 8):
-            at = align(base + r)
-            x, flow = ld(source, G + r), ld(FL, G + r)
+            beside = ld(WL, G + r) * (x - form.left(x)) + ld(wx_o, at) * (x - form.right(x))
             down = ld(wy_o, align(at + G)) * (x - ld(source, G + r + 1))
             up = ld(wy_o, base + (r + G - 1)) * (x - ld(source, G + r - 1))
-            y = (ld(an_o, at) * x + (flow - form.left(flow))) + (down + up)
+            y = (ld(an_o, at) * x + beside) + (down + up)
             st(image, G + r, y)
             if image is T:
                 st(V, G + r, ld(DI, G + r) * y)
@@ -407,7 +422,7 @@
     for k in range(4):
         at = base + (near + k)
         w_x = ld(wx_o, at, 8, 4)
-        first, last = form.first_only(form.left(w_x)), form.last_only(w_x)
+        first, last = form.first_only(ld(WL, near + (G + k), 8, 4)), form.last_only(w_x)
         a = ld(an_o, at, 8, 4) + first + last
         inverse = ld(DI, near + (G + k), 8, 4)
         sides = []
@@ -468,21 +483,16 @@
         st(msg, 4 * HR + FAR - 1 + k, form.pack(*four))
 
 
-def flows(form, v, w_x, flow, starts):
-    for r in starts:
-        x = ld(v, r)
-        st(flow, r, ld(w_x, r) * (x - form.right(x)))
-
-
-def apply_a(v, flow_left, flow, w_y, an, r):
+def apply_a(form, v, w_l, w_r, w_y, an, r):
     x = ld(v, r)
     down = ld(w_y, r) * (x - ld(v, r + 1))
     up = ld(w_y, r - 1) * (x - ld(v, r - 1))
-    return (ld(an, r) * x + (ld(flow, r) - flow_left(ld(flow, r)))) + (down + up)
-
-
-def basis(r_i, wx_i, wy_i, an_i, fy_i, g_a, cr_a, cd_a, ca_a, di_i, g_b, cr_b, cd_b, ca_b, msg_in, msg_out, mom, p0, p1, p2, q0, q1, q2, r0,
-         R, WX, WY, AN, DI, SP, PA, PB, QA, FL, C_L, C_R, C_D, C_A, C_I, EA, EB, GC, KF, KV):
+    beside = w_l.chunk(r) * (x - form.left(x)) + w_r.chunk(r) * (x - form.right(x))
+    return (an.chunk(r) * x + beside) + (down + up)
+
+
+def basis(r_i, wx_i, wy_i, an_i, fy_i, g_a, cr_a, cd_a, ca_a, di_i, wl_i, g_b, cr_b, cd_b, ca_b, msg_in, msg_out, mom, p0, p1, p2, q0, q1, q2, r0,
+         ENDS, WY, PA, PB, QA, C_L, C_R, C_D, C_A, C_I, EA, EB, GC, KF, KV):
     blocks, n, _ = r_i.shape
     form = layout(blocks)
     fine = n + 2 * HR
@@ -498,25 +508,36 @@
 
     zeros = jnp.zeros((B, blocks * 128), F32)
     coarse_zeros = jnp.zeros((B, form.coarse_blocks * 128), F32)
-    for ref in (R, WX, WY, AN, PA, PB):
+    R, WX, AN, DI, WL = [Rows(own, ENDS.at[k]) for k, own in enumerate((r_i, wx_i, an_i, di_i, wl_i))]
+    for ref in (WY, PA, PB):
         st(ref, 0, zeros)
         st(ref, B + fine, zeros)
-    for k, (ref, own, top) in enumerate(((R, r_i, 0), (WX, wx_i, 0), (WY, wy_i, GUARD), (AN, an_i, 0))):
-        up, down = sides(k * HR, (k + 1) * HR)
-        st(ref, B, up)
-        st(ref, B + HR + n, down)
-        for r in range(0, n, 8):
-            st(ref, B + HR + r, ld(own, top + r))
+    for k, ends in ((0, ENDS.at[0]), (1, ENDS.at[1]), (3, ENDS.at[2])):
+        for end, x in enumerate(sides(k * HR, (k + 1) * HR)):
+            st(ends.at[end], 0, x)
+    up, down = sides(2 * HR, 3 * HR)
+    st(WY, B, up)
+    st(WY, B + HR + n, down)
+    for r in range(0, n, 8):
+        st(WY, B + HR + r, ld(wy_i, GUARD + r))
     flux_up, _ = sides(3 * HR, 3 * HR + 1)
-    st(R, B + HR, ld(R, B + HR, 1) + flux_up)
-    st(R, B + HR + n, ld(R, B + HR + n, 1) + ld(fy_i, 0, 1))
-
-    for r in range(8, n, 8):
-        st(DI, B + HR + r, ld(di_i, r))
-    for r in [*range(B, B + HR + 8, 8), *range(B + HR + n, B + fine, 8)]:
-        w_x, w_y = ld(WX, r), ld(WY, r)
-        diag = ld(AN, r) + w_x + form.left(w_x) + w_y + ld(WY, r - 1)
-        st(DI, r, jnp.where(diag > zero, F32(1.0) / diag, zero))
+    first_rows = ld(r_i, 0) + jnp.where(rows(zeros.shape) == 0, jnp.broadcast_to(flux_up, zeros.shape), zero)
+    below = ENDS.at[0, 1]
+    st(below, 0, ld(below, 0, 1) + ld(fy_i, 0, 1))
+
+    for end in (0, 1):
+        st(ENDS.at[4, end], 0, form.left(ld(ENDS.at[1, end], 0)))
+
+    def inverse(r):
+        diag = AN.chunk(r) + WX.chunk(r) + WL.chunk(r) + ld(WY, r) + ld(WY, r - 1)
+        return jnp.where(diag > zero, F32(1.0) / diag, zero)
+
+    st(ENDS.at[3, 0], 0, inverse(B))
+    st(ENDS.at[3, 1], 0, inverse(B + HR + n))
+    first_inverse = inverse(B + HR)
+
+    def read(field, r, first):
+        return first if r == B + HR else field.chunk(r)
 
     for ref in (EA, EB, C_D):
         st(ref, 0, coarse_zeros)
@@ -533,20 +554,25 @@
     st(C_D, B - 1, form.take(beyond))
     for c in (FAR - 1, coarse - FAR):
         f = B + 4 * c - 40
-        st(GC, B + c, form.total(four_rows(R, f, 1)))
-        st(C_R, B + c, form.last_column(four_rows(WX, f, 1)))
+        end, at = (0, 4) if c < FAR else (1, 0)
+        st(GC, B + c, form.total(four_rows(ENDS.at[0, end], at, 1)))
+        st(C_R, B + c, form.last_column(four_rows(ENDS.at[1, end], at, 1)))
         st(C_D, B + c, form.total(ld(WY, f + 3, 1)))
-        st(C_A, B + c, form.total(four_rows(AN, f, 1)))
+        st(C_A, B + c, form.total(four_rows(ENDS.at[2, end], at, 1)))
     for c in range(B, B + coarse, 8):
         c_r = ld(C_R, c)
         c_l = form.coarse_left(c_r)
         total = ld(C_A, c) + c_l + c_r + ld(C_D, c - 1) + ld(C_D, c)
         st(C_L, c, c_l)
-        st(C_I, c, jnp.where(total > zero, F32(DAMP) / total, zero))
+        inverse_c = jnp.where(total > zero, F32(DAMP) / total, zero)
+        st(C_I, c, inverse_c)
+        st(EA, c, inverse_c * ld(GC, c))
+
+    def set_sums(c, g):
+        st(GC, B + c, g)
+        st(EA, B + c, ld(C_I, B + c, g.shape[0]) * g)
 
     def smooth(lo, hi):
-        for c in range(lo, hi, 8):
-            st(EA, B + c, ld(C_I, B + c) * ld(GC, B + c))
         if lo > 0:
             st(EA, B + lo - 8, coarse_zeros)
             st(EB, B + lo - 8, coarse_zeros)
@@ -561,13 +587,34 @@
                 beside = beside + (ld(C_D, c - 1) * ld(old, c - 1) + ld(C_D, c) * ld(old, c + 1))
                 st(new, c, F32(1.0 - DAMP) * e + ld(C_I, c) * (ld(GC, c) + beside))
             old, new = new, old
-        for k in range(4):
-            st(SP, B + k, form.spread(ld(EB, B + 10, fine // 4)), 4)
+
+    def coarse_part(r):
+        at = B + 10 + (r - B) // 4
+        shape = (8, form.coarse_blocks * 128)
+        a, b = [jnp.broadcast_to(ld(EB, at + k, 1), shape) for k in (0, 1)]
+        return form.spread(jnp.where(rows(shape) < 4, a, b))
+
+    def direct(p, residual, before):
+        for r in range(B, B + fine, 8):
+            x = read(DI, r, first_inverse) * residual(r) + coarse_part(r)
+            if before is not None:
+                x = x - F32(SHIFT) * ld(before, r)
+            st(p, r, x)
+
+    def image_of(p, p_out, q_out):
+        for r in range(B, B + fine, 8):
+            q = apply_a(form, p, WL, WX, WY, AN, r)
+            st(QA, r, q)
+            at = r - B - HR
+            if 0 <= at < n:
+                for k in range(own_blocks):
+                    p_out[k, at : at + 8, :] = p[k, r : r + 8, :]
+                    q_out[k, at : at + 8, :] = q[:, k * 128 : k * 128 + 128]
 
     def restrict(q):
         for c in range(FAR - 1, coarse - FAR + 1, 8):
             count = min(8, coarse - FAR + 1 - c)
-            st(GC, B + c, form.total(four_rows(q, B + 4 * c - 40, count)))
+            set_sums(c, form.total(four_rows(q, B + 4 * c - 40, count)))
 
     def coarse_image(c, count):
         e = ld(EB, B + c, count)
@@ -595,11 +642,11 @@
         st(KV.at[side], 0, image + form.unpack_rows(jnp.broadcast_to(sums, (4, sums.shape[1]))))
 
     smooth(0, coarse)
-    for r in range(B, B + fine, 8):
-        st(PA, r, ld(DI, r) * ld(R, r) + ld(SP, r))
-    flows(form, PA, WX, FL, range(B, B + fine, 8))
-    for r in range(B, B + fine, 8):
-        st(QA, r, apply_a(PA, form.left, FL, WY, AN, r))
+    direct(PA, lambda r: read(R, r, first_rows), None)
+    image_of(PA, p0, q0)
+    for r in range(0, n, 8):
+        for k in range(own_blocks):
+            r0[k, r : r + 8, :] = first_rows[:, k * 128 : k * 128 + 128] if r == 0 else r_i[k, r : r + 8, :]
     restrict(QA)
     far_up, _ = sides(0, 1)
     near_up, _ = sides(1, 2)
@@ -608,39 +655,26 @@
     up = stretch(far_up, near_up)
     down = stretch(near_down, far_down)
     image = coarse_image(0, FAR - 1)
-    st(GC, B, image[0:4])
-    st(GC, B + 4, image[4:] + up[0 : FAR - 5])
+    set_sums(0, image[0:4])
+    set_sums(4, image[4:] + up[0 : FAR - 5])
     image = coarse_image(coarse - FAR + 1, FAR - 1)
-    st(GC, B + coarse - FAR + 1, image[0:7] + down[1:])
-    st(GC, B + coarse - 4, image[7:])
+    set_sums(coarse - FAR + 1, image[0:7] + down[1:])
+    set_sums(coarse - 4, image[7:])
     second_sums(0, 7, sides(HR + 1, HR + 2)[0])
     second_sums(1, coarse - FAR, sides(2 * HR - 2, 2 * HR - 1)[1])
-    for r in range(0, n, 8):
-        f = B + HR + r
-        for out, ref in ((p0, PA), (q0, QA), (r0, R)):
-            out[:, r : r + 8, :] = ref[:own_blocks, f : f + 8, :]
     smooth(0, coarse)
-    for r in range(B, B + fine, 8):
-        st(PB, r, (ld(DI, r) * ld(QA, r) + ld(SP, r)) - F32(SHIFT) * ld(PA, r))
-    flows(form, PB, WX, FL, range(B, B + fine, 8))
-    for r in range(B, B + fine, 8):
-        st(QA, r, apply_a(PB, form.left, FL, WY, AN, r))
+    direct(PB, lambda r: ld(QA, r), PA)
+    image_of(PB, p1, q1)
     restrict(QA)
     for c, side, first in ((8, 0, 1), (coarse - FAR + 1, 1, 1)):
         image = coarse_image(c, 3) + ld(KV.at[side], first, 3)
-        st(GC, B + c, image - F32(SHIFT) * ld(GC, B + c, 3))
-    for r in range(0, n, 8):
-        f = B + HR + r
-        for out, ref in ((p1, PB), (q1, QA)):
-            out[:, r : r + 8, :] = ref[:own_blocks, f : f + 8, :]
+        set_sums(c, image - F32(SHIFT) * ld(GC, B + c, 3))
     smooth(8, coarse - 8)
-    for r in range(B + HR - 8, B + HR + n + 8, 8):
-        st(PA, r, (ld(DI, r) * ld(QA, r) + ld(SP, r)) - F32(SHIFT) * ld(PB, r))
-    flows(form, PA, WX, FL, range(B + HR, B + HR + n, 8))
+    direct(PA, lambda r: ld(QA, r), PB)
     acc = [jnp.zeros((8, 128), F32) for _ in range(9)]
     for r in range(0, n, 8):
         f = B + HR + r
-        image = apply_a(PA, form.left, FL, WY, AN, f)
+        image = apply_a(form, PA, WL, WX, WY, AN, f)
         sums = [[] for _ in acc]
         for j in range(own_blocks):
             z2, i2 = PA[j, f : f + 8, :], image[:, j * 128 : (j + 1) * 128]
@@ -677,16 +711,13 @@
     x2 = y2 / d2
     x1 = y1 / d1 - l21 * x2
     x0 = b0 / g00 - l10 * x1 - l20 * x2
-    sums, spare, done = [[work.at[k], work.at[k + 1]] for k in (0, 2, 4)]
+    sums, spare = [[work.at[k], work.at[k + 1]] for k in (0, 2)]
     for r in range(0, n, 8):
         for j in range(blocks):
             z0, z1, z2, i0, i1, i2, res = [x[j, r : r + 8, :] for x in (p0, p1, p2, q0, q1, q2, r0)]
             sums[0][j, r : r + 8, :] = x0 * z0 + x1 * z1 + x2 * z2
             sums[1][j, r : r + 8, :] = res - (x0 * i0 + x1 * i1 + x2 * i2)
-    reorder(form.steps_out, sums, done, spare)
-    for r in range(0, n, 8):
-        heights[r : r + 8, :] = ld(done[0], r)
-        residual[r : r + 8, :] = ld(done[1], r)
+    reorder(form.steps_out, sums, [heights, residual], spare)
 
 
 def swap(x, axis, size, inner):
@@ -737,20 +768,20 @@
         work,
     )
     from_out = swap(to_out, "row", nrow, False)
-    di, to_in, *far_b = call(near_rows, "near_rows", fields, [field, msg] + [far] * 4, work)
+    di, wl, to_in, *far_b = call(near_rows, "near_rows", fields, [field, field, msg] + [far] * 4, work)
     from_in = swap(to_in, "row", nrow, True)
     fine = n + 2 * HR
     coarse = n // 4 + 2 * FAR
     mom, *vectors = call(
         basis,
         "basis",
-        (*fields, g_a, cr_a, cd_a, ca_a, di, *far_b, from_in, from_out),
+        (*fields, g_a, cr_a, cd_a, ca_a, di, wl, *far_b, from_in, from_out),
         [shape(nrow * ncol, 1, 128)] + [tile] * 7,
-        [(nb, fine + 2 * GUARD, 128)] * 10 + [(cb, coarse + 2 * GUARD, 128)] * 8 + [(5, cb, 16, 128), (2, cb, 8, 128)],
+        [(5, 2, nb, HR, 128)] + [(nb, fine + 2 * GUARD, 128)] * 4 + [(cb, coarse + 2 * GUARD, 128)] * 8 + [(5, cb, 16, 128), (2, cb, 8, 128)],
     )
     mom = lax.all_to_all(mom, ("row", "col"), 0, 0, tiled=True)
     out = shape(n, width)
-    return tuple(call(combine, "combine", (mom, *vectors), [out, out], [(6, nb - 1, n, 128)]))
+    return tuple(call(combine, "combine", (mom, *vectors), [out, out], [(4, nb - 1, n, 128)]))
 
 
 def solution(mesh):

time: 32.5 us -> 31.9 us (0.982)
  Pallas kernels: 8.99 us -> 8.16 us
    pallas_call x6, Pallas kernels: 8.99 us -> 8.16 us  [call(): pl.pallas_call(kernel, in_specs=[HBM if fetches else VMEM] * len(args), o...]
where the time goes in v6:
time: 31.9 us; the launch traced here: 31.7 us
  blocking collectives  14.2 us (45%)
  Pallas kernels  8.16 us (26%)
  starting transfers between devices  6.85 us (21%)
  waiting for transfers between devices  1.77 us (6%)
  between operations  0.66 us (2%)
    all_to_all x1, blocking collectives, local(): mom = lax.all_to_all(mom, ('row', 'col'), 0, 0, tiled=True)  14.2 us
    pallas_call x6, Pallas kernels, call(): pl.pallas_call(kernel, in_specs=[HBM if fetches else VMEM] * len(args), o...  8.16 us
    ppermute x3, starting transfers between devices, swap(): return lax.ppermute(x, axis, pairs)  6.85 us
    ppermute x3, waiting for transfers between devices, swap(): return lax.ppermute(x, axis, pairs)  1.77 us
  transfers between devices with their start and end apart: 3, of which 2 were waited for; matrix products, arithmetic and copies ran while one was open for 0% of the time, Pallas kernels for 9%

profile of v6, /device:TPU:0, one launch (start us, length us, event | category | flops | bytes accessed | tf_op | source)
XLA Modules:
  0.0 31.7 jit_solution(9876544442569681654)
XLA Ops:
  0.6 1.2 %edge_columns.1 = f32[104,256]{1,0:T(8,128)S(1)} custom-call(f32[96,512]{1,0:T(8,128)} %refs_0_.3, f32[96,512]{1,0:T(8,128)} %refs_1_.3, f32[96,512]{1,0:T(8,128)} %refs_2_.3, f32[96,512]{1,0:T(8,128)} %refs_3_.3, f32[96,512]{1,0:T(8,128)} %refs_4_.3, f32[96,512]{1,0:T(8,128)} %refs_5_.3), custom_call_target="tpu_custom_call" | custom-call | flops 2000000 | bytes 2000000 | tf_op jit(solution)/shard_map/edge_columns/pallas_call | solution.py:741
  1.8 3.0 %collective-permute-start = (f32[104,256]{1,0:T(8,128)S(1)}, f32[104,256]{1,0:T(8,128)S(1)}, u32[]{:S(2)}, u32[]{:S(2)}) collective-permute-start(f32[104,256]{1,0:T(8,128)S(1)} %edge_columns.1), channel_id=1, source_target_pairs={{0,1},{1,0},{2,3},{3,2},{4,5},{5,4},{6,7},{7,6},{8,9},{9,8},{10,11... | collective-permute-start | bytes 319496 | tf_op jit(solution)/shard_map/ppermute | solution.py:728
  4.8 2.2 %tile_fields.1 = (f32[4,96,128]{2,1,0:T(8,128)S(1)}, f32[4,96,128]{2,1,0:T(8,128)S(1)}, f32[4,96,128]{2,1,0:T(8,128)S(1)}, f32[4,96,128]{2,1,0:T(8,128)S(1)}, f3...) custom-call(f32[96,512]{1,0:T(8,128)} %refs_0_.3, f32[96,512]{1,0:T(8,128)} %refs_1_.3, f32[96,512]{1,0:T(8,128)} %refs_2_.3, ...), custom_call_target="tpu_custom_call" | custom-call | flops 2000000 | bytes 2000000 | tf_op jit(solution)/shard_map/tile_fields/pallas_call | solution.py:741
  7.0 0.8 %collective-permute-done.refs_0_ = f32[104,256]{1,0:T(8,128)S(1)} collective-permute-done((f32[104,256]{1,0:T(8,128)S(1)}, f32[104,256]{1,0:T(8,128)S(1)}, u32[]{:S(2)}, u32[]{:S(2)}) %collective-permute-start) | collective-permute-done | bytes 106528 | tf_op jit(solution)/shard_map/ppermute | solution.py:728
  7.8 0.7 %edge_rows.1 = (f32[5,96,128]{2,1,0:T(8,128)S(1)}, f32[5,96,128]{2,1,0:T(8,128)S(1)}, f32[5,104,128]{2,1,0:T(8,128)S(1)}, f32[5,96,128]{2,1,0:T(8,128)S(1)}, f32...) custom-call(f32[4,96,128]{2,1,0:T(8,128)S(1)} %get-tuple-element.33., ...), custom_call_target="tpu_custom_call" | custom-call | flops 2000000 | bytes 2000000 | tf_op jit(solution)/shard_map/edge_rows/pallas_call | solution.py:741
  8.4 0.7 %collective-permute-start.2 = (f32[5,48,128]{2,1,0:T(8,128)S(1)}, f32[5,48,128]{2,1,0:T(8,128)S(1)}, u32[]{:S(2)}, u32[]{:S(2)}) collective-permute-start(f32[5,48,128]{2,1,0:T(8,128)S(1)} %get-tuple-element.55), channel_id=1, source_target_pairs={{2,4},{4,2},{6,8},{8,6},{10,12},{12,10},{14,16},{16,14},{18,20},{2... | collective-permute-start | bytes 368648 | tf_op jit(solution)/shard_map/ppermute | solution.py:728
  9.1 0.6 %near_rows.1 = (f32[5,96,128]{2,1,0:T(8,128)S(1)}, f32[5,96,128]{2,1,0:T(8,128)S(1)}, f32[5,48,128]{2,1,0:T(8,128)S(1)}, f32[2,12,128]{2,1,0:T(8,128)S(1)}, f32[...) custom-call(f32[5,96,128]{2,1,0:T(8,128)S(1)} %get-tuple-element.39.r_i, ...), custom_call_target="tpu_custom_call" | custom-call | flops 2000000 | bytes 2000000 | tf_op jit(solution)/shard_map/near_rows/pallas_call | solution.py:741
  9.6 3.2 %collective-permute-start.1 = (f32[5,48,128]{2,1,0:T(8,128)S(1)}, f32[5,48,128]{2,1,0:T(8,128)S(1)}, u32[]{:S(2)}, u32[]{:S(2)}) collective-permute-start(f32[5,48,128]{2,1,0:T(8,128)S(1)} %get-tuple-element.54), channel_id=1, source_target_pairs={{0,2},{2,0},{4,6},{6,4},{8,10},{10,8},{12,14},{14,12},{16,18},{18,... | collective-permute-start | bytes 368648 | tf_op jit(solution)/shard_map/ppermute | solution.py:728
  12.8 0.0 collective-permute-done.2.msg_out
  12.8 1.0 %collective-permute-done.1.msg_in = f32[5,48,128]{2,1,0:T(8,128)S(1)} collective-permute-done((f32[5,48,128]{2,1,0:T(8,128)S(1)}, f32[5,48,128]{2,1,0:T(8,128)S(1)}, u32[]{:S(2)}, u32[]{:S(2)}) %collective-permute-start.1) | collective-permute-done | bytes 122912 | tf_op jit(solution)/shard_map/ppermute | solution.py:728
  13.8 2.5 %basis.1 = (f32[32,1,128]{2,1,0:T(1,128)S(1)}, f32[4,96,128]{2,1,0:T(8,128)S(1)}, f32[4,96,128]{2,1,0:T(8,128)S(1)}, f32[4,96,128]{2,1,0:T(8,128)S(1)}, f32[4,96...) custom-call(f32[5,96,128]{2,1,0:T(8,128)S(1)} %get-tuple-element.39.r_i, ...), custom_call_target="tpu_custom_call" | custom-call | flops 2000000 | bytes 2000000 | tf_op jit(solution)/shard_map/basis/pallas_call | solution.py:741
  16.3 14.2 %all_to_all.5.mom = f32[32,1,128]{2,1,0:T(1,128)S(1)} all-to-all(f32[32,1,128]{2,1,0:T(1,128)S(1)} %get-tuple-element.56), channel_id=1, replica_groups=mesh['row'=16,'col'=2] {'row','col'}, dimensions={0} | all-to-all | bytes 32768 | tf_op jit(solution)/shard_map/all_to_all | solution.py:782
  30.5 1.2 %combine.1 = (f32[96,512]{1,0:T(8,128)}, f32[96,512]{1,0:T(8,128)}) custom-call(f32[32,1,128]{2,1,0:T(1,128)S(1)} %all_to_all.5.mom, f32[4,96,128]{2,1,0:T(8,128)S(1)} %get-tuple-element.57.p0, f32[4,96,128]{2,1,0:T(8,128)S(1)} %get-tuple-element.58.p1, f32[4,96,128]{2,1,0:T(8,128)S(1)} %get-tuple-element.59.p2, f32[4,96,128]{2,1,0:T(8,128)S(1)} %get-tuple-element.60.q0, ...), custom_call_target="tpu_custom_call" | custom-call | flops 2000000 | bytes 2000000 | tf_op jit(solution)/shard_map/combine/pallas_call | solution.py:741
Async XLA Ops:
  1.8 6.0 %collective-permute-start = (f32[104,256]{1,0:T(8,128)S(1)}, f32[104,256]{1,0:T(8,128)S(1)}, u32[]{:S(2)}, u32[]{:S(2)}) collective-permute-start(f32[104,256]{1,0:T(8,128)S(1)} %edge_columns.1), channel_id=1, source_target_pairs={{0,1},{1,0},{2,3},{3,2},{4,5},{5,4},{6,7},{7,6},{8,9},{9,8},{10,11... | collective-permute-start | bytes 319496 | tf_op jit(solution)/shard_map/ppermute | solution.py:728
  8.4 4.4 %collective-permute-start.2 = (f32[5,48,128]{2,1,0:T(8,128)S(1)}, f32[5,48,128]{2,1,0:T(8,128)S(1)}, u32[]{:S(2)}, u32[]{:S(2)}) collective-permute-start(f32[5,48,128]{2,1,0:T(8,128)S(1)} %get-tuple-element.55), channel_id=1, source_target_pairs={{2,4},{4,2},{6,8},{8,6},{10,12},{12,10},{14,16},{16,14},{18,20},{2... | collective-permute-start | bytes 368648 | tf_op jit(solution)/shard_map/ppermute | solution.py:728
  9.6 4.2 %collective-permute-start.1 = (f32[5,48,128]{2,1,0:T(8,128)S(1)}, f32[5,48,128]{2,1,0:T(8,128)S(1)}, u32[]{:S(2)}, u32[]{:S(2)}) collective-permute-start(f32[5,48,128]{2,1,0:T(8,128)S(1)} %get-tuple-element.54), channel_id=1, source_target_pairs={{0,2},{2,0},{4,6},{6,4},{8,10},{10,8},{12,14},{14,12},{16,18},{18,... | collective-permute-start | bytes 368648 | tf_op jit(solution)/shard_map/ppermute | solution.py:728

commit v7 on v6

--- a/solution.py
+++ b/solution.py
@@ -10,6 +10,7 @@
 DAMP = 2.0 / 3.0
 SHIFT = 1.0
 HC = 64
+SENT = 48
 HR = 8
 FAR = 12
 DEPTH = 4 * HR + FAR - 1 + 5
@@ -264,6 +265,7 @@
 def edge_columns(inner, *refs):
     fields, (out, *held, sems) = refs[:6], refs[6:]
     n, width = fields[0].shape
+    half = n // 2
     _, col_odd, end_row, _ = position()
     last = jnp.logical_not(col_odd) if inner else col_odd
     offset = pl.multiple_of(jnp.where(last, width - 128, 0), 128)
@@ -271,29 +273,33 @@
     zero = F32(0.0)
     fetch([f.at[:, pl.ds(offset, 128)] for f in fields], held, sems)
 
-    def pair(x, y):
-        low = jnp.where(lane < HC, x, roll_right(y, HC))
-        high = jnp.where(lane < HC, roll_right(x, HC), y)
-        return jnp.where(last, high, low)
-
-    carry = jnp.zeros((1, 128), F32)
-    for r in range(0, n, 8):
+    def to(x, target):
+        return pltpu.roll(x, jnp.where(last, (target + SENT) % 128, target % 128), 1)
+
+    def chunk(r, second):
         g_x, g_y, w_x, w_y, a, p = [f[r : r + 8, :] for f in held]
         if r == n - 8:
             w_y = jnp.where((row == 7) & end_row, zero, w_y)
         fx = w_x * g_x
         fy = w_y * g_y
-        before_x = jnp.where(lane == 0, zero, roll_right(fx))
-        before_y = jnp.where(row == 0, jnp.broadcast_to(carry, fy.shape), pltpu.roll(fy, 1, 0))
-        carry = fy[7:8, :]
-        src = a * p + before_x - fx + before_y - fy
-        edge = jnp.broadcast_to(fx[:, 127:128], fx.shape)
-        out[r : r + 8, 0:128] = jnp.where((lane == 0) & last, edge, pair(src, w_x))
-        out[r : r + 8, 128:256] = pair(w_y, a)
-    tail = jnp.broadcast_to(carry, (8, 128))
-    tail = pair(tail, tail)
-    out[n : n + 8, 0:128] = tail
-    out[n : n + 8, 128:256] = tail
+        before = jnp.zeros((1, 128), F32) if r == 0 else held[3][r - 1 : r, :] * held[1][r - 1 : r, :]
+        before_y = jnp.where(row == 0, jnp.broadcast_to(before, fy.shape), pltpu.roll(fy, 1, 0))
+        src = to(a * p - fx + before_y - fy, 0)
+        src = src + jnp.where((lane == 0) & jnp.logical_not(last), zero, to(fx, 1))
+        flux = jnp.broadcast_to(fx[:, 127:128], fx.shape)
+        right = jnp.where((lane == SENT) & last, flux, to(w_x, SENT))
+        down = to(w_y, 2 * SENT)
+        out[r : r + 8, :] = jnp.where(lane < SENT, src, jnp.where(lane < 2 * SENT, right, down))
+        start = 80 if second else 16
+        beyond = jnp.where((lane == start) & last, to(w_x, start + 1), zero)
+        rest = jnp.where(lane < start, to(w_y, 32) if second else down, to(a, start) + beyond)
+        return rest, fy[7:8, :]
+
+    for r in range(0, half, 8):
+        first, _ = chunk(r, False)
+        second, tail = chunk(r + half, True)
+        out[n + r : n + r + 8, :] = jnp.where(lane < HC, first, second)
+    out[n + half :, :] = to(jnp.broadcast_to(tail, (8, 128)), 0)
 
 
 def tile_fields(*refs):
@@ -338,19 +344,35 @@
     lane = lanes((8, 128))
     zero = F32(0.0)
 
-    def halo(r, c):
-        x = inner[r : r + 8, c : c + 128]
-        y = outer[r : r + 8, c : c + 128] if has_outer else jnp.zeros_like(x)
-        before, after = jnp.where(odd, x, y), jnp.where(odd, y, x)
-        first = jnp.where(lane < HC, after, roll_right(before, HC))
-        second = jnp.where(lane < HC, roll_right(after, HC), before)
-        return first, second
+    messages = [(inner, odd)] + ([(outer, jnp.logical_not(odd))] if has_outer else [])
+
+    def placed(x, source, before):
+        return pltpu.roll(x, jnp.where(before, (128 - SENT - source) % 128, -source % 128), 1)
+
+    def within(x, before):
+        start = jnp.where(before, 128 - SENT, 0)
+        return jnp.where((lane >= start) & (lane < start + SENT), x, zero)
+
+    def halo(m, before, r):
+        half = n // 2
+        main = m[r : r + 8, :]
+        second = r >= half
+        rest = m[n + r % half : n + r % half + 8, :]
+        src = placed(main, 0, before)
+        right = jnp.where(lane == 128 - SENT, zero, placed(main, SENT, before))
+        if second:
+            near = lane < jnp.where(before, 128 - SENT + 32, 32)
+            down = jnp.where(near, placed(main, 2 * SENT, before), placed(rest, 32, before))
+        else:
+            down = placed(jnp.where(lane < 2 * SENT, rest, main), 2 * SENT, before)
+        a = placed(rest, 80 if second else 16, before)
+        flux = jnp.where(before, jnp.broadcast_to(main[:, SENT : SENT + 1], main.shape), zero)
+        return [within(x, before) for x in (src, right, down, a)] + [flux]
 
     for r in range(0, n, 8):
-        src_h, wx_h = halo(r, 0)
-        wy_h, an_h = halo(r, 128)
-        incoming = jnp.broadcast_to(src_h[:, HC : HC + 1], (8, 128))
-        src_h = jnp.where(lane == 0, src_h + fx_t[r : r + 8, :], jnp.where(lane == HC, zero, src_h))
+        parts = [halo(m, before, r) for m, before in messages]
+        src_h, wx_h, wy_h, an_h, incoming = [tree(list(x)) for x in zip(*parts)]
+        src_h = jnp.where(lane == 0, src_h + fx_t[r : r + 8, :], src_h)
         for out, tile, h in ((r_o, r_t, src_h), (wx_o, wx_t, wx_h), (wy_o, wy_t, wy_h), (an_o, an_t, an_h)):
             top = GUARD if out is wy_o else 0
             for j in range(own):
@@ -362,7 +384,8 @@
     st(wy_o, 0, jnp.zeros((GUARD, (own + 1) * 128), F32))
     for j in range(own):
         fy_o[j] = fy_t[j]
-    fy_o[own] = halo(n, 0)[0]
+    tails = [within(placed(m[n + n // 2 :, :], 0, before), before) for m, before in messages]
+    fy_o[own] = tree(tails)
 
     message(form, row_odd, r_o, wx_o, wy_o, an_o, fy_o, *rest)
 
@@ -751,7 +774,7 @@
 
     halos = []
     for inner in (True, False) if ncol > 2 else (True,):
-        (edge,) = call(functools.partial(edge_columns, inner), "edge_columns", fields, [shape(n + 8, 256)], [(n, 128)] * 6, 1, 6)
+        (edge,) = call(functools.partial(edge_columns, inner), "edge_columns", fields, [shape(n + n // 2 + 8, 128)], [(n, 128)] * 6, 1, 6)
         halos.append(swap(edge, "col", ncol, inner))
     tile = shape(nb - 1, n, 128)
     own = call(tile_fields, "tile_fields", fields, [tile] * 4 + [shape(n, 128), shape(nb - 1, 8, 128)], [(n, width)] * 6 + [(4, nb - 1, n, 128)] * 2 + [(2, nb - 1, 8, 128)], 1, 6)

time: 31.9 us -> 31.6 us (level)
  waiting for transfers between devices: 1.77 us -> 1.18 us
    ppermute x3, waiting for transfers between devices: 1.77 us -> 1.18 us  [swap(): return lax.ppermute(x, axis, pairs)]
where the time goes in v7:
time: 31.6 us; the launch traced here: 31.4 us
  blocking collectives  14.2 us (45%)
  Pallas kernels  8.15 us (26%)
  starting transfers between devices  7.13 us (23%)
  waiting for transfers between devices  1.18 us (4%)
  between operations  0.66 us (2%)
    all_to_all x1, blocking collectives, local(): mom = lax.all_to_all(mom, ('row', 'col'), 0, 0, tiled=True)  14.2 us
    pallas_call x6, Pallas kernels, call(): pl.pallas_call(kernel, in_specs=[HBM if fetches else VMEM] * len(args), o...  8.15 us
    ppermute x3, starting transfers between devices, swap(): return lax.ppermute(x, axis, pairs)  7.13 us
    ppermute x3, waiting for transfers between devices, swap(): return lax.ppermute(x, axis, pairs)  1.18 us
  transfers between devices with their start and end apart: 3, of which 2 were waited for; matrix products, arithmetic and copies ran while one was open for 0% of the time, Pallas kernels for 9%

profile of v7, /device:TPU:0, one launch (start us, length us, event | category | flops | bytes accessed | tf_op | source)
XLA Modules:
  0.0 31.4 jit_solution(10898758775726436784)
XLA Ops:
  0.6 1.2 %edge_columns.1 = f32[152,128]{1,0:T(8,128)S(1)} custom-call(f32[96,512]{1,0:T(8,128)} %refs_0_.3, f32[96,512]{1,0:T(8,128)} %refs_1_.3, f32[96,512]{1,0:T(8,128)} %refs_2_.3, f32[96,512]{1,0:T(8,128)} %refs_3_.3, f32[96,512]{1,0:T(8,128)} %refs_4_.3, f32[96,512]{1,0:T(8,128)} %refs_5_.3), custom_call_target="tpu_custom_call" | custom-call | flops 2000000 | bytes 2000000 | tf_op jit(solution)/shard_map/edge_columns/pallas_call | solution.py:764
  1.8 3.0 %collective-permute-start = (f32[152,128]{1,0:T(8,128)S(1)}, f32[152,128]{1,0:T(8,128)S(1)}, u32[]{:S(2)}, u32[]{:S(2)}) collective-permute-start(f32[152,128]{1,0:T(8,128)S(1)} %edge_columns.1), channel_id=1, source_target_pairs={{0,1},{1,0},{2,3},{3,2},{4,5},{5,4},{6,7},{7,6},{8,9},{9,8},{10,11... | collective-permute-start | bytes 233480 | tf_op jit(solution)/shard_map/ppermute | solution.py:751
  4.8 2.2 %tile_fields.1 = (f32[4,96,128]{2,1,0:T(8,128)S(1)}, f32[4,96,128]{2,1,0:T(8,128)S(1)}, f32[4,96,128]{2,1,0:T(8,128)S(1)}, f32[4,96,128]{2,1,0:T(8,128)S(1)}, f3...) custom-call(f32[96,512]{1,0:T(8,128)} %refs_0_.3, f32[96,512]{1,0:T(8,128)} %refs_1_.3, f32[96,512]{1,0:T(8,128)} %refs_2_.3, ...), custom_call_target="tpu_custom_call" | custom-call | flops 2000000 | bytes 2000000 | tf_op jit(solution)/shard_map/tile_fields/pallas_call | solution.py:764
  7.0 0.2 collective-permute-done.refs_0_
  7.2 0.7 %edge_rows.1 = (f32[5,96,128]{2,1,0:T(8,128)S(1)}, f32[5,96,128]{2,1,0:T(8,128)S(1)}, f32[5,104,128]{2,1,0:T(8,128)S(1)}, f32[5,96,128]{2,1,0:T(8,128)S(1)}, f32...) custom-call(f32[4,96,128]{2,1,0:T(8,128)S(1)} %get-tuple-element.33., ...), custom_call_target="tpu_custom_call" | custom-call | flops 2000000 | bytes 2000000 | tf_op jit(solution)/shard_map/edge_rows/pallas_call | solution.py:764
  7.8 0.7 %collective-permute-start.2 = (f32[5,48,128]{2,1,0:T(8,128)S(1)}, f32[5,48,128]{2,1,0:T(8,128)S(1)}, u32[]{:S(2)}, u32[]{:S(2)}) collective-permute-start(f32[5,48,128]{2,1,0:T(8,128)S(1)} %get-tuple-element.55), channel_id=1, source_target_pairs={{2,4},{4,2},{6,8},{8,6},{10,12},{12,10},{14,16},{16,14},{18,20},{2... | collective-permute-start | bytes 368648 | tf_op jit(solution)/shard_map/ppermute | solution.py:751
  8.5 0.6 %near_rows.1 = (f32[5,96,128]{2,1,0:T(8,128)S(1)}, f32[5,96,128]{2,1,0:T(8,128)S(1)}, f32[5,48,128]{2,1,0:T(8,128)S(1)}, f32[2,12,128]{2,1,0:T(8,128)S(1)}, f32[...) custom-call(f32[5,96,128]{2,1,0:T(8,128)S(1)} %get-tuple-element.39.r_i, ...), custom_call_target="tpu_custom_call" | custom-call | flops 2000000 | bytes 2000000 | tf_op jit(solution)/shard_map/near_rows/pallas_call | solution.py:764
  9.1 3.5 %collective-permute-start.1 = (f32[5,48,128]{2,1,0:T(8,128)S(1)}, f32[5,48,128]{2,1,0:T(8,128)S(1)}, u32[]{:S(2)}, u32[]{:S(2)}) collective-permute-start(f32[5,48,128]{2,1,0:T(8,128)S(1)} %get-tuple-element.54), channel_id=1, source_target_pairs={{0,2},{2,0},{4,6},{6,4},{8,10},{10,8},{12,14},{14,12},{16,18},{18,... | collective-permute-start | bytes 368648 | tf_op jit(solution)/shard_map/ppermute | solution.py:751
  12.5 0.0 collective-permute-done.2.msg_out
  12.5 1.0 %collective-permute-done.1.msg_in = f32[5,48,128]{2,1,0:T(8,128)S(1)} collective-permute-done((f32[5,48,128]{2,1,0:T(8,128)S(1)}, f32[5,48,128]{2,1,0:T(8,128)S(1)}, u32[]{:S(2)}, u32[]{:S(2)}) %collective-permute-start.1) | collective-permute-done | bytes 122912 | tf_op jit(solution)/shard_map/ppermute | solution.py:751
  13.5 2.5 %basis.1 = (f32[32,1,128]{2,1,0:T(1,128)S(1)}, f32[4,96,128]{2,1,0:T(8,128)S(1)}, f32[4,96,128]{2,1,0:T(8,128)S(1)}, f32[4,96,128]{2,1,0:T(8,128)S(1)}, f32[4,96...) custom-call(f32[5,96,128]{2,1,0:T(8,128)S(1)} %get-tuple-element.39.r_i, ...), custom_call_target="tpu_custom_call" | custom-call | flops 2000000 | bytes 2000000 | tf_op jit(solution)/shard_map/basis/pallas_call | solution.py:764
  16.0 14.2 %all_to_all.5.mom = f32[32,1,128]{2,1,0:T(1,128)S(1)} all-to-all(f32[32,1,128]{2,1,0:T(1,128)S(1)} %get-tuple-element.56), channel_id=1, replica_groups=mesh['row'=16,'col'=2] {'row','col'}, dimensions={0} | all-to-all | bytes 32768 | tf_op jit(solution)/shard_map/all_to_all | solution.py:805
  30.2 1.2 %combine.1 = (f32[96,512]{1,0:T(8,128)}, f32[96,512]{1,0:T(8,128)}) custom-call(f32[32,1,128]{2,1,0:T(1,128)S(1)} %all_to_all.5.mom, f32[4,96,128]{2,1,0:T(8,128)S(1)} %get-tuple-element.57.p0, f32[4,96,128]{2,1,0:T(8,128)S(1)} %get-tuple-element.58.p1, f32[4,96,128]{2,1,0:T(8,128)S(1)} %get-tuple-element.59.p2, f32[4,96,128]{2,1,0:T(8,128)S(1)} %get-tuple-element.60.q0, ...), custom_call_target="tpu_custom_call" | custom-call | flops 2000000 | bytes 2000000 | tf_op jit(solution)/shard_map/combine/pallas_call | solution.py:764
Async XLA Ops:
  1.8 5.4 %collective-permute-start = (f32[152,128]{1,0:T(8,128)S(1)}, f32[152,128]{1,0:T(8,128)S(1)}, u32[]{:S(2)}, u32[]{:S(2)}) collective-permute-start(f32[152,128]{1,0:T(8,128)S(1)} %edge_columns.1), channel_id=1, source_target_pairs={{0,1},{1,0},{2,3},{3,2},{4,5},{5,4},{6,7},{7,6},{8,9},{9,8},{10,11... | collective-permute-start | bytes 233480 | tf_op jit(solution)/shard_map/ppermute | solution.py:751
  7.8 4.7 %collective-permute-start.2 = (f32[5,48,128]{2,1,0:T(8,128)S(1)}, f32[5,48,128]{2,1,0:T(8,128)S(1)}, u32[]{:S(2)}, u32[]{:S(2)}) collective-permute-start(f32[5,48,128]{2,1,0:T(8,128)S(1)} %get-tuple-element.55), channel_id=1, source_target_pairs={{2,4},{4,2},{6,8},{8,6},{10,12},{12,10},{14,16},{16,14},{18,20},{2... | collective-permute-start | bytes 368648 | tf_op jit(solution)/shard_map/ppermute | solution.py:751
  9.1 4.4 %collective-permute-start.1 = (f32[5,48,128]{2,1,0:T(8,128)S(1)}, f32[5,48,128]{2,1,0:T(8,128)S(1)}, u32[]{:S(2)}, u32[]{:S(2)}) collective-permute-start(f32[5,48,128]{2,1,0:T(8,128)S(1)} %get-tuple-element.54), channel_id=1, source_target_pairs={{0,2},{2,0},{4,6},{6,4},{8,10},{10,8},{12,14},{14,12},{16,18},{18,... | collective-permute-start | bytes 368648 | tf_op jit(solution)/shard_map/ppermute | solution.py:751

commit v8 on v7

--- a/solution.py
+++ b/solution.py
@@ -80,6 +80,9 @@
     def unpack_rows(self, m):
         return group_sum(jnp.where(lanes(m.shape) % 4 == rows(m.shape) % 4, m, F32(0.0)))
 
+    def at_sides(self, w_l, d_l, w_r, d_r):
+        return self.first_only(w_l * d_l) + self.last_only(w_r * d_r)
+
     def first_only(self, x):
         return jnp.where(lanes(x.shape) % 4 == 0, x, F32(0.0))
 
@@ -145,6 +148,13 @@
         key = rows(h.shape) % 4
         own = jnp.where(key < 2, jnp.where(key == 0, a, b), jnp.where(key == 2, c, d))
         return join([own, group_sum(jnp.where(lanes(h.shape) % 4 == key, h, F32(0.0)))])
+
+    def at_sides(self, w_l, d_l, w_r, d_r):
+        w_l, d_l, w_r, d_r = split(w_l), split(d_l), split(w_r), split(d_r)
+        four = lanes(d_l[1].shape) % 4
+        none = jnp.zeros_like(d_l[1])
+        halo = jnp.where(four == 0, w_l[4] * d_l[1], jnp.where(four == 3, w_r[4] * d_r[1], none))
+        return join([w_l[0] * d_l[0], none, none, w_r[3] * d_r[0], halo])
 
     def first_only(self, x):
         a, _, _, _, h = split(x)
@@ -390,16 +400,28 @@
     message(form, row_odd, r_o, wx_o, wy_o, an_o, fy_o, *rest)
 
 
-def near_rows(r_i, wx_i, wy_i, an_i, fy_i, di, wl, *rest):
+def near_rows(r_i, wx_i, wy_i, an_i, fy_i, di, wl, t_o, s_o, *rest):
     form = layout(wx_i.shape[0])
     row_odd, _, _, _ = position()
+    *rest, U = rest
     message(form, jnp.logical_not(row_odd), r_i, wx_i, wy_i, an_i, fy_i, *rest)
+    n, G = wx_i.shape[1], GUARD
     for r in range(0, wx_i.shape[1], 8):
         w_x, w_y = ld(wx_i, r), ld(wy_i, GUARD + r)
         w_l = form.left(w_x)
         st(wl, r, w_l)
         diag = ld(an_i, r) + w_x + w_l + w_y + ld(wy_i, GUARD + r - 1)
-        st(di, r, jnp.where(diag > F32(0.0), F32(1.0) / diag, F32(0.0)))
+        inverse = jnp.where(diag > F32(0.0), F32(1.0) / diag, F32(0.0))
+        st(di, r, inverse)
+        st(U, G + r, inverse * ld(r_i, r))
+    for r in range(0, n, 8):
+        x = ld(U, G + r)
+        down = ld(wy_i, G + r) * (x - ld(U, G + r + 1))
+        up = ld(wy_i, G + r - 1) * (x - ld(U, G + r - 1))
+        beside = ld(wl, r) * (x - form.left(x)) + ld(wx_i, r) * (x - form.right(x))
+        st(t_o, r, (ld(an_i, r) * x + beside) + (down + up))
+    for c in range(0, n // 4, 8):
+        st(s_o, c, form.total(four_rows(t_o, 4 * c, 8)))
 
 
 def message(form, bottom, r_o, wx_o, wy_o, an_o, fy_o, msg, g_o, cr_o, cd_o, ca_o, U, DI, V, WL, T, H, K):
@@ -514,8 +536,8 @@
     return (an.chunk(r) * x + beside) + (down + up)
 
 
-def basis(r_i, wx_i, wy_i, an_i, fy_i, g_a, cr_a, cd_a, ca_a, di_i, wl_i, g_b, cr_b, cd_b, ca_b, msg_in, msg_out, mom, p0, p1, p2, q0, q1, q2, r0,
-         ENDS, WY, PA, PB, QA, C_L, C_R, C_D, C_A, C_I, EA, EB, GC, KF, KV):
+def basis(r_i, wx_i, wy_i, an_i, fy_i, g_a, cr_a, cd_a, ca_a, di_i, wl_i, t_i, s_i, g_b, cr_b, cd_b, ca_b, msg_in, msg_out, mom, PA, PB, PC, QA, QB, q2, r0,
+         ENDS, WY, WM, T0, T1, T2, C_L, C_R, C_D, C_A, C_I, EA, EC, GC, SUM, E, D, KF, KV):
     blocks, n, _ = r_i.shape
     form = layout(blocks)
     fine = n + 2 * HR
@@ -532,7 +554,7 @@
     zeros = jnp.zeros((B, blocks * 128), F32)
     coarse_zeros = jnp.zeros((B, form.coarse_blocks * 128), F32)
     R, WX, AN, DI, WL = [Rows(own, ENDS.at[k]) for k, own in enumerate((r_i, wx_i, an_i, di_i, wl_i))]
-    for ref in (WY, PA, PB):
+    for ref in (WY, PA, PB, PC):
         st(ref, 0, zeros)
         st(ref, B + fine, zeros)
     for k, ends in ((0, ENDS.at[0]), (1, ENDS.at[1]), (3, ENDS.at[2])):
@@ -562,7 +584,7 @@
     def read(field, r, first):
         return first if r == B + HR else field.chunk(r)
 
-    for ref in (EA, EB, C_D):
+    for ref in (EA, EC, C_D, E.at[0], E.at[1], E.at[2]):
         st(ref, 0, coarse_zeros)
         st(ref, B + coarse, coarse_zeros)
     up, down = sides(4 * HR, 4 * HR + FAR - 1)
@@ -595,56 +617,51 @@
         st(GC, B + c, g)
         st(EA, B + c, ld(C_I, B + c, g.shape[0]) * g)
 
-    def smooth(lo, hi):
+    def smooth(turn, lo, hi):
         if lo > 0:
             st(EA, B + lo - 8, coarse_zeros)
-            st(EB, B + lo - 8, coarse_zeros)
+            st(EC, B + lo - 8, coarse_zeros)
         if hi < coarse:
             st(EA, B + hi, coarse_zeros)
-            st(EB, B + hi, coarse_zeros)
-        old, new = EA, EB
-        for turn in range(3):
+            st(EC, B + hi, coarse_zeros)
+        for old, new in ((EA, EC), (EC, EA), (EA, E.at[turn])):
             for c in range(B + lo, B + hi, 8):
                 e = ld(old, c)
                 beside = ld(C_L, c) * form.coarse_left(e) + ld(C_R, c) * form.coarse_right(e)
                 beside = beside + (ld(C_D, c - 1) * ld(old, c - 1) + ld(C_D, c) * ld(old, c + 1))
                 st(new, c, F32(1.0 - DAMP) * e + ld(C_I, c) * (ld(GC, c) + beside))
-            old, new = new, old
-
-    def coarse_part(r):
+
+    def differences(turn, lo, hi, with_sums):
+        e_ref = E.at[turn]
+        for c in range(B + lo, B + hi, 8):
+            e = ld(e_ref, c)
+            parts = (e - form.coarse_left(e), e - form.coarse_right(e), e - ld(e_ref, c - 1), e - ld(e_ref, c + 1))
+            for k, x in enumerate(parts):
+                st(D.at[turn, k], c, x)
+            if with_sums:
+                d_l, d_r, d_u, d_d = parts
+                image = ld(C_A, c) * e + ld(C_L, c) * d_l + ld(C_R, c) * d_r
+                g = ld(SUM, c) + (image + (ld(C_D, c - 1) * d_u + ld(C_D, c) * d_d))
+                st(GC, c, g)
+                st(EA, c, ld(C_I, c) * g)
+
+    def lifted(turn, r):
         at = B + 10 + (r - B) // 4
         shape = (8, form.coarse_blocks * 128)
-        a, b = [jnp.broadcast_to(ld(EB, at + k, 1), shape) for k in (0, 1)]
-        return form.spread(jnp.where(rows(shape) < 4, a, b))
-
-    def direct(p, residual, before):
-        for r in range(B, B + fine, 8):
-            x = read(DI, r, first_inverse) * residual(r) + coarse_part(r)
-            if before is not None:
-                x = x - F32(SHIFT) * ld(before, r)
-            st(p, r, x)
-
-    def image_of(p, p_out, q_out):
-        for r in range(B, B + fine, 8):
-            q = apply_a(form, p, WL, WX, WY, AN, r)
-            st(QA, r, q)
-            at = r - B - HR
-            if 0 <= at < n:
-                for k in range(own_blocks):
-                    p_out[k, at : at + 8, :] = p[k, r : r + 8, :]
-                    q_out[k, at : at + 8, :] = q[:, k * 128 : k * 128 + 128]
-
-    def restrict(q):
-        for c in range(FAR - 1, coarse - FAR + 1, 8):
-            count = min(8, coarse - FAR + 1 - c)
-            set_sums(c, form.total(four_rows(q, B + 4 * c - 40, count)))
-
-    def coarse_image(c, count):
-        e = ld(EB, B + c, count)
-        c_l, c_r = ld(C_L, B + c, count), ld(C_R, B + c, count)
-        image = ld(C_A, B + c, count) * e + c_l * (e - form.coarse_left(e)) + c_r * (e - form.coarse_right(e))
-        image = image + ld(C_D, B + c - 1, count) * (e - ld(EB, B + c - 1, count))
-        return image + ld(C_D, B + c, count) * (e - ld(EB, B + c + 1, count))
+        row = rows(shape)
+
+        def two(ref):
+            a, b = [jnp.broadcast_to(ld(ref, at + k, 1), shape) for k in (0, 1)]
+            return jnp.where(row < 4, a, b)
+
+        e, d_l, d_r, d_u, d_d = two(E.at[turn]), *[two(D.at[turn, k]) for k in range(4)]
+        e = form.spread(e)
+        vertical = ld(WM, r) * form.spread(jnp.where(row % 4 == 0, d_u, d_d))
+        return e, AN.chunk(r) * e + (form.at_sides(WL.chunk(r), d_l, WX.chunk(r), d_r) + vertical)
+
+    def operate(v, t, chunks):
+        for r in chunks:
+            st(t, r, apply_a(form, v, WL, WX, WY, AN, r))
 
     def stretch(a, b):
         shape = (8, a.shape[1])
@@ -657,53 +674,76 @@
             st(KF.at[k], 8, form.unpack_rows(jnp.broadcast_to(row, (4, row.shape[1]))))
         centre, east, south, south_east, south_west = [ld(KF.at[k], 8, 4) for k in range(5)]
         north, north_west, north_east = [ld(KF.at[k], 7, 4) for k in (2, 3, 4)]
-        e, below, above = [ld(EB, B + c + d, 4) for d in (0, 1, -1)]
+        e, below, above = [ld(E.at[0], B + c + d, 4) for d in (0, 1, -1)]
         image = centre * e + east * form.coarse_right(e) + form.coarse_left(east * e)
         image = image + south * below + north * above
         image = image + south_east * form.coarse_right(below) + form.coarse_left(north_west * above)
         image = image + south_west * form.coarse_left(below) + form.coarse_right(north_east * above)
         st(KV.at[side], 0, image + form.unpack_rows(jnp.broadcast_to(sums, (4, sums.shape[1]))))
 
-    smooth(0, coarse)
-    direct(PA, lambda r: read(R, r, first_rows), None)
-    image_of(PA, p0, q0)
-    for r in range(0, n, 8):
-        for k in range(own_blocks):
-            r0[k, r : r + 8, :] = first_rows[:, k * 128 : k * 128 + 128] if r == 0 else r_i[k, r : r + 8, :]
-    restrict(QA)
+    chunks = range(B, B + fine, 8)
+    end = B + fine
+    for r in (*chunks[:3], *chunks[-3:]):
+        st(PA, r, read(DI, r, first_inverse) * read(R, r, first_rows))
+    operate(PA, T0, (*chunks[:2], *chunks[-2:]))
     far_up, _ = sides(0, 1)
     near_up, _ = sides(1, 2)
     _, near_down = sides(HR - 1, HR)
     _, far_down = sides(HR - 2, HR - 1)
-    up = stretch(far_up, near_up)
-    down = stretch(near_down, far_down)
-    image = coarse_image(0, FAR - 1)
-    set_sums(0, image[0:4])
-    set_sums(4, image[4:] + up[0 : FAR - 5])
-    image = coarse_image(coarse - FAR + 1, FAR - 1)
-    set_sums(coarse - FAR + 1, image[0:7] + down[1:])
-    set_sums(coarse - 4, image[7:])
+    st(SUM, B, coarse_zeros)
+    st(SUM, B + coarse - 8, coarse_zeros)
+    st(SUM, B + 4, stretch(far_up, near_up)[0:7])
+    st(SUM, B + coarse - FAR + 1, stretch(near_down, far_down)[1:])
+    st(SUM, B + FAR + 1, ld(s_i, 1, n // 4 - 2))
+    st(SUM, B + FAR - 1, form.total(four_rows(T0, B + 4, 2)))
+    st(SUM, B + coarse - FAR - 1, form.total(four_rows(T0, end - 12, 2)))
+    for r in chunks:
+        w_u, w_d = ld(WY, r - 1), ld(WY, r)
+        row = rows(w_d.shape) % 4
+        st(WM, r, jnp.where(row == 0, w_u, jnp.where(row == 3, w_d, zero)))
+
+    smooth(0, 0, coarse)
+    differences(0, 0, coarse, True)
     second_sums(0, 7, sides(HR + 1, HR + 2)[0])
     second_sums(1, coarse - FAR, sides(2 * HR - 2, 2 * HR - 1)[1])
-    smooth(0, coarse)
-    direct(PB, lambda r: ld(QA, r), PA)
-    image_of(PB, p1, q1)
-    restrict(QA)
-    for c, side, first in ((8, 0, 1), (coarse - FAR + 1, 1, 1)):
-        image = coarse_image(c, 3) + ld(KV.at[side], first, 3)
-        set_sums(c, image - F32(SHIFT) * ld(GC, B + c, 3))
-    smooth(8, coarse - 8)
-    direct(PA, lambda r: ld(QA, r), PB)
+    for r in chunks:
+        e, image = lifted(0, r)
+        inner = chunks[2] <= r < chunks[-2]
+        p = read(DI, r, first_inverse) * read(R, r, first_rows) + e
+        q = (ld(t_i, r - B - HR) if inner else ld(T0, r)) + image
+        st(PA, r, p)
+        st(QA, r, q)
+        st(PB, r, read(DI, r, first_inverse) * q - F32(SHIFT) * p)
+    st(r0, 0, first_rows)
+    operate(PB, T1, chunks)
+    for c, side in ((8, 0), (coarse - FAR + 1, 1)):
+        st(SUM, B + c, ld(KV.at[side], 1, 3) - F32(SHIFT) * ld(GC, B + c, 3))
+    for c in range(FAR - 1, coarse - FAR + 1, 8):
+        st(SUM, B + c, form.total(four_rows(T1, B + 4 * c - 40, min(8, coarse - FAR + 1 - c))))
+    smooth(1, 0, coarse)
+    differences(1, 8, coarse - 8, True)
+    for r in chunks:
+        e, image = lifted(1, r)
+        p = ld(PB, r) + e
+        q = ld(T1, r) + image
+        st(PB, r, p)
+        st(QB, r, q)
+        st(PC, r, read(DI, r, first_inverse) * q - F32(SHIFT) * p)
+    operate(PC, T2, chunks[1:-1])
+    smooth(2, 8, coarse - 8)
+    differences(2, 8, coarse - 8, False)
     acc = [jnp.zeros((8, 128), F32) for _ in range(9)]
     for r in range(0, n, 8):
         f = B + HR + r
-        image = apply_a(form, PA, WL, WX, WY, AN, f)
+        e, image = lifted(2, f)
+        image = ld(T2, f) + image
+        st(PC, f, ld(PC, f) + e)
         sums = [[] for _ in acc]
         for j in range(own_blocks):
-            z2, i2 = PA[j, f : f + 8, :], image[:, j * 128 : (j + 1) * 128]
-            p2[j, r : r + 8, :] = z2
+            i2 = image[:, j * 128 : (j + 1) * 128]
             q2[j, r : r + 8, :] = i2
-            z0, z1, i0, i1, res = [x[j, r : r + 8, :] for x in (p0, p1, q0, q1, r0)]
+            z0, z1, z2, i0, i1 = [x[j, f : f + 8, :] for x in (PA, PB, PC, QA, QB)]
+            res = read(R, f, first_rows)[:, j * 128 : (j + 1) * 128]
             pairs = ((z0, i0), (z1, i0), (z1, i1), (z2, i0), (z2, i1), (z2, i2), (z0, res), (z1, res), (z2, res))
             for k, (x, y) in enumerate(pairs):
                 sums[k].append(x * y)
@@ -718,8 +758,9 @@
         mom[j] = line[0:1]
 
 
-def combine(mom, p0, p1, p2, q0, q1, q2, r0, heights, residual, work):
-    blocks, n, _ = p0.shape
+def combine(mom, p0, p1, p2, q0, q1, q2, r_first, r_i, heights, residual, work):
+    blocks, n, _ = q2.shape
+    skip = GUARD + HR
     form = layout(blocks + 1)
     tot = jnp.broadcast_to(tree([mom[j] for j in range(mom.shape[0])]), (8, 128))
     m = [jnp.broadcast_to(tot[:, k : k + 1], (8, 128)) for k in range(9)]
@@ -737,7 +778,8 @@
     sums, spare = [[work.at[k], work.at[k + 1]] for k in (0, 2)]
     for r in range(0, n, 8):
         for j in range(blocks):
-            z0, z1, z2, i0, i1, i2, res = [x[j, r : r + 8, :] for x in (p0, p1, p2, q0, q1, q2, r0)]
+            z0, z1, z2, i0, i1 = [x[j, skip + r : skip + r + 8, :] for x in (p0, p1, p2, q0, q1)]
+            i2, res = q2[j, r : r + 8, :], r_first[j] if r == 0 else r_i[j, r : r + 8, :]
             sums[0][j, r : r + 8, :] = x0 * z0 + x1 * z1 + x2 * z2
             sums[1][j, r : r + 8, :] = res - (x0 * i0 + x1 * i1 + x2 * i2)
     reorder(form.steps_out, sums, [heights, residual], spare)
@@ -791,20 +833,27 @@
         work,
     )
     from_out = swap(to_out, "row", nrow, False)
-    di, wl, to_in, *far_b = call(near_rows, "near_rows", fields, [field, field, msg] + [far] * 4, work)
+    di, wl, t, sums, to_in, *far_b = call(
+        near_rows,
+        "near_rows",
+        fields,
+        [field, field, field, shape(cb, n // 4, 128), msg] + [far] * 4,
+        work + [(nb, n + 2 * GUARD, 128)],
+    )
     from_in = swap(to_in, "row", nrow, True)
     fine = n + 2 * HR
     coarse = n // 4 + 2 * FAR
     mom, *vectors = call(
         basis,
         "basis",
-        (*fields, g_a, cr_a, cd_a, ca_a, di, wl, *far_b, from_in, from_out),
-        [shape(nrow * ncol, 1, 128)] + [tile] * 7,
-        [(5, 2, nb, HR, 128)] + [(nb, fine + 2 * GUARD, 128)] * 4 + [(cb, coarse + 2 * GUARD, 128)] * 8 + [(5, cb, 16, 128), (2, cb, 8, 128)],
+        (*fields, g_a, cr_a, cd_a, ca_a, di, wl, t, sums, *far_b, from_in, from_out),
+        [shape(nrow * ncol, 1, 128)] + [shape(nb, fine + 2 * GUARD, 128)] * 5 + [tile, shape(nb, 8, 128)],
+        [(5, 2, nb, HR, 128)] + [(nb, fine + 2 * GUARD, 128)] * 5 + [(cb, coarse + 2 * GUARD, 128)] * 9
+        + [(3, cb, coarse + 2 * GUARD, 128), (3, 4, cb, coarse + 2 * GUARD, 128), (5, cb, 16, 128), (2, cb, 8, 128)],
     )
     mom = lax.all_to_all(mom, ("row", "col"), 0, 0, tiled=True)
     out = shape(n, width)
-    return tuple(call(combine, "combine", (mom, *vectors), [out, out], [(4, nb - 1, n, 128)]))
+    return tuple(call(combine, "combine", (mom, *vectors, fields[0]), [out, out], [(4, nb - 1, n, 128)]))
 
 
 def solution(mesh):

time: 31.6 us -> 31.6 us (level)
  no operation moved by 1% of the time
where the time goes in v8:
time: 31.6 us; the launch traced here: 31.4 us
  blocking collectives  14 us (44%)
  Pallas kernels  8.42 us (27%)
  starting transfers between devices  7.13 us (23%)
  waiting for transfers between devices  1.18 us (4%)
  between operations  0.66 us (2%)
    all_to_all x1, blocking collectives, local(): mom = lax.all_to_all(mom, ('row', 'col'), 0, 0, tiled=True)  14 us
    pallas_call x6, Pallas kernels, call(): pl.pallas_call(kernel, in_specs=[HBM if fetches else VMEM] * len(args), o...  8.42 us
    ppermute x3, starting transfers between devices, swap(): return lax.ppermute(x, axis, pairs)  7.13 us
    ppermute x3, waiting for transfers between devices, swap(): return lax.ppermute(x, axis, pairs)  1.18 us
  transfers between devices with their start and end apart: 3, of which 2 were waited for; matrix products, arithmetic and copies ran while one was open for 0% of the time, Pallas kernels for 9%

profile of v8, /device:TPU:0, one launch (start us, length us, event | category | flops | bytes accessed | tf_op | source)
XLA Modules:
  0.0 31.4 jit_solution(1797944569851879355)
XLA Ops:
  0.6 1.2 %edge_columns.1 = f32[152,128]{1,0:T(8,128)S(1)} custom-call(f32[96,512]{1,0:T(8,128)} %refs_0_.3, f32[96,512]{1,0:T(8,128)} %refs_1_.3, f32[96,512]{1,0:T(8,128)} %refs_2_.3, f32[96,512]{1,0:T(8,128)} %refs_3_.3, f32[96,512]{1,0:T(8,128)} %refs_4_.3, f32[96,512]{1,0:T(8,128)} %refs_5_.3), custom_call_target="tpu_custom_call" | custom-call | flops 2000000 | bytes 2000000 | tf_op jit(solution)/shard_map/edge_columns/pallas_call | solution.py:806
  1.8 3.0 %collective-permute-start = (f32[152,128]{1,0:T(8,128)S(1)}, f32[152,128]{1,0:T(8,128)S(1)}, u32[]{:S(2)}, u32[]{:S(2)}) collective-permute-start(f32[152,128]{1,0:T(8,128)S(1)} %edge_columns.1), channel_id=1, source_target_pairs={{0,1},{1,0},{2,3},{3,2},{4,5},{5,4},{6,7},{7,6},{8,9},{9,8},{10,11... | collective-permute-start | bytes 233480 | tf_op jit(solution)/shard_map/ppermute | solution.py:793
  4.8 2.2 %tile_fields.1 = (f32[4,96,128]{2,1,0:T(8,128)S(1)}, f32[4,96,128]{2,1,0:T(8,128)S(1)}, f32[4,96,128]{2,1,0:T(8,128)S(1)}, f32[4,96,128]{2,1,0:T(8,128)S(1)}, f3...) custom-call(f32[96,512]{1,0:T(8,128)} %refs_0_.3, f32[96,512]{1,0:T(8,128)} %refs_1_.3, f32[96,512]{1,0:T(8,128)} %refs_2_.3, ...), custom_call_target="tpu_custom_call" | custom-call | flops 2000000 | bytes 2000000 | tf_op jit(solution)/shard_map/tile_fields/pallas_call | solution.py:806
  7.0 0.2 collective-permute-done.refs_0_
  7.2 0.6 %edge_rows.1 = (f32[5,96,128]{2,1,0:T(8,128)S(1)}, f32[5,96,128]{2,1,0:T(8,128)S(1)}, f32[5,104,128]{2,1,0:T(8,128)S(1)}, f32[5,96,128]{2,1,0:T(8,128)S(1)}, f32...) custom-call(f32[4,96,128]{2,1,0:T(8,128)S(1)} %get-tuple-element.35., ...), custom_call_target="tpu_custom_call" | custom-call | flops 2000000 | bytes 2000000 | tf_op jit(solution)/shard_map/edge_rows/pallas_call | solution.py:806
  7.8 0.7 %collective-permute-start.2 = (f32[5,48,128]{2,1,0:T(8,128)S(1)}, f32[5,48,128]{2,1,0:T(8,128)S(1)}, u32[]{:S(2)}, u32[]{:S(2)}) collective-permute-start(f32[5,48,128]{2,1,0:T(8,128)S(1)} %get-tuple-element.59), channel_id=1, source_target_pairs={{2,4},{4,2},{6,8},{8,6},{10,12},{12,10},{14,16},{16,14},{18,20},{2... | collective-permute-start | bytes 368648 | tf_op jit(solution)/shard_map/ppermute | solution.py:793
  8.5 0.8 %near_rows.1 = (f32[5,96,128]{2,1,0:T(8,128)S(1)}, f32[5,96,128]{2,1,0:T(8,128)S(1)}, f32[5,96,128]{2,1,0:T(8,128)S(1)}, f32[2,24,128]{2,1,0:T(8,128)S(1)}, f32[...) custom-call(f32[5,96,128]{2,1,0:T(8,128)S(1)} %get-tuple-element.41., ...), custom_call_target="tpu_custom_call" | custom-call | flops 2000000 | bytes 2000000 | tf_op jit(solution)/shard_map/near_rows/pallas_call | solution.py:806
  9.3 3.5 %collective-permute-start.1 = (f32[5,48,128]{2,1,0:T(8,128)S(1)}, f32[5,48,128]{2,1,0:T(8,128)S(1)}, u32[]{:S(2)}, u32[]{:S(2)}) collective-permute-start(f32[5,48,128]{2,1,0:T(8,128)S(1)} %get-tuple-element.58), channel_id=1, source_target_pairs={{0,2},{2,0},{4,6},{6,4},{8,10},{10,8},{12,14},{14,12},{16,18},{18,... | collective-permute-start | bytes 368648 | tf_op jit(solution)/shard_map/ppermute | solution.py:793
  12.8 0.0 collective-permute-done.2.msg_out
  12.8 1.0 %collective-permute-done.1.msg_in = f32[5,48,128]{2,1,0:T(8,128)S(1)} collective-permute-done((f32[5,48,128]{2,1,0:T(8,128)S(1)}, f32[5,48,128]{2,1,0:T(8,128)S(1)}, u32[]{:S(2)}, u32[]{:S(2)}) %collective-permute-start.1) | collective-permute-done | bytes 122912 | tf_op jit(solution)/shard_map/ppermute | solution.py:793
  13.7 2.5 %basis.1 = (f32[32,1,128]{2,1,0:T(1,128)S(1)}, f32[5,128,128]{2,1,0:T(8,128)S(1)}, f32[5,128,128]{2,1,0:T(8,128)S(1)}, f32[5,128,128]{2,1,0:T(8,128)S(1)}, f32[5...) custom-call(f32[5,96,128]{2,1,0:T(8,128)S(1)} %get-tuple-element.41.r_, ...), custom_call_target="tpu_custom_call" | custom-call | flops 2000000 | bytes 2000000 | tf_op jit(solution)/shard_map/basis/pallas_call | solution.py:806
  16.2 14.0 %all_to_all.5.mom = f32[32,1,128]{2,1,0:T(1,128)S(1)} all-to-all(f32[32,1,128]{2,1,0:T(1,128)S(1)} %get-tuple-element.60), channel_id=1, replica_groups=mesh['row'=16,'col'=2] {'row','col'}, dimensions={0} | all-to-all | bytes 32768 | tf_op jit(solution)/shard_map/all_to_all | solution.py:854
  30.2 1.2 %combine.1 = (f32[96,512]{1,0:T(8,128)}, f32[96,512]{1,0:T(8,128)}) custom-call(f32[32,1,128]{2,1,0:T(1,128)S(1)} %all_to_all.5.mom, f32[5,128,128]{2,1,0:T(8,128)S(1)} %get-tuple-element.61.p0, f32[5,128,128]{2,1,0:T(8,128)S(1)} %get-tuple-element.62.p1, f32[5,128,128]{2,1,0:T(8,128)S(1)} %get-tuple-element.63.p2, f32[5,128,128]{2,1,0:T(8,128)S(1)} %get-tuple-element.64.q0, ...), custom_call_target="tpu_custom_call" | custom-call | flops 2000000 | bytes 2000000 | tf_op jit(solution)/shard_map/combine/pallas_call | solution.py:806
Async XLA Ops:
  1.8 5.4 %collective-permute-start = (f32[152,128]{1,0:T(8,128)S(1)}, f32[152,128]{1,0:T(8,128)S(1)}, u32[]{:S(2)}, u32[]{:S(2)}) collective-permute-start(f32[152,128]{1,0:T(8,128)S(1)} %edge_columns.1), channel_id=1, source_target_pairs={{0,1},{1,0},{2,3},{3,2},{4,5},{5,4},{6,7},{7,6},{8,9},{9,8},{10,11... | collective-permute-start | bytes 233480 | tf_op jit(solution)/shard_map/ppermute | solution.py:793
  7.8 4.9 %collective-permute-start.2 = (f32[5,48,128]{2,1,0:T(8,128)S(1)}, f32[5,48,128]{2,1,0:T(8,128)S(1)}, u32[]{:S(2)}, u32[]{:S(2)}) collective-permute-start(f32[5,48,128]{2,1,0:T(8,128)S(1)} %get-tuple-element.59), channel_id=1, source_target_pairs={{2,4},{4,2},{6,8},{8,6},{10,12},{12,10},{14,16},{16,14},{18,20},{2... | collective-permute-start | bytes 368648 | tf_op jit(solution)/shard_map/ppermute | solution.py:793
  9.3 4.4 %collective-permute-start.1 = (f32[5,48,128]{2,1,0:T(8,128)S(1)}, f32[5,48,128]{2,1,0:T(8,128)S(1)}, u32[]{:S(2)}, u32[]{:S(2)}) collective-permute-start(f32[5,48,128]{2,1,0:T(8,128)S(1)} %get-tuple-element.58), channel_id=1, source_target_pairs={{0,2},{2,0},{4,6},{6,4},{8,10},{10,8},{12,14},{14,12},{16,18},{18,... | collective-permute-start | bytes 368648 | tf_op jit(solution)/shard_map/ppermute | solution.py:793

commit v9 on v8

--- a/solution.py
+++ b/solution.py
@@ -537,7 +537,7 @@
 
 
 def basis(r_i, wx_i, wy_i, an_i, fy_i, g_a, cr_a, cd_a, ca_a, di_i, wl_i, t_i, s_i, g_b, cr_b, cd_b, ca_b, msg_in, msg_out, mom, PA, PB, PC, QA, QB, q2, r0,
-         ENDS, WY, WM, T0, T1, T2, C_L, C_R, C_D, C_A, C_I, EA, EC, GC, SUM, E, D, KF, KV):
+         ENDS, WY, WM, T0, T1, T2, C_L, C_R, C_D, C_A, C_I, M_L, M_R, M_U, M_D, EA, EC, GC, SUM, E, D, KF, KV):
     blocks, n, _ = r_i.shape
     form = layout(blocks)
     fine = n + 2 * HR
@@ -611,11 +611,11 @@
         st(C_L, c, c_l)
         inverse_c = jnp.where(total > zero, F32(DAMP) / total, zero)
         st(C_I, c, inverse_c)
-        st(EA, c, inverse_c * ld(GC, c))
-
-    def set_sums(c, g):
-        st(GC, B + c, g)
-        st(EA, B + c, ld(C_I, B + c, g.shape[0]) * g)
+        for ref, w in ((M_L, c_l), (M_R, c_r), (M_U, ld(C_D, c - 1)), (M_D, ld(C_D, c))):
+            st(ref, c, inverse_c * w)
+        g = inverse_c * ld(GC, c)
+        st(EA, c, g)
+        st(GC, c, g)
 
     def smooth(turn, lo, hi):
         if lo > 0:
@@ -627,9 +627,10 @@
         for old, new in ((EA, EC), (EC, EA), (EA, E.at[turn])):
             for c in range(B + lo, B + hi, 8):
                 e = ld(old, c)
-                beside = ld(C_L, c) * form.coarse_left(e) + ld(C_R, c) * form.coarse_right(e)
-                beside = beside + (ld(C_D, c - 1) * ld(old, c - 1) + ld(C_D, c) * ld(old, c + 1))
-                st(new, c, F32(1.0 - DAMP) * e + ld(C_I, c) * (ld(GC, c) + beside))
+                fixed = F32(1.0 - DAMP) * e + ld(GC, c)
+                vertical = ld(M_U, c) * ld(old, c - 1) + ld(M_D, c) * ld(old, c + 1)
+                beside = ld(M_L, c) * form.coarse_left(e) + ld(M_R, c) * form.coarse_right(e)
+                st(new, c, (fixed + vertical) + beside)
 
     def differences(turn, lo, hi, with_sums):
         e_ref = E.at[turn]
@@ -642,8 +643,10 @@
                 d_l, d_r, d_u, d_d = parts
                 image = ld(C_A, c) * e + ld(C_L, c) * d_l + ld(C_R, c) * d_r
                 g = ld(SUM, c) + (image + (ld(C_D, c - 1) * d_u + ld(C_D, c) * d_d))
+                st(SUM, c, g)
+                g = ld(C_I, c) * g
                 st(GC, c, g)
-                st(EA, c, ld(C_I, c) * g)
+                st(EA, c, g)
 
     def lifted(turn, r):
         at = B + 10 + (r - B) // 4
@@ -717,7 +720,7 @@
     st(r0, 0, first_rows)
     operate(PB, T1, chunks)
     for c, side in ((8, 0), (coarse - FAR + 1, 1)):
-        st(SUM, B + c, ld(KV.at[side], 1, 3) - F32(SHIFT) * ld(GC, B + c, 3))
+        st(SUM, B + c, ld(KV.at[side], 1, 3) - F32(SHIFT) * ld(SUM, B + c, 3))
     for c in range(FAR - 1, coarse - FAR + 1, 8):
         st(SUM, B + c, form.total(four_rows(T1, B + 4 * c - 40, min(8, coarse - FAR + 1 - c))))
     smooth(1, 0, coarse)
@@ -848,7 +851,7 @@
         "basis",
         (*fields, g_a, cr_a, cd_a, ca_a, di, wl, t, sums, *far_b, from_in, from_out),
         [shape(nrow * ncol, 1, 128)] + [shape(nb, fine + 2 * GUARD, 128)] * 5 + [tile, shape(nb, 8, 128)],
-        [(5, 2, nb, HR, 128)] + [(nb, fine + 2 * GUARD, 128)] * 5 + [(cb, coarse + 2 * GUARD, 128)] * 9
+        [(5, 2, nb, HR, 128)] + [(nb, fine + 2 * GUARD, 128)] * 5 + [(cb, coarse + 2 * GUARD, 128)] * 13
         + [(3, cb, coarse + 2 * GUARD, 128), (3, 4, cb, coarse + 2 * GUARD, 128), (5, cb, 16, 128), (2, cb, 8, 128)],
     )
     mom = lax.all_to_all(mom, ("row", "col"), 0, 0, tiled=True)

time: 31.6 us -> 31.6 us (level)
  no operation moved by 1% of the time
where the time goes in v9:
time: 31.6 us; the launch traced here: 31.4 us
  blocking collectives  14 us (44%)
  Pallas kernels  8.42 us (27%)
  starting transfers between devices  7.13 us (23%)
  waiting for transfers between devices  1.18 us (4%)
  between operations  0.66 us (2%)
    all_to_all x1, blocking collectives, local(): mom = lax.all_to_all(mom, ('row', 'col'), 0, 0, tiled=True)  14 us
    pallas_call x6, Pallas kernels, call(): pl.pallas_call(kernel, in_specs=[HBM if fetches else VMEM] * len(args), o...  8.42 us
    ppermute x3, starting transfers between devices, swap(): return lax.ppermute(x, axis, pairs)  7.13 us
    ppermute x3, waiting for transfers between devices, swap(): return lax.ppermute(x, axis, pairs)  1.18 us
  transfers between devices with their start and end apart: 3, of which 2 were waited for; matrix products, arithmetic and copies ran while one was open for 0% of the time, Pallas kernels for 9%

profile of v9, /device:TPU:0, one launch (start us, length us, event | category | flops | bytes accessed | tf_op | source)
XLA Modules:
  0.0 31.4 jit_solution(12426448868454970456)
XLA Ops:
  0.6 1.2 %edge_columns.1 = f32[152,128]{1,0:T(8,128)S(1)} custom-call(f32[96,512]{1,0:T(8,128)} %refs_0_.3, f32[96,512]{1,0:T(8,128)} %refs_1_.3, f32[96,512]{1,0:T(8,128)} %refs_2_.3, f32[96,512]{1,0:T(8,128)} %refs_3_.3, f32[96,512]{1,0:T(8,128)} %refs_4_.3, f32[96,512]{1,0:T(8,128)} %refs_5_.3), custom_call_target="tpu_custom_call" | custom-call | flops 2000000 | bytes 2000000 | tf_op jit(solution)/shard_map/edge_columns/pallas_call | solution.py:809
  1.8 3.0 %collective-permute-start = (f32[152,128]{1,0:T(8,128)S(1)}, f32[152,128]{1,0:T(8,128)S(1)}, u32[]{:S(2)}, u32[]{:S(2)}) collective-permute-start(f32[152,128]{1,0:T(8,128)S(1)} %edge_columns.1), channel_id=1, source_target_pairs={{0,1},{1,0},{2,3},{3,2},{4,5},{5,4},{6,7},{7,6},{8,9},{9,8},{10,11... | collective-permute-start | bytes 233480 | tf_op jit(solution)/shard_map/ppermute | solution.py:796
  4.8 2.2 %tile_fields.1 = (f32[4,96,128]{2,1,0:T(8,128)S(1)}, f32[4,96,128]{2,1,0:T(8,128)S(1)}, f32[4,96,128]{2,1,0:T(8,128)S(1)}, f32[4,96,128]{2,1,0:T(8,128)S(1)}, f3...) custom-call(f32[96,512]{1,0:T(8,128)} %refs_0_.3, f32[96,512]{1,0:T(8,128)} %refs_1_.3, f32[96,512]{1,0:T(8,128)} %refs_2_.3, ...), custom_call_target="tpu_custom_call" | custom-call | flops 2000000 | bytes 2000000 | tf_op jit(solution)/shard_map/tile_fields/pallas_call | solution.py:809
  7.0 0.2 collective-permute-done.refs_0_
  7.2 0.6 %edge_rows.1 = (f32[5,96,128]{2,1,0:T(8,128)S(1)}, f32[5,96,128]{2,1,0:T(8,128)S(1)}, f32[5,104,128]{2,1,0:T(8,128)S(1)}, f32[5,96,128]{2,1,0:T(8,128)S(1)}, f32...) custom-call(f32[4,96,128]{2,1,0:T(8,128)S(1)} %get-tuple-element.35., ...), custom_call_target="tpu_custom_call" | custom-call | flops 2000000 | bytes 2000000 | tf_op jit(solution)/shard_map/edge_rows/pallas_call | solution.py:809
  7.8 0.7 %collective-permute-start.2 = (f32[5,48,128]{2,1,0:T(8,128)S(1)}, f32[5,48,128]{2,1,0:T(8,128)S(1)}, u32[]{:S(2)}, u32[]{:S(2)}) collective-permute-start(f32[5,48,128]{2,1,0:T(8,128)S(1)} %get-tuple-element.59), channel_id=1, source_target_pairs={{2,4},{4,2},{6,8},{8,6},{10,12},{12,10},{14,16},{16,14},{18,20},{2... | collective-permute-start | bytes 368648 | tf_op jit(solution)/shard_map/ppermute | solution.py:796
  8.5 0.8 %near_rows.1 = (f32[5,96,128]{2,1,0:T(8,128)S(1)}, f32[5,96,128]{2,1,0:T(8,128)S(1)}, f32[5,96,128]{2,1,0:T(8,128)S(1)}, f32[2,24,128]{2,1,0:T(8,128)S(1)}, f32[...) custom-call(f32[5,96,128]{2,1,0:T(8,128)S(1)} %get-tuple-element.41., ...), custom_call_target="tpu_custom_call" | custom-call | flops 2000000 | bytes 2000000 | tf_op jit(solution)/shard_map/near_rows/pallas_call | solution.py:809
  9.3 3.5 %collective-permute-start.1 = (f32[5,48,128]{2,1,0:T(8,128)S(1)}, f32[5,48,128]{2,1,0:T(8,128)S(1)}, u32[]{:S(2)}, u32[]{:S(2)}) collective-permute-start(f32[5,48,128]{2,1,0:T(8,128)S(1)} %get-tuple-element.58), channel_id=1, source_target_pairs={{0,2},{2,0},{4,6},{6,4},{8,10},{10,8},{12,14},{14,12},{16,18},{18,... | collective-permute-start | bytes 368648 | tf_op jit(solution)/shard_map/ppermute | solution.py:796
  12.8 0.0 collective-permute-done.2.msg_out
  12.8 1.0 %collective-permute-done.1.msg_in = f32[5,48,128]{2,1,0:T(8,128)S(1)} collective-permute-done((f32[5,48,128]{2,1,0:T(8,128)S(1)}, f32[5,48,128]{2,1,0:T(8,128)S(1)}, u32[]{:S(2)}, u32[]{:S(2)}) %collective-permute-start.1) | collective-permute-done | bytes 122912 | tf_op jit(solution)/shard_map/ppermute | solution.py:796
  13.7 2.5 %basis.1 = (f32[32,1,128]{2,1,0:T(1,128)S(1)}, f32[5,128,128]{2,1,0:T(8,128)S(1)}, f32[5,128,128]{2,1,0:T(8,128)S(1)}, f32[5,128,128]{2,1,0:T(8,128)S(1)}, f32[5...) custom-call(f32[5,96,128]{2,1,0:T(8,128)S(1)} %get-tuple-element.41.r_, ...), custom_call_target="tpu_custom_call" | custom-call | flops 2000000 | bytes 2000000 | tf_op jit(solution)/shard_map/basis/pallas_call | solution.py:809
  16.2 14.0 %all_to_all.5.mom = f32[32,1,128]{2,1,0:T(1,128)S(1)} all-to-all(f32[32,1,128]{2,1,0:T(1,128)S(1)} %get-tuple-element.60), channel_id=1, replica_groups=mesh['row'=16,'col'=2] {'row','col'}, dimensions={0} | all-to-all | bytes 32768 | tf_op jit(solution)/shard_map/all_to_all | solution.py:857
  30.2 1.2 %combine.1 = (f32[96,512]{1,0:T(8,128)}, f32[96,512]{1,0:T(8,128)}) custom-call(f32[32,1,128]{2,1,0:T(1,128)S(1)} %all_to_all.5.mom, f32[5,128,128]{2,1,0:T(8,128)S(1)} %get-tuple-element.61.p0, f32[5,128,128]{2,1,0:T(8,128)S(1)} %get-tuple-element.62.p1, f32[5,128,128]{2,1,0:T(8,128)S(1)} %get-tuple-element.63.p2, f32[5,128,128]{2,1,0:T(8,128)S(1)} %get-tuple-element.64.q0, ...), custom_call_target="tpu_custom_call" | custom-call | flops 2000000 | bytes 2000000 | tf_op jit(solution)/shard_map/combine/pallas_call | solution.py:809
Async XLA Ops:
  1.8 5.4 %collective-permute-start = (f32[152,128]{1,0:T(8,128)S(1)}, f32[152,128]{1,0:T(8,128)S(1)}, u32[]{:S(2)}, u32[]{:S(2)}) collective-permute-start(f32[152,128]{1,0:T(8,128)S(1)} %edge_columns.1), channel_id=1, source_target_pairs={{0,1},{1,0},{2,3},{3,2},{4,5},{5,4},{6,7},{7,6},{8,9},{9,8},{10,11... | collective-permute-start | bytes 233480 | tf_op jit(solution)/shard_map/ppermute | solution.py:796
  7.8 4.9 %collective-permute-start.2 = (f32[5,48,128]{2,1,0:T(8,128)S(1)}, f32[5,48,128]{2,1,0:T(8,128)S(1)}, u32[]{:S(2)}, u32[]{:S(2)}) collective-permute-start(f32[5,48,128]{2,1,0:T(8,128)S(1)} %get-tuple-element.59), channel_id=1, source_target_pairs={{2,4},{4,2},{6,8},{8,6},{10,12},{12,10},{14,16},{16,14},{18,20},{2... | collective-permute-start | bytes 368648 | tf_op jit(solution)/shard_map/ppermute | solution.py:796
  9.3 4.4 %collective-permute-start.1 = (f32[5,48,128]{2,1,0:T(8,128)S(1)}, f32[5,48,128]{2,1,0:T(8,128)S(1)}, u32[]{:S(2)}, u32[]{:S(2)}) collective-permute-start(f32[5,48,128]{2,1,0:T(8,128)S(1)} %get-tuple-element.58), channel_id=1, source_target_pairs={{0,2},{2,0},{4,6},{6,4},{8,10},{10,8},{12,14},{14,12},{16,18},{18,... | collective-permute-start | bytes 368648 | tf_op jit(solution)/shard_map/ppermute | solution.py:796
